TPU v7x, 256 devices: a whole 4x4x8 slice. The times are simulated.
256 devices in a mesh: row: 8 (over z_hi, core), col: 32 (over x, z_lo, y).
Axes of the slice: x: 4, y: 4, z: 8 (z_hi: 4, z_lo: 2; z = z_hi * 2 + z_lo), core: 2. Of those that a mesh axis runs over, the one named last changes fastest.
Arguments:
- features: bfloat16 [8, 32, 1024, 512], P('row', 'col'), may hold values from -64 to 64
- values: bfloat16 [8, 32, 1024, 512], P('row', 'col'), may hold values from -6 to 6
- out_grad: bfloat16 [8, 32, 1024, 512], P('row', 'col'), may hold values from -6 to 6
- query_weight: float32 [8, 32, 512, 512], P('row', 'col'), may hold values from -6 to 6
- key_weight: float32 [8, 32, 512, 512], P('row', 'col'), may hold values from -6 to 6
- query_mean: float32 [8, 32, 512, 512], P('row', 'col'), may hold values from -0.3 to 0.3
- query_square: float32 [8, 32, 512, 512], P('row', 'col'), may hold values from 0.001 to 0.01
- key_mean: float32 [8, 32, 512, 512], P('row', 'col'), may hold values from -0.3 to 0.3
- key_square: float32 [8, 32, 512, 512], P('row', 'col'), may hold values from 0.001 to 0.01
- members: int32 [8, 32, 2], P('row', 'col'), may hold values 0 or 1
Outputs:
- query_result: float32 [8, 32, 512, 512], P('row', 'col')
- key_result: float32 [8, 32, 512, 512], P('row', 'col')
All inputs are finite; a program needn't handle non-finite values. No bound on the sum of `members` on one device may be relied on, other than what follows from the above.
Results may differ from a plain program's by a relative error of at most 0.023.
The roundings to bfloat16 on the way count: a program that leaves them out, or rounds other values in their place, can miss the bound.
Values sent between devices are 32-bit elements; how exact they have to be, the bound alone decides.
No kernel may reach another device: no remote copies, remote signals or barrier semaphores. Data moves between devices by JAX's collectives and lax.ppermute only.
A program may use at most 64 MiB of HBM per device.

v0:
```python
import math

import jax
import jax.numpy as jnp
from jax import lax
from jax.sharding import PartitionSpec as P

HD = 64
SEQ = 512


beta_one = 0.9
beta_two = 0.999
epsilon = 1e-06
decay_rate = 0.01
learn_rate = 0.1
correction_one = 1.0 - math.exp(100.0 * math.log(0.9))
correction_two = 1.0 - math.exp(100.0 * math.log(0.999))


def from_partner(shard, axis, stride):
    return lax.ppermute(shard, axis, [(i, i ^ 1 << stride) for i in range(lax.axis_size(axis))])


def attend_back(seq_block):
    queries, key_rows, value_rows, grad_rows = seq_block
    length = queries.shape[0]
    head_count = queries.shape[1] // HD
    score_scale = 1.0 / math.sqrt(HD)
    query_heads = queries.reshape(length, head_count, HD)
    key_heads = key_rows.reshape(length, head_count, HD)
    value_heads = value_rows.reshape(length, head_count, HD)
    grad_heads = grad_rows.reshape(length, head_count, HD)
    scores = (
        jnp.einsum("qhd,khd->hqk", query_heads, key_heads, preferred_element_type=jnp.float32)
        * score_scale
    )
    highest = jnp.max(scores, axis=-1, keepdims=True)
    exponent = jnp.exp(scores - highest)
    softmax_out = exponent / jnp.sum(exponent, axis=-1, keepdims=True)
    prob_low = softmax_out.astype(jnp.bfloat16)
    output = jnp.einsum("hqk,khd->qhd", prob_low, value_heads, preferred_element_type=jnp.float32)
    grad_prob = jnp.einsum(
        "qhd,khd->hqk", grad_heads, value_heads, preferred_element_type=jnp.float32
    )
    row_delta = jnp.transpose(jnp.sum(grad_heads.astype(jnp.float32) * output, axis=-1))[:, :, None]
    grad_score = (softmax_out * (grad_prob - row_delta) * score_scale).astype(jnp.bfloat16)
    grad_query = jnp.einsum(
        "hqk,khd->qhd", grad_score, key_heads, preferred_element_type=jnp.float32
    ).astype(jnp.bfloat16)
    grad_key = jnp.einsum(
        "hqk,qhd->khd", grad_score, query_heads, preferred_element_type=jnp.float32
    ).astype(jnp.bfloat16)
    return (grad_query.reshape(length, -1), grad_key.reshape(length, -1))


def lamb_update(weight, first, second, grad):
    first_new = beta_one * first + (1.0 - beta_one) * grad
    second_new = beta_two * second + (1.0 - beta_two) * grad * grad
    update = (
        first_new / correction_one / (jnp.sqrt(second_new / correction_two) + epsilon)
        + decay_rate * weight
    )
    ratio = jnp.sqrt(jnp.sum(weight * weight)) / jnp.sqrt(jnp.sum(update * update) + epsilon)
    return weight - learn_rate * ratio * update


def row_trade(payload, tally, bit_pos):
    return from_partner((payload, tally), "row", bit_pos)


def col_trade(payload, tally, bit_pos):
    return from_partner((payload, tally), "col", bit_pos)


def bit_order(axis_size):
    bit_list = list(range(min(2, axis_size.bit_length() - 1)))
    return bit_list


def group_mean(stacked, active, bit_list, trade):
    tally = active
    summed = stacked * active
    for bit_pos in bit_list:
        other_sum, other_tally = trade(summed, tally, bit_pos)
        summed = summed + other_sum
        tally = tally + other_tally
    return jnp.where(active > 0, summed / (tally + 1.0 - active), stacked)


def per_device(
    features,
    values,
    out_grad,
    query_weight,
    key_weight,
    query_mean,
    query_square,
    key_mean,
    key_square,
    members,
):
    feature_rows = features[0, 0]
    in_scale = 1.0 / math.sqrt(feature_rows.shape[1])
    queries = (
        jnp.dot(
            feature_rows,
            query_weight[0, 0].astype(jnp.bfloat16),
            preferred_element_type=jnp.float32,
        )
        * in_scale
    ).astype(jnp.bfloat16)
    key_rows = (
        jnp.dot(
            feature_rows, key_weight[0, 0].astype(jnp.bfloat16), preferred_element_type=jnp.float32
        )
        * in_scale
    ).astype(jnp.bfloat16)
    seq_count = feature_rows.shape[0] // SEQ

    def by_sequence(array):
        return array.reshape(seq_count, SEQ, array.shape[-1])

    grad_query, grad_key = lax.map(
        attend_back,
        (
            by_sequence(queries),
            by_sequence(key_rows),
            by_sequence(values[0, 0]),
            by_sequence(out_grad[0, 0]),
        ),
    )
    active_row = members[0, 0, 0].astype(jnp.float32)
    active_col = members[0, 0, 1].astype(jnp.float32)
    row_bits = bit_order(lax.axis_size("row"))
    col_bits = bit_order(lax.axis_size("col"))
    query_grad = (
        jnp.einsum(
            "td,th->dh",
            feature_rows,
            grad_query.reshape(-1, grad_query.shape[-1]),
            preferred_element_type=jnp.float32,
        )
        * in_scale
    )
    query_new = lamb_update(query_weight[0, 0], query_mean[0, 0], query_square[0, 0], query_grad)
    query_row = group_mean(query_new, active_row, row_bits, row_trade)
    key_grad = (
        jnp.einsum(
            "td,th->dh",
            feature_rows,
            grad_key.reshape(-1, grad_key.shape[-1]),
            preferred_element_type=jnp.float32,
        )
        * in_scale
    )
    key_new = lamb_update(key_weight[0, 0], key_mean[0, 0], key_square[0, 0], key_grad)
    key_row = group_mean(key_new, active_row, row_bits, row_trade)
    both_rows = jnp.stack([query_row, key_row])
    both_final = group_mean(both_rows, active_col, col_bits, col_trade)
    return (both_final[0][None, None], both_final[1][None, None])


def solution(mesh):
    placed = (
        P("row", "col", None, None),
        P("row", "col", None, None),
        P("row", "col", None, None),
        P("row", "col", None, None),
        P("row", "col", None, None),
        P("row", "col", None, None),
        P("row", "col", None, None),
        P("row", "col", None, None),
        P("row", "col", None, None),
        P("row", "col", None),
    )
    return jax.shard_map(
        per_device,
        mesh=mesh,
        in_specs=placed,
        out_specs=(P("row", "col", None, None), P("row", "col", None, None)),
        check_vma=False,
    )
```

profile of v0, /device:TPU:1, one launch (start us, length us, event | category | flops | bytes accessed | tf_op | source)
XLA Modules:
  0.0 297.8 jit_solution(6165507011151509260)
XLA Ops:
  0.7 2.8 copy.30
  6.3 54.4 %while.12 = (s32[]{:T(128)}, bf16[2,512,512]{2,1,0:T(8,128)(2,1)}, bf16[2,512,512]{2,1,0:T(8,128)(2,1)}, bf16[2,512,512]{2,1,0:T(8,128)(2,1)}, bf16[2,512,512]{2...) while((s32[]{:T(128)}, bf16[2,512,512]{2,1,0:T(8,128)(2,1)}, ...), condition=%wide.region_5.6_spmd, body=%wide.region_1.5_spmd.sunk | while | flops 1364455936 | bytes 82920144 | solution.py:124
  8.6 5.0 %fusion.86 = (f32[8,512]{1,0:T(8,128)S(1)}, f32[8,512,512]{1,2,0:T(8,128)}) fusion(bf16[512,8,64]{0,2,1:T(8,128)(2,1)S(1)} %bitcast.171, bf16[512,8,64]{0,2,1:T(8,128)(2,1)S(1)} %bitcast.173), kind=kOutput, calls=%fused_computation.69.clone.1 | convolution fusion | flops 274727424 | bytes 9453568 | tf_op jit(solution)/shard_map/while/body/eval_jaxpr/sub | solution.py:39
  17.0 4.4 %fusion.87 = f32[512,8]{0,1:T(8,128)S(1)} fusion(bf16[512,8,64]{0,2,1:T(8,128)(2,1)S(1)} %bitcast.177, f32[8,512,512]{1,2,0:T(8,128)} %get-tuple-element.133, f32[8,512]{1,0:T(8,128)S(1)} %get-tuple-element.134, bf16[512,8,64]{0,2,1:T(8,128)(2,1)} %bitcast.179), kind=kOutput, calls=%fused_computation.13.clone.1 | convolution fusion | flops 273412096 | bytes 9469952 | tf_op jit(solution)/shard_map/while/body/eval_jaxpr/hqk,khd->qhd/dot_general | solution.py:42
  21.5 4.4 %multiply_convert_fusion.4 = bf16[8,512,512]{1,2,0:T(8,128)(2,1)S(1)} fusion(f32[8,512]{1,0:T(8,128)S(1)} %bitcast.187, f32[8,512,512]{1,2,0:T(8,128)} %get-tuple-element.133, f32[8,512]{1,0:T(8,128)S(1)} %get-tuple-element.134, bf16[512,8,64]{0,2,1:T(8,128)(2,1)S(1)} %bitcast.180, bf16[512,8,64]{0,2,1:T(8,128)(2,1)S(1)} %bitcast.178), kind=kOutput, calls=%fused_computation.1.clone.1 | convolution fusion | flops 278921216 | bytes 13664256 | tf_op jit(solution)/shard_map/while/body/eval_jaxpr/qhd,khd->hqk/dot_general | solution.py:43
  28.1 3.6 %convolution_convert_fusion.4 = bf16[8,64,512]{2,1,0:T(8,128)(2,1)S(1)} fusion(bf16[512,8,64]{0,2,1:T(8,128)(2,1)S(1)} %bitcast.172, bf16[8,512,512]{1,2,0:T(8,128)(2,1)} %copy-done.1), kind=kOutput, calls=%fused_computation.11.clone.1 | convolution fusion | flops 268697600 | bytes 5242880 | tf_op jit(solution)/shard_map/while/body/eval_jaxpr/hqk,qhd->khd/dot_general | solution.py:51
  35.8 5.0 %fusion.86 = (f32[8,512]{1,0:T(8,128)S(1)}, f32[8,512,512]{1,2,0:T(8,128)}) fusion(bf16[512,8,64]{0,2,1:T(8,128)(2,1)S(1)} %bitcast.171, bf16[512,8,64]{0,2,1:T(8,128)(2,1)S(1)} %bitcast.173), kind=kOutput, calls=%fused_computation.69.clone.1 | convolution fusion | flops 274727424 | bytes 9453568 | tf_op jit(solution)/shard_map/while/body/eval_jaxpr/sub | solution.py:39
  44.2 4.4 %fusion.87 = f32[512,8]{0,1:T(8,128)S(1)} fusion(bf16[512,8,64]{0,2,1:T(8,128)(2,1)S(1)} %bitcast.177, f32[8,512,512]{1,2,0:T(8,128)} %get-tuple-element.133, f32[8,512]{1,0:T(8,128)S(1)} %get-tuple-element.134, bf16[512,8,64]{0,2,1:T(8,128)(2,1)} %bitcast.179), kind=kOutput, calls=%fused_computation.13.clone.1 | convolution fusion | flops 273412096 | bytes 9469952 | tf_op jit(solution)/shard_map/while/body/eval_jaxpr/hqk,khd->qhd/dot_general | solution.py:42
  48.7 4.4 %multiply_convert_fusion.4 = bf16[8,512,512]{1,2,0:T(8,128)(2,1)S(1)} fusion(f32[8,512]{1,0:T(8,128)S(1)} %bitcast.187, f32[8,512,512]{1,2,0:T(8,128)} %get-tuple-element.133, f32[8,512]{1,0:T(8,128)S(1)} %get-tuple-element.134, bf16[512,8,64]{0,2,1:T(8,128)(2,1)S(1)} %bitcast.180, bf16[512,8,64]{0,2,1:T(8,128)(2,1)S(1)} %bitcast.178), kind=kOutput, calls=%fused_computation.1.clone.1 | convolution fusion | flops 278921216 | bytes 13664256 | tf_op jit(solution)/shard_map/while/body/eval_jaxpr/qhd,khd->hqk/dot_general | solution.py:43
  55.3 3.6 %convolution_convert_fusion.4 = bf16[8,64,512]{2,1,0:T(8,128)(2,1)S(1)} fusion(bf16[512,8,64]{0,2,1:T(8,128)(2,1)S(1)} %bitcast.172, bf16[8,512,512]{1,2,0:T(8,128)(2,1)} %copy-done.1), kind=kOutput, calls=%fused_computation.11.clone.1 | convolution fusion | flops 268697600 | bytes 5242880 | tf_op jit(solution)/shard_map/while/body/eval_jaxpr/hqk,qhd->khd/dot_general | solution.py:51
  60.7 2.7 copy.31
  65.7 4.0 %multiply_reduce_fusion.2 = (f32[]{:T(128)}, f32[512,512]{0,1:T(8,128)S(1)}) fusion(f32[1,1,512,512]{2,3,1,0:T(8,128)S(1)} %copy-done.2, f32[1,1,512,512]{2,3,1,0:T(8,128)} %copy.37, bf16[1024,512]{1,0:T(8,128)(2,1)} %bitcast.185, bf16[1,1,1024,512]{3,2,1,0:T(8,128)(2,1)S(1)} %copy-done, f32[1,1,512,512]{2,3,1,0:T(8,128)} %copy.31), kind=kOutput, calls=%fused_computation.62 | convolution fusion | flops 541065216 | bytes 6291460 | tf_op jit(solution)/shard_map/td,th->dh/dot_general | solution.py:138
  73.4 3.2 %collective-permute-start = (f32[512,512]{0,1:T(8,128)}, f32[512,512]{0,1:T(8,128)}, u32[]{:S(2)}, u32[]{:S(2)}) collective-permute-start(f32[512,512]{0,1:T(8,128)} %broadcast_multiply_fusion.1), channel_id=1, source_target_pairs={{0,32},{32,0},{64,96},{96,64},{128,160},{160,128},{192,224},{224,1... | collective-permute-start | bytes 3145736 | tf_op jit(solution)/shard_map/ppermute | solution.py:22
  78.3 2.9 copy.39
  81.2 2.5 copy.41
  83.7 4.9 %multiply_reduce_fusion.1 = (f32[]{:T(128)}, f32[512,512]{0,1:T(8,128)}) fusion(f32[1,1,512,512]{2,3,1,0:T(8,128)S(1)} %copy.38, f32[1,1,512,512]{2,3,1,0:T(8,128)} %copy.41, bf16[1024,512]{1,0:T(8,128)(2,1)} %bitcast.186, bf16[1,1,1024,512]{3,2,1,0:T(8,128)(2,1)S(1)} %copy-done, f32[1,1,512,512]{2,3,1,0:T(8,128)} %copy.39), kind=kOutput, calls=%fused_computation.60 | convolution fusion | flops 541065216 | bytes 6291460 | tf_op jit(solution)/shard_map/td,th->dh/dot_general | solution.py:149
  101.1 39.1 %collective-permute-start.3 = (f32[]{:T(128)}, f32[]{:T(128)}, u32[]{:S(2)}, u32[]{:S(2)}) collective-permute-start(f32[]{:T(128)} %add.79), channel_id=1, source_target_pairs={{0,64},{32,96},{64,0},{96,32},{128,192},{160,224},{192,128},{224,1... | collective-permute-start | bytes 20 | tf_op jit(solution)/shard_map/ppermute | solution.py:22
  140.2 47.3 %collective-permute-done.3 = f32[]{:T(128)} collective-permute-done((f32[]{:T(128)}, f32[]{:T(128)}, u32[]{:S(2)}, u32[]{:S(2)}) %collective-permute-start.3) | collective-permute-done | bytes 36 | tf_op jit(solution)/shard_map/ppermute | solution.py:22
  188.2 2.5 select_bitcast_fusion.1
  190.7 2.0 select_bitcast_fusion
  193.1 46.3 %collective-permute-done.6 = f32[2,512,512]{1,2,0:T(8,128)S(1)} collective-permute-done((f32[2,512,512]{1,2,0:T(8,128)S(1)}, f32[2,512,512]{1,2,0:T(8,128)S(1)}, u32[]{:S(2)}, u32[]{:S(2)}) %collective-permute-start.6) | collective-permute-done | bytes 2097184 | tf_op jit(solution)/shard_map/ppermute | solution.py:22
  242.5 43.2 %collective-permute-start.8 = (f32[]{:T(128)}, f32[]{:T(128)}, u32[]{:S(2)}, u32[]{:S(2)}) collective-permute-start(f32[]{:T(128)} %bitcast.10), channel_id=1, source_target_pairs={{0,1},{1,0},{2,3},{3,2},{4,5},{5,4},{6,7},{7,6},{8,9},{9,8},{10,11... | collective-permute-start | bytes 20 | tf_op jit(solution)/shard_map/ppermute | solution.py:22
  287.4 2.7 collective-permute-start.9
  292.0 3.0 %divide_select_fusion = f32[2,512,512]{1,2,0:T(8,128)S(1)} fusion(f32[2,512,512]{1,2,0:T(8,128)} %fusion.63, f32[2,512,512]{1,2,0:T(8,128)} %collective-permute-done.7, f32[1,512,512]{1,2,0:T(8,128)S(1)} %select_bitcast_fusion, f32[1,512,512]{1,2,0:T(8,128)S(1)} %select_bitcast_fusion.1, f32[]{:T(128)S(6)} %sub.32, pred[]{:T(512)S(6)} %gt.7), kind=kLoop, calls=%fused_computation.23 | loop fusion | flops 2097152 | bytes 8388613 | tf_op jit(solution)/shard_map/jit(_where)/select_n | solution.py:88
  (94 shorter events, 46.1 us)
Async XLA Ops:
  0.6 2.8 copy-start
  0.6 2.8 copy-start.8
  17.0 4.5 %copy-start.5 = (bf16[1,512,512]{1,2,0:T(8,128)(2,1)S(1)}, bf16[1,512,512]{1,2,0:T(8,128)(2,1)}, u32[]{:S(2)}) copy-start(bf16[1,512,512]{1,2,0:T(8,128)(2,1)} %copy.65) | copy-start | bytes 1572868 | tf_op jit(solution)/shard_map/while
  26.0 2.0 copy-start.1
  44.2 4.5 %copy-start.5 = (bf16[1,512,512]{1,2,0:T(8,128)(2,1)S(1)}, bf16[1,512,512]{1,2,0:T(8,128)(2,1)}, u32[]{:S(2)}) copy-start(bf16[1,512,512]{1,2,0:T(8,128)(2,1)} %copy.65) | copy-start | bytes 1572868 | tf_op jit(solution)/shard_map/while
  53.1 2.0 copy-start.1
  60.7 2.7 copy-start.13
  60.7 4.0 %copy-start.2 = (f32[1,1,512,512]{2,3,1,0:T(8,128)S(1)}, f32[1,1,512,512]{2,3,1,0:T(8,128)}, u32[]{:S(2)}) copy-start(f32[1,1,512,512]{2,3,1,0:T(8,128)} %copy.30) | copy-start | bytes 3145732
  65.6 5.3 %copy-start.14 = (s32[1,1,2]{2,1,0:T(1,128)S(1)}, s32[1,1,2]{2,1,0:T(1,128)}, u32[]{:S(2)}) copy-start(s32[1,1,2]{2,1,0:T(1,128)} %param.21) | copy-start | bytes 28
  69.6 3.8 %copy-start.11 = (f32[512,512]{0,1:T(8,128)}, f32[512,512]{0,1:T(8,128)S(1)}, u32[]{:S(2)}) copy-start(f32[512,512]{0,1:T(8,128)S(1)} %get-tuple-element.85) | copy-start | bytes 3145732
  73.4 18.9 %collective-permute-start = (f32[512,512]{0,1:T(8,128)}, f32[512,512]{0,1:T(8,128)}, u32[]{:S(2)}, u32[]{:S(2)}) collective-permute-start(f32[512,512]{0,1:T(8,128)} %broadcast_multiply_fusion.1), channel_id=1, source_target_pairs={{0,32},{32,0},{64,96},{96,64},{128,160},{160,128},{192,224},{224,1... | collective-permute-start | bytes 3145736 | tf_op jit(solution)/shard_map/ppermute | solution.py:22
  78.2 12.6 %copy-start.3 = (f32[1,1,512,512]{2,3,1,0:T(8,128)}, f32[1,1,512,512]{2,3,1,0:T(8,128)S(1)}, u32[]{:S(2)}) copy-start(f32[1,1,512,512]{2,3,1,0:T(8,128)S(1)} %copy.38) | copy-start | bytes 3145732
  92.3 3.2 %collective-permute-start.4 = (f32[512,512]{0,1:T(8,128)S(1)}, f32[512,512]{0,1:T(8,128)S(1)}, u32[]{:S(2)}, u32[]{:S(2)}) collective-permute-start(f32[512,512]{0,1:T(8,128)S(1)} %broadcast_multiply_fusion), channel_id=1, source_target_pairs={{0,32},{32,0},{64,96},{96,64},{128,160},{160,128},{192,224},{224,1... | collective-permute-start | bytes 3145736 | tf_op jit(solution)/shard_map/ppermute | solution.py:22
  94.2 94.0 %copy-start.10 = (f32[512,512]{0,1:T(8,128)}, f32[512,512]{0,1:T(8,128)S(1)}, u32[]{:S(2)}) copy-start(f32[512,512]{0,1:T(8,128)S(1)} %add.77) | copy-start | bytes 3145732
  94.2 94.0 %collective-permute-start.1 = (f32[512,512]{0,1:T(8,128)S(1)}, f32[512,512]{0,1:T(8,128)}, u32[]{:S(2)}, u32[]{:S(2)}) collective-permute-start(f32[512,512]{0,1:T(8,128)S(1)} %add.77), channel_id=1, source_target_pairs={{0,64},{32,96},{64,0},{96,32},{128,192},{160,224},{192,128},{224,1... | collective-permute-start | bytes 3145736 | tf_op jit(solution)/shard_map/ppermute | solution.py:22
  96.7 94.0 %collective-permute-start.5 = (f32[512,512]{0,1:T(8,128)}, f32[512,512]{0,1:T(8,128)}, u32[]{:S(2)}, u32[]{:S(2)}) collective-permute-start(f32[512,512]{0,1:T(8,128)} %add.87), channel_id=1, source_target_pairs={{0,64},{32,96},{64,0},{96,32},{128,192},{160,224},{192,128},{224,1... | collective-permute-start | bytes 3145736 | tf_op jit(solution)/shard_map/ppermute | solution.py:22
  97.8 2.6 collective-permute-start.2
  101.1 86.4 %collective-permute-start.3 = (f32[]{:T(128)}, f32[]{:T(128)}, u32[]{:S(2)}, u32[]{:S(2)}) collective-permute-start(f32[]{:T(128)} %add.79), channel_id=1, source_target_pairs={{0,64},{32,96},{64,0},{96,32},{128,192},{160,224},{192,128},{224,1... | collective-permute-start | bytes 20 | tf_op jit(solution)/shard_map/ppermute | solution.py:22
  188.2 2.6 copy-start.4
  188.2 2.6 copy-start.12
  193.0 46.4 %collective-permute-start.6 = (f32[2,512,512]{1,2,0:T(8,128)S(1)}, f32[2,512,512]{1,2,0:T(8,128)S(1)}, u32[]{:S(2)}, u32[]{:S(2)}) collective-permute-start(f32[2,512,512]{1,2,0:T(8,128)S(1)} %fusion.19), channel_id=1, source_target_pairs={{0,1},{1,0},{2,3},{3,2},{4,5},{5,4},{6,7},{7,6},{8,9},{9,8},{10,11... | collective-permute-start | bytes 6291464 | tf_op jit(solution)/shard_map/ppermute | solution.py:22
  241.3 50.7 %collective-permute-start.7 = (f32[2,512,512]{1,2,0:T(8,128)}, f32[2,512,512]{1,2,0:T(8,128)}, u32[]{:S(2)}, u32[]{:S(2)}) collective-permute-start(f32[2,512,512]{1,2,0:T(8,128)} %fusion.63), channel_id=1, source_target_pairs={{0,2},{1,3},{2,0},{3,1},{4,6},{5,7},{6,4},{7,5},{8,10},{9,11},{10,... | collective-permute-start | bytes 6291464 | tf_op jit(solution)/shard_map/ppermute | solution.py:22
  242.5 44.3 %collective-permute-start.8 = (f32[]{:T(128)}, f32[]{:T(128)}, u32[]{:S(2)}, u32[]{:S(2)}) collective-permute-start(f32[]{:T(128)} %bitcast.10), channel_id=1, source_target_pairs={{0,1},{1,0},{2,3},{3,2},{4,5},{5,4},{6,7},{7,6},{8,9},{9,8},{10,11... | collective-permute-start | bytes 20 | tf_op jit(solution)/shard_map/ppermute | solution.py:22
  287.4 3.9 %collective-permute-start.9 = (f32[]{:T(128)}, f32[]{:T(128)}, u32[]{:S(2)}, u32[]{:S(2)}) collective-permute-start(f32[]{:T(128)} %add.91), channel_id=1, source_target_pairs={{0,2},{1,3},{2,0},{3,1},{4,6},{5,7},{6,4},{7,5},{8,10},{9,11},{10,... | collective-permute-start | bytes 20 | tf_op jit(solution)/shard_map/ppermute | solution.py:22
  (5 other events, 6.4 us)
where the time goes:
time: 301 us; the launch traced here: 298 us
  waiting for transfers between devices  96.1 us (32%)
  starting transfers between devices  94.1 us (31%)
  matrix products  47.8 us (16%)
  local copies, waits for them, and re-layouts  35.3 us (12%)
  other arithmetic  17 us (6%)
  between operations  7.28 us (2%)
    ppermute x10, waiting for transfers between devices, from_partner(): lax.ppermute(shard, axis, [(i, i ^ 1 << stride) for i in range(lax.axis_s...  96.1 us
    ppermute x10, starting transfers between devices, from_partner(): lax.ppermute(shard, axis, [(i, i ^ 1 << stride) for i in range(lax.axis_s...  94.1 us
    unnamed x30, local copies, waits for them, and re-layouts  16.9 us
    sub x2, matrix products, attend_back(): exponent = jnp.exp(scores - highest)  10.1 us
    dynamic_slice x16, local copies, waits for them, and re-layouts, per_device(): lax.map(attend_back, (by_sequence(queries), by_sequence(key_rows), by_seq...  9.83 us
    dot_general x2, matrix products, attend_back(): jnp.einsum('hqk,khd->qhd', prob_low, value_heads, preferred_element_type=...  8.89 us
    dot_general x2, matrix products, attend_back(): jnp.einsum('qhd,khd->hqk', grad_heads, value_heads, preferred_element_typ...  8.87 us
    dot_general x2, matrix products, attend_back(): jnp.einsum('hqk,qhd->khd', grad_score, query_heads, preferred_element_typ...  7.13 us
  transfers between devices with their start and end apart: 10, of which 4 were waited for; matrix products, arithmetic and copies ran while one was open for 7% of the time, Pallas kernels for 0%

commit v1 on v0

v1 whole, which is shorter than its diff:
```python
import functools
import math
import jax
import jax.numpy as jnp
from jax import lax
from jax.experimental import pallas as pl
from jax.experimental.pallas import tpu as pltpu
from jax.sharding import PartitionSpec as P

HD = 64
SEQ = 512
beta_one = 0.9
beta_two = 0.999
epsilon = 1e-06
decay_rate = 0.01
learn_rate = 0.1
correction_one = 1.0 - math.exp(100.0 * math.log(0.9))
correction_two = 1.0 - math.exp(100.0 * math.log(0.999))
QUAD = 256
PAIR = 128
bf16 = jnp.bfloat16
f32 = jnp.float32

def dot(a, b, ca=1, cb=0):
    return lax.dot_general(a, b, (((ca,), (cb,)), ((), ())), preferred_element_type=f32)

def lamb_direction(w, m, s, g):
    first = beta_one * m + (1.0 - beta_one) * g
    second = beta_two * s + (1.0 - beta_two) * g * g
    return first / correction_one / (jnp.sqrt(second / correction_two) + epsilon) + decay_rate * w

def step_kernel(f_ref, v_ref, og_ref, wq_ref, wk_ref, mq_ref, sq_ref, mk_ref, sk_ref,
                nq_ref, nk_ref, ft, qs, ks, kt, gqt, gks, u_all, norms, *, qb):
    step = pl.program_id(0)
    last = pl.num_programs(0) - 1
    tokens, width = f_ref.shape
    in_scale = 1.0 / math.sqrt(width)
    soft_scale = math.log2(math.e) / math.sqrt(HD)

    @pl.when(step == 0)
    def _():
        ft[...] = f_ref[...].T
        for i in range(4):
            norms[i] = 0.0

    feats = f_ref[...]
    qs[...] = (dot(feats, wq_ref[...].astype(bf16)) * in_scale).astype(bf16)
    keys = (dot(feats, wk_ref[...].astype(bf16)) * in_scale).astype(bf16)
    ks[...] = keys
    kt[...] = keys.T
    lane = lax.broadcasted_iota(jnp.int32, (1, PAIR), 1)
    for s in range(tokens // SEQ):
        rows = slice(s * SEQ, (s + 1) * SEQ)
        for p in range(QUAD // PAIR):
            lanes = slice(p * PAIR, (p + 1) * PAIR)
            k_pair = ks[rows, lanes]
            v_pair = v_ref[rows, lanes]
            gk = jnp.zeros((SEQ, PAIR), f32)
            for h in range(PAIR // HD):
                keep = (lane >= h * HD) & (lane < (h + 1) * HD)
                head = p * PAIR + h * HD
                for b in range(SEQ // qb):
                    at = slice(s * SEQ + b * qb, s * SEQ + (b + 1) * qb)
                    q_head = jnp.where(keep, qs[at, lanes], jnp.zeros((), bf16))
                    o_head = jnp.where(keep, og_ref[at, lanes] * (1.0 / math.sqrt(HD)), 0.0).astype(bf16)
                    st = dot(k_pair, q_head, 1, 1)
                    gp = dot(v_pair, o_head, 1, 1)
                    top = jnp.max(st, axis=0, keepdims=True)
                    e = jnp.exp2((st - top) * soft_scale)
                    inv = 1.0 / jnp.sum(e, axis=0, keepdims=True)
                    prob = e * inv
                    low = prob.astype(bf16).astype(f32)
                    delta = jnp.sum(low * gp, axis=0, keepdims=True)
                    ds = (prob * (gp - delta)).astype(bf16)
                    gk = gk + dot(ds, q_head)
                    gqt[head:head + HD, at] = dot(kt[head:head + HD, rows], ds).astype(bf16)
            gks[rows, lanes] = gk.astype(bf16)
    gq = dot(ft[...], gqt[...], 1, 1) * in_scale
    gk = dot(ft[...], gks[...]) * in_scale
    wq = wq_ref[...]
    wk = wk_ref[...]
    uq = lamb_direction(wq, mq_ref[...], sq_ref[...], gq)
    uk = lamb_direction(wk, mk_ref[...], sk_ref[...], gk)
    cols = pl.ds(pl.multiple_of(step * QUAD, QUAD), QUAD)
    u_all[0, :, cols] = uq
    u_all[1, :, cols] = uk
    nq_ref[:, cols] = wq
    nk_ref[:, cols] = wk
    norms[0] += jnp.sum(wq * wq)
    norms[1] += jnp.sum(uq * uq)
    norms[2] += jnp.sum(wk * wk)
    norms[3] += jnp.sum(uk * uk)

    @pl.when(step == last)
    def _():
        def ratio(i):
            w2 = jnp.full((1, 1), norms[i], f32)
            u2 = jnp.full((1, 1), norms[i + 1], f32)
            return learn_rate * jnp.sqrt(w2) / jnp.sqrt(u2 + epsilon)
        nq_ref[...] = nq_ref[...] - ratio(0) * u_all[0]
        nk_ref[...] = nk_ref[...] - ratio(2) * u_all[1]

def local_step(f, v, og, wq, wk, mq, sq, mk, sk, qb=512):
    tokens, width = f.shape
    heads = wq.shape[1]
    full = pl.BlockSpec((tokens, width), lambda i: (0, 0))
    tok = pl.BlockSpec((tokens, QUAD), lambda i: (0, i))
    wsp = pl.BlockSpec((width, QUAD), lambda i: (0, i))
    osp = pl.BlockSpec((width, heads), lambda i: (0, 0))
    return pl.pallas_call(
        functools.partial(step_kernel, qb=qb),
        grid=(heads // QUAD,),
        in_specs=[full, tok, tok] + [wsp] * 6,
        out_specs=[osp, osp],
        out_shape=[jax.ShapeDtypeStruct((width, heads), f32)] * 2,
        scratch_shapes=[
            pltpu.VMEM((width, tokens), bf16),
            pltpu.VMEM((tokens, QUAD), bf16),
            pltpu.VMEM((tokens, QUAD), bf16),
            pltpu.VMEM((QUAD, tokens), bf16),
            pltpu.VMEM((QUAD, tokens), bf16),
            pltpu.VMEM((tokens, QUAD), bf16),
            pltpu.VMEM((2, width, heads), f32),
            pltpu.SMEM((4,), f32),
        ],
        compiler_params=pltpu.CompilerParams(vmem_limit_bytes=56 << 20),
    )(f, v, og, wq, wk, mq, sq, mk, sk)


CHUNKS = 2
GROUP = 4


def ring(axis, step):
    size = lax.axis_size(axis)
    return [(i, i - i % GROUP + (i + step) % GROUP) for i in range(size)]


def swap(axis, bit):
    return [(i, i ^ bit) for i in range(lax.axis_size(axis))]


def member_facts(members):
    r = lax.axis_index("row")
    c = lax.axis_index("col")
    grid = lax.all_gather(members, ("row", "col"))
    grid = grid.reshape(lax.axis_size("row"), lax.axis_size("col"), 2)
    base_r = r - r % GROUP
    base_c = c - c % GROUP
    here = lax.dynamic_slice_in_dim(grid, c, 1, axis=1)[:, 0, 0]
    column = lax.dynamic_slice_in_dim(here, base_r, GROUP)
    count_a = jnp.sum(column)
    pair = lax.dynamic_slice_in_dim(grid, r - r % 2, 2, axis=0)
    pair = jnp.where(r % 2 == 0, pair, pair[::-1])
    own = lax.dynamic_slice_in_dim(pair, c, 1, axis=1)[:, 0]
    count_b = jnp.sum(lax.dynamic_slice_in_dim(pair[:, :, 1], base_c, GROUP, axis=1), axis=1)
    return own[:, 0], own[:, 1], jnp.maximum(count_a, 1.0), jnp.maximum(count_b, 1.0)


def average(full, facts, at, rows):
    in_a, in_b, count_a, count_b = facts
    core = lax.axis_index("row") % 2
    y = lax.axis_index("col") % GROUP
    half = full.shape[0] // 2
    width = full.shape[1]
    mine = lax.dynamic_slice_in_dim(full, core * half + at, rows)
    other = lax.dynamic_slice_in_dim(full, (1 - core) * half + at, rows)
    theirs = lax.ppermute(other, "row", swap("row", 1))
    part = in_a[0] * mine + in_a[1] * theirs
    far = lax.ppermute(part, "row", swap("row", 2))
    mean = (part + far) / count_a
    held = jnp.stack([jnp.where(in_a[0] > 0, mean, mine), jnp.where(in_a[1] > 0, mean, theirs)])
    piece = rows // GROUP
    cut = piece // 2

    def block(d):
        got = lax.dynamic_slice_in_dim(held, (y + d) % GROUP * piece, piece, axis=1)
        return got * in_b[:, None, None]

    opposite = block(2)
    fwd = lax.ppermute(opposite[:, :cut], "col", ring("col", 1))
    bwd = lax.ppermute(opposite[:, cut:], "col", ring("col", -1))
    none = jnp.zeros_like(fwd)
    to_next = block(1) + jnp.concatenate([fwd, none], axis=1)
    to_prev = block(3) + jnp.concatenate([none, bwd], axis=1)
    from_prev = lax.ppermute(to_next, "col", ring("col", 1))
    from_next = lax.ppermute(to_prev, "col", ring("col", -1))
    total = (block(0) + from_prev + from_next) / count_b[:, None, None]
    before = lax.ppermute(total, "col", ring("col", 1))
    after = lax.ppermute(total, "col", ring("col", -1))
    low = lax.ppermute(before[:, :cut], "col", ring("col", 1))
    high = lax.ppermute(after[:, cut:], "col", ring("col", -1))
    cycle = jnp.concatenate([total, after, low, high, before] * 2, axis=1)
    means = lax.dynamic_slice_in_dim(cycle, (GROUP - y) % GROUP * piece, rows, axis=1)
    final = jnp.where(in_b[:, None, None] > 0, means, held)
    mate = lax.ppermute(final[1], "row", swap("row", 1))
    return final[0], mate


def per_device(
    features,
    values,
    out_grad,
    query_weight,
    key_weight,
    query_mean,
    query_square,
    key_mean,
    key_square,
    members,
):
    facts = member_facts(members[0, 0].astype(f32))
    new = local_step(
        features[0, 0],
        values[0, 0],
        out_grad[0, 0],
        query_weight[0, 0],
        key_weight[0, 0],
        query_mean[0, 0],
        query_square[0, 0],
        key_mean[0, 0],
        key_square[0, 0],
    )
    core = lax.axis_index("row") % 2
    outs = []
    per_matrix = CHUNKS // 2
    for full in new:
        rows = full.shape[0] // 2 // per_matrix
        parts = [average(full, facts, j * rows, rows) for j in range(per_matrix)]
        own = jnp.concatenate([p[0] for p in parts])
        mate = jnp.concatenate([p[1] for p in parts])
        first = jnp.where(core == 0, own, mate)
        second = jnp.where(core == 0, mate, own)
        outs.append(jnp.concatenate([first, second])[None, None])
    return tuple(outs)


def solution(mesh):
    mats = P("row", "col", None, None)
    return jax.shard_map(
        per_device,
        mesh=mesh,
        in_specs=(mats,) * 9 + (P("row", "col", None),),
        out_specs=(mats, mats),
        check_vma=False,
    )
```

time: 301 us -> 732 us (2.43)
  blocking collectives: 0 us -> 562 us
  waiting for transfers between devices: 96.1 us -> 12.1 us
  matrix products: 47.8 us -> 0 us
  Pallas kernels: 0 us -> 22.4 us
  local copies, waits for them, and re-layouts: 35.3 us -> 18.5 us
    all_gather x0 -> x1, blocking collectives: none -> 562 us  [member_facts(): grid = lax.all_gather(members, ('row', 'col'))]
    ppermute x10 -> x22, waiting for transfers between devices: 96.1 us -> 12.1 us  [the longest x2 4.03 us: average(): from_prev = lax.ppermute(to_next, 'col', ring('col', 1))]
    dot_general x12 -> x0, matrix products: 37.7 us -> none  [the longest x2 8.89 us: attend_back(): jnp.einsum('hqk,khd->qhd', prob_low, value_heads, preferred_element_type=...]
    pallas_call x0 -> x1, Pallas kernels: none -> 22.4 us  [local_step(): pl.pallas_call(functools.partial(step_kernel, qb=qb), grid=(heads // QUAD...]
    sub x2 -> x0, matrix products: 10.1 us -> none  [attend_back(): exponent = jnp.exp(scores - highest)]
    ppermute x10 -> x22, starting transfers between devices: 94.1 us -> 101 us  [the longest x2 72.2 us: average(): mate = lax.ppermute(final[1], 'row', swap('row', 1))]
    unnamed x30 -> x29, local copies, waits for them, and re-layouts: 16.9 us -> 12 us
  transfers between devices with their start and end apart: 10 -> 22, of which waited for: 4 -> 7; matrix products, arithmetic and copies ran while one was open for 7% -> 2% of each run, Pallas kernels for 0% -> 0%
where the time goes in v1:
time: 732 us
  blocking collectives  562 us (77%)
  starting transfers between devices  101 us (14%)
  Pallas kernels  22.4 us (3%)
  local copies, waits for them, and re-layouts  18.5 us (3%)
  other arithmetic  13.3 us (2%)
  waiting for transfers between devices  12.1 us (2%)
    all_gather x1, blocking collectives, member_facts(): grid = lax.all_gather(members, ('row', 'col'))  562 us
    ppermute x2, starting transfers between devices, average(): mate = lax.ppermute(final[1], 'row', swap('row', 1))  72.2 us
    pallas_call x1, Pallas kernels, local_step(): pl.pallas_call(functools.partial(step_kernel, qb=qb), grid=(heads // QUAD...  22.4 us
  transfers between devices with their start and end apart: 22, of which 7 were waited for; matrix products, arithmetic and copies ran while one was open for 2% of the time, Pallas kernels for 0%

profile of v1, /device:TPU:1, one launch (start us, length us, event | category | flops | bytes accessed | tf_op | source)
XLA Modules:
  0.0 731.7 jit_solution(471841482359019531)
XLA Ops:
  0.7 22.4 %shard_map.113 = (f32[512,512]{1,0:T(8,128)}, f32[512,512]{1,0:T(8,128)}) custom-call(bf16[1024,512]{1,0:T(8,128)(2,1)} %bitcast.42, bf16[1024,512]{1,0:T(8,128)(2,1)} %bitcast.43, bf16[1024,512]{1,0:T(8,128)(2,1)} %bitcast.44, f32[512,512]{1,0:T(8,128)} %bitcast.45, f32[512,512]{1,0:T(8,128)} %bitcast.46, f32[512,512]{1,0:T(8,128)} %bitcast.47, ...), custom_call_target="tpu_custom_call" | custom-call | tf_op jit(solution)/shard_map/pallas_call | solution.py:110
  23.1 2.0 constant_dynamic-slice_fusion
  25.1 3.3 collective-permute-start.11
  28.4 1.9 constant_dynamic-slice_fusion.3
  30.3 562.1 %all-gather = f32[256,1,2]{2,1,0:T(1,128)S(1)} all-gather(f32[1,1,2]{2,1,0:T(1,128)S(1)} %convert_element_type.13), channel_id=2, replica_groups=mesh['row'=8,'col'=32] {'row','col'}, dimensions={0}, use_global_device_ids=true | all-gather | bytes 2056 | tf_op jit(solution)/shard_map/all_gather | solution.py:146
  593.1 2.1 multiply_add_fusion
  597.9 1.3 multiply_add_fusion.1
  599.3 2.6 collective-permute-start.1
  601.9 2.9 collective-permute-done.12
  604.8 1.5 select_bitcast_fusion.1
  606.5 2.7 collective-permute-start.15
  612.5 3.0 collective-permute-start.4
  615.6 2.7 collective-permute-start.16
  619.6 2.2 collective-permute-start.5
  622.2 3.9 collective-permute-done.3
  627.7 2.3 collective-permute-start.17
  629.9 2.7 collective-permute-start.6
  632.6 1.6 collective-permute-done.18
  634.3 2.7 collective-permute-start.20
  637.4 2.7 collective-permute-start.9
  644.3 1.7 constant_dynamic-update-slice_fusion.14
  653.6 2.1 fusion
  655.7 72.1 %collective-permute-start.10 = (f32[256,512]{1,0:T(8,128)S(1)}, f32[256,512]{1,0:T(8,128)S(1)}, u32[]{:S(2)}, u32[]{:S(2)}) collective-permute-start(f32[256,512]{1,0:T(8,128)S(1)} %slice_bitcast_fusion.2), channel_id=1, source_target_pairs={{0,32},{32,0},{64,96},{96,64},{128,160},{160,128},{192,224},{224,1... | collective-permute-start | bytes 1572872 | tf_op jit(solution)/shard_map/ppermute | solution.py:196
  728.0 1.4 collective-permute-done.10
  (88 shorter events, 23.0 us)
Async XLA Ops:
  23.0 570.1 %copy-start.1 = (f32[512,512]{1,0:T(8,128)S(1)}, f32[512,512]{1,0:T(8,128)}, u32[]{:S(2)}) copy-start(f32[512,512]{1,0:T(8,128)} %get-tuple-element.5) | copy-start | bytes 3145732
  23.1 574.9 %copy-start = (f32[512,512]{1,0:T(8,128)S(1)}, f32[512,512]{1,0:T(8,128)}, u32[]{:S(2)}) copy-start(f32[512,512]{1,0:T(8,128)} %get-tuple-element.4) | copy-start | bytes 3145732
  25.1 568.0 %collective-permute-start.11 = (f32[256,512]{1,0:T(8,128)}, f32[256,512]{1,0:T(8,128)S(1)}, u32[]{:S(2)}, u32[]{:S(2)}) collective-permute-start(f32[256,512]{1,0:T(8,128)} %constant_dynamic-slice_fusion), channel_id=1, source_target_pairs={{0,32},{32,0},{64,96},{96,64},{128,160},{160,128},{192,224},{224,1... | collective-permute-start | bytes 1572872 | tf_op jit(solution)/shard_map/ppermute | solution.py:168
  30.2 567.7 %collective-permute-start = (f32[256,512]{1,0:T(8,128)}, f32[256,512]{1,0:T(8,128)S(1)}, u32[]{:S(2)}, u32[]{:S(2)}) collective-permute-start(f32[256,512]{1,0:T(8,128)} %constant_dynamic-slice_fusion.3), channel_id=1, source_target_pairs={{0,32},{32,0},{64,96},{96,64},{128,160},{160,128},{192,224},{224,1... | collective-permute-start | bytes 1572872 | tf_op jit(solution)/shard_map/ppermute | solution.py:168
  595.2 9.6 %collective-permute-start.12 = (f32[256,512]{1,0:T(8,128)}, f32[256,512]{1,0:T(8,128)}, u32[]{:S(2)}, u32[]{:S(2)}) collective-permute-start(f32[256,512]{1,0:T(8,128)} %multiply_add_fusion), channel_id=1, source_target_pairs={{0,64},{32,96},{64,0},{96,32},{128,192},{160,224},{192,128},{224,1... | collective-permute-start | bytes 1572872 | tf_op jit(solution)/shard_map/ppermute | solution.py:170
  599.3 10.9 %collective-permute-start.1 = (f32[256,512]{1,0:T(8,128)S(1)}, f32[256,512]{1,0:T(8,128)S(1)}, u32[]{:S(2)}, u32[]{:S(2)}) collective-permute-start(f32[256,512]{1,0:T(8,128)S(1)} %multiply_add_fusion.1), channel_id=1, source_target_pairs={{0,64},{32,96},{64,0},{96,32},{128,192},{160,224},{192,128},{224,1... | collective-permute-start | bytes 1572872 | tf_op jit(solution)/shard_map/ppermute | solution.py:170
  606.4 5.1 collective-permute-start.13
  606.5 5.0 collective-permute-start.15
  612.4 5.8 collective-permute-start.2
  612.5 5.7 collective-permute-start.4
  615.6 6.6 collective-permute-start.14
  615.6 6.6 collective-permute-start.16
  619.2 6.9 collective-permute-start.3
  619.6 6.5 collective-permute-start.5
  627.3 6.9 collective-permute-start.18
  627.7 6.6 collective-permute-start.17
  629.9 7.1 collective-permute-start.7
  629.9 7.5 %collective-permute-start.6 = (f32[2,64,512]{2,1,0:T(8,128)S(1)}, f32[2,64,512]{2,1,0:T(8,128)S(1)}, u32[]{:S(2)}, u32[]{:S(2)}) collective-permute-start(f32[2,64,512]{2,1,0:T(8,128)S(1)} %get-tuple-element.27), channel_id=1, source_target_pairs={{0,3},{1,0},{2,1},{3,2},{4,7},{5,4},{6,5},{7,6},{8,11},{9,8},{10,9... | collective-permute-start | bytes 786440 | tf_op jit(solution)/shard_map/ppermute | solution.py:190
  634.2 7.4 %collective-permute-start.19 = (f32[2,32,512]{2,1,0:T(8,128)S(1)}, f32[2,32,512]{2,1,0:T(8,128)S(1)}, u32[]{:S(2)}, u32[]{:S(2)}) collective-permute-start(f32[2,32,512]{2,1,0:T(8,128)S(1)} %slice.88), channel_id=1, source_target_pairs={{0,1},{1,2},{2,3},{3,0},{4,5},{5,6},{6,7},{7,4},{8,9},{9,10},{10,1... | collective-permute-start | bytes 393224 | tf_op jit(solution)/shard_map/ppermute | solution.py:191
  634.3 7.9 %collective-permute-start.20 = (f32[2,32,512]{2,1,0:T(8,128)S(1)}, f32[2,32,512]{2,1,0:T(8,128)S(1)}, u32[]{:S(2)}, u32[]{:S(2)}) collective-permute-start(f32[2,32,512]{2,1,0:T(8,128)S(1)} %slice.89), channel_id=1, source_target_pairs={{0,3},{1,0},{2,1},{3,2},{4,7},{5,4},{6,5},{7,6},{8,11},{9,8},{10,9... | collective-permute-start | bytes 393224 | tf_op jit(solution)/shard_map/ppermute | solution.py:192
  637.1 6.6 collective-permute-start.8
  637.4 8.6 %collective-permute-start.9 = (f32[2,32,512]{2,1,0:T(8,128)S(1)}, f32[2,32,512]{2,1,0:T(8,128)S(1)}, u32[]{:S(2)}, u32[]{:S(2)}) collective-permute-start(f32[2,32,512]{2,1,0:T(8,128)S(1)} %slice.83), channel_id=1, source_target_pairs={{0,3},{1,0},{2,1},{3,2},{4,7},{5,4},{6,5},{7,6},{8,11},{9,8},{10,9... | collective-permute-start | bytes 393224 | tf_op jit(solution)/shard_map/ppermute | solution.py:192
  655.7 73.7 %collective-permute-start.10 = (f32[256,512]{1,0:T(8,128)S(1)}, f32[256,512]{1,0:T(8,128)S(1)}, u32[]{:S(2)}, u32[]{:S(2)}) collective-permute-start(f32[256,512]{1,0:T(8,128)S(1)} %slice_bitcast_fusion.2), channel_id=1, source_target_pairs={{0,32},{32,0},{64,96},{96,64},{128,160},{160,128},{192,224},{224,1... | collective-permute-start | bytes 1572872 | tf_op jit(solution)/shard_map/ppermute | solution.py:196
  727.9 2.6 collective-permute-start.21
  (4 other events, 25.3 us)

commit v2 on v1

v2 whole, which is shorter than its diff:
```python
import functools
import math

import jax
import jax.numpy as jnp
from jax import lax
from jax.experimental import pallas as pl
from jax.experimental.pallas import tpu as pltpu
from jax.sharding import PartitionSpec as P

HD = 64
SEQ = 512
QUAD = 256
PAIR = 128
GROUP = 4
NOTE = 8
CHUNKS = ((64, 0), (0, 64))
bf16 = jnp.bfloat16
f32 = jnp.float32

beta_one = 0.9
beta_two = 0.999
epsilon = 1e-06
decay_rate = 0.01
learn_rate = 0.1
correction_one = 1.0 - math.exp(100.0 * math.log(0.9))
correction_two = 1.0 - math.exp(100.0 * math.log(0.999))


def dot(a, b, ca=1, cb=0):
    return lax.dot_general(a, b, (((ca,), (cb,)), ((), ())), preferred_element_type=f32)


def lamb_direction(w, m, s, g):
    first = beta_one * m + (1.0 - beta_one) * g
    second = beta_two * s + (1.0 - beta_two) * g * g
    return first / correction_one / (jnp.sqrt(second / correction_two) + epsilon) + decay_rate * w


def lamb_ratio(norms):
    w2 = jnp.full((1, 1), norms[0], f32)
    u2 = jnp.full((1, 1), norms[1], f32)
    return learn_rate * jnp.sqrt(w2) / jnp.sqrt(u2 + epsilon)


def only_head(pair, h):
    lane = lax.broadcasted_iota(jnp.int32, (1, PAIR), 1)
    return jnp.where((lane >= h * HD) & (lane < (h + 1) * HD), pair, jnp.zeros((), pair.dtype))


def core_at():
    return lax.axis_index("row") % 2


def ring_at():
    return lax.axis_index("col") % GROUP


def deal(core, fill, mine, other, mat, size):
    for side, outs in ((core, mine), (1 - core, other)):
        at = side * (size // 2)
        for chunk, out in zip(CHUNKS, outs):
            count = chunk[mat]
            skip = chunk[0] if mat else 0
            if not count:
                continue
            for j in range(GROUP):
                to = j * sum(chunk) + skip
                out[to : to + count] = fill(pl.ds(pl.multiple_of(at, 8), count))
                at = at + count


def query_kernel(
    members, f_ref, v_ref, o_ref, wq_ref, wk_ref, m_ref, s_ref,
    mine0, other0, mine1, other1, facts_ref, ds_ref, q_ref, ft_ref, ks, kt, gqt, u_all, w_all, norms,
):
    step = pl.program_id(0)
    last = pl.num_programs(0) - 1
    tokens, width = f_ref.shape
    in_scale = 1.0 / math.sqrt(width)
    soft_scale = math.log2(math.e) / math.sqrt(HD)
    cols = pl.ds(pl.multiple_of(step * QUAD, QUAD), QUAD)

    @pl.when(step == 0)
    def _():
        ft_ref[...] = f_ref[...].T
        norms[0] = 0.0
        norms[1] = 0.0

    feats = f_ref[...]
    queries = (dot(feats, wq_ref[...].astype(bf16)) * in_scale).astype(bf16)
    q_ref[:, cols] = queries
    keys = (dot(feats, wk_ref[...].astype(bf16)) * in_scale).astype(bf16)
    ks[...] = keys
    kt[...] = keys.T
    for s in range(tokens // SEQ):
        rows = slice(s * SEQ, (s + 1) * SEQ)
        for p in range(QUAD // PAIR):
            lanes = slice(p * PAIR, (p + 1) * PAIR)
            for h in range(PAIR // HD):
                head = p * PAIR + h * HD
                o_head = only_head(o_ref[rows, lanes], h) * (1.0 / math.sqrt(HD))
                scores = dot(ks[rows, lanes], only_head(queries[rows, lanes], h), 1, 1)
                grad_prob = dot(v_ref[rows, lanes], o_head.astype(bf16), 1, 1)
                top = jnp.max(scores, axis=0, keepdims=True)
                e = jnp.exp2((scores - top) * soft_scale)
                prob = e * (1.0 / jnp.sum(e, axis=0, keepdims=True))
                prob_low = prob.astype(bf16).astype(f32)
                delta = jnp.sum(prob_low * grad_prob, axis=0, keepdims=True)
                grad_score = (prob * (grad_prob - delta)).astype(bf16)
                unit = step * (QUAD // HD) + head // HD
                ds_ref[unit, rows, :] = grad_score
                gqt[head : head + HD, rows] = dot(kt[head : head + HD, rows], grad_score).astype(bf16)
    grad = dot(ft_ref[...], gqt[...], 1, 1) * in_scale
    w = wq_ref[...]
    u = lamb_direction(w, m_ref[...], s_ref[...], grad)
    u_all[:, cols] = u
    w_all[:, cols] = w
    norms[0] += jnp.sum(w * w)
    norms[1] += jnp.sum(u * u)

    @pl.when(step == last)
    def _():
        ratio = lamb_ratio(norms)
        new = lambda here: w_all[here, :] - ratio * u_all[here, :]
        deal(core_at(), new, (mine0, mine1), (other0, other1), 0, width)
        at = lax.broadcasted_iota(jnp.int32, facts_ref.shape, 0)
        facts = jnp.where(at == 0, members[0], jnp.where(at == 1, members[1], 0)).astype(f32)
        facts_ref[...] = facts
        other0[mine0.shape[0] :] = facts


def key_kernel(
    ds_ref, q_ref, ft_ref, query_mine, query_other, w_ref, m_ref, s_ref,
    mine1, other1, gks, u_all, w_all, norms,
):
    step = pl.program_id(0)
    last = pl.num_programs(0) - 1
    tokens, width = q_ref.shape
    in_scale = 1.0 / math.sqrt(width)
    cols = pl.ds(pl.multiple_of(step * QUAD, QUAD), QUAD)

    @pl.when(step == 0)
    def _():
        norms[0] = 0.0
        norms[1] = 0.0

    for s in range(tokens // SEQ):
        rows = slice(s * SEQ, (s + 1) * SEQ)
        for p in range(QUAD // PAIR):
            lanes = pl.ds(pl.multiple_of(step * QUAD + p * PAIR, PAIR), PAIR)
            pair = q_ref[rows, lanes]
            grad = jnp.zeros((SEQ, PAIR), f32)
            for h in range(PAIR // HD):
                unit = step * (QUAD // HD) + p * (PAIR // HD) + h
                grad = grad + dot(ds_ref[unit, rows, :], only_head(pair, h))
            gks[rows, p * PAIR : (p + 1) * PAIR] = grad.astype(bf16)
    grad = dot(ft_ref[...], gks[...]) * in_scale
    w = w_ref[...]
    u = lamb_direction(w, m_ref[...], s_ref[...], grad)
    u_all[:, cols] = u
    w_all[:, cols] = w
    norms[0] += jnp.sum(w * w)
    norms[1] += jnp.sum(u * u)

    @pl.when(step == last)
    def _():
        ratio = lamb_ratio(norms)
        new = lambda here: w_all[here, :] - ratio * u_all[here, :]
        deal(core_at(), new, (None, mine1), (None, other1), 1, width)
        for j in range(GROUP):
            here = slice(j * sum(CHUNKS[1]), j * sum(CHUNKS[1]) + CHUNKS[1][0])
            if CHUNKS[1][0]:
                mine1[here] = query_mine[here]
                other1[here] = query_other[here]


SCALARS = pl.BlockSpec(memory_space=pltpu.SMEM)
STAYS = pl.BlockSpec(memory_space=pltpu.VMEM)


def in_hbm(*xs):
    return [pltpu.with_memory_space_constraint(x, pltpu.HBM) for x in xs]


def in_vmem(*xs):
    return [pltpu.with_memory_space_constraint(x, pltpu.VMEM) for x in xs]


def chunk_rows(c):
    return GROUP * sum(CHUNKS[c])


def query_step(members, f, v, o, wq, wk, m, s):
    tokens, width = f.shape
    heads = wq.shape[1]
    tok = pl.BlockSpec((tokens, QUAD), lambda i: (0, i))
    mat = pl.BlockSpec((width, QUAD), lambda i: (0, i))
    full = pl.BlockSpec((tokens, width), lambda i: (0, 0))
    later = chunk_rows(1) if CHUNKS[1][0] else NOTE
    shapes = [(chunk_rows(0), heads), (chunk_rows(0) + NOTE, heads), (later, heads), (later, heads), (NOTE, heads)]
    return pl.pallas_call(
        query_kernel,
        grid=(heads // QUAD,),
        in_specs=[SCALARS, full, tok, tok, mat, mat, mat, mat],
        out_specs=[STAYS] * 8,
        out_shape=[pltpu.VMEM(x, f32) for x in shapes]
        + [pltpu.VMEM(x, bf16) for x in ((heads // HD, tokens, SEQ), (tokens, heads), (width, tokens))],
        scratch_shapes=[
            pltpu.VMEM((tokens, QUAD), bf16),
            pltpu.VMEM((QUAD, tokens), bf16),
            pltpu.VMEM((QUAD, tokens), bf16),
            pltpu.VMEM((width, heads), f32),
            pltpu.VMEM((width, heads), f32),
            pltpu.SMEM((2,), f32),
        ],
        compiler_params=pltpu.CompilerParams(vmem_limit_bytes=36 << 20),
        name="query_step",
    )(members, *in_hbm(f, v, o, wq, wk, m, s))


def key_step(ds, q, ft, query_mine, query_other, w, m, s):
    tokens, heads = q.shape
    width = ft.shape[0]
    mat = pl.BlockSpec((width, QUAD), lambda i: (0, i))
    return pl.pallas_call(
        key_kernel,
        grid=(heads // QUAD,),
        in_specs=[STAYS] * 5 + [mat, mat, mat],
        out_specs=[STAYS] * 2,
        out_shape=[pltpu.VMEM((chunk_rows(1), heads), f32)] * 2,
        scratch_shapes=[
            pltpu.VMEM((tokens, QUAD), bf16),
            pltpu.VMEM((width, heads), f32),
            pltpu.VMEM((width, heads), f32),
            pltpu.SMEM((2,), f32),
        ],
        compiler_params=pltpu.CompilerParams(vmem_limit_bytes=24 << 20),
        name="key_step",
    )(*in_vmem(ds, q, ft, query_mine, query_other), *in_hbm(w, m, s))


A_ME, B_ME, A_MATE, B_MATE, A_CHIP, A_COUNT, B_COUNT, B_COUNT_MATE = range(8)
DISTANCES = (1, 3, 2)
NO_HBM = pl.CostEstimate(flops=0, transcendentals=0, bytes_accessed=0)


def small_call(kernel, name, shapes, *operands):
    got = pl.pallas_call(
        kernel,
        in_specs=[STAYS] * len(operands),
        out_specs=[STAYS] * len(shapes),
        out_shape=[pltpu.VMEM(s, f32) for s in shapes],
        compiler_params=pltpu.CompilerParams(vmem_limit_bytes=8 << 20),
        cost_estimate=NO_HBM,
        name=name,
    )(*in_vmem(*operands))
    return list(got)


def row(facts, i):
    return facts[i : i + 1, :]


def chip_sum(mine, theirs, facts, first):
    rows, width = mine.shape

    def kernel(mine_ref, theirs_ref, facts_ref, out_ref, *maybe_facts):
        f = facts_ref[...]
        if first:
            got = theirs_ref[rows:]
            at = lax.broadcasted_iota(jnp.int32, f.shape, 0)
            f = jnp.where(at == A_MATE, row(got, 0), jnp.where(at == B_MATE, row(got, 1), f))
            f = jnp.where(at == A_CHIP, row(f, A_ME) + row(f, A_MATE), f)
            out_ref[rows:] = f
            maybe_facts[0][...] = f
        out_ref[:rows] = row(f, A_ME) * mine_ref[...] + row(f, A_MATE) * theirs_ref[:rows]

    shapes = [(rows + NOTE, width), facts.shape] if first else [(rows, width)]
    got = small_call(kernel, "chip_sum", shapes, mine, theirs, facts)
    return got if first else got + [facts]


def row_mean(mine, theirs, far, facts, first):
    rows, width = mine.shape
    piece = rows // GROUP

    def kernel(mine_ref, theirs_ref, far_ref, facts_ref, own, s1, s2, s3, held, held_mate, *maybe_facts):
        f = facts_ref[...]
        if first:
            at = lax.broadcasted_iota(jnp.int32, f.shape, 0)
            count = row(f, A_CHIP) + row(far_ref[rows:], A_CHIP)
            f = jnp.where(at == A_COUNT, jnp.maximum(count, 1.0), f)
            maybe_facts[0][...] = f
        y = ring_at()
        for d, out in enumerate((own, s1, s2, s3)):
            here = pl.ds(pl.multiple_of((y + d) % GROUP * piece, 8), piece)
            m, t = mine_ref[here, :], theirs_ref[here, :]
            mean = (row(f, A_ME) * m + row(f, A_MATE) * t + far_ref[here, :]) / row(f, A_COUNT)
            m = jnp.where(row(f, A_ME) > 0, mean, m)
            t = jnp.where(row(f, A_MATE) > 0, mean, t)
            held[here, :] = m
            held_mate[here, :] = t
            out[:piece] = m * row(f, B_ME)
            out[piece : 2 * piece] = t * row(f, B_MATE)
            if first and d:
                out[2 * piece :] = f

    sent = (2 * piece + (NOTE if first else 0), width)
    shapes = [(2 * piece, width), sent, sent, sent, (rows, width), (rows, width)]
    if first:
        shapes = shapes + [facts.shape]
    got = small_call(kernel, "row_mean", shapes, mine, theirs, far, facts)
    return got if first else got + [facts]


def col_mean(own, got, facts, first):
    rows, width = own.shape
    piece = rows // 2

    def kernel(own_ref, g1, g2, g3, facts_ref, me, mate, *maybe_facts):
        f = facts_ref[...]
        if first:
            at = lax.broadcasted_iota(jnp.int32, f.shape, 0)
            notes = [g[rows:] for g in (g1, g2, g3)]
            count = sum([row(n, B_ME) for n in notes], row(f, B_ME))
            count_mate = sum([row(n, B_MATE) for n in notes], row(f, B_MATE))
            f = jnp.where(at == B_COUNT, jnp.maximum(count, 1.0), f)
            f = jnp.where(at == B_COUNT_MATE, jnp.maximum(count_mate, 1.0), f)
            maybe_facts[0][...] = f
        total = own_ref[...] + g1[:rows] + g2[:rows] + g3[:rows]
        me[...] = total[:piece] / row(f, B_COUNT)
        mate[...] = total[piece:] / row(f, B_COUNT_MATE)

    shapes = [(piece, width), (piece, width)] + ([facts.shape] if first else [])
    got = small_call(kernel, "col_mean", shapes, own, *got, facts)
    return got if first else got + [facts]


def joined(me, mate):
    piece, width = me.shape

    def kernel(me_ref, mate_ref, out):
        out[:piece] = me_ref[...]
        out[piece:] = mate_ref[...]

    return small_call(kernel, "joined", [(2 * piece, width)], me, mate)[0]


def finish(mat, size, parts, facts):
    width = facts.shape[1]
    half = size // 2

    def kernel(*refs):
        facts_ref, out_ref, made, sems = refs[-4:]
        takes = row(facts_ref[...], B_ME) > 0
        core, y = core_at(), ring_at()
        copies = []
        base = sum(GROUP * CHUNKS[c][mat] for c in range(parts[0][0]))
        for n, (c, *_) in enumerate(parts):
            count, piece = CHUNKS[c][mat], sum(CHUNKS[c])
            skip = CHUNKS[c][0] if mat else 0
            held, held_mate, *pieces = refs[6 * n : 6 * n + 6]
            for side, (whose, kept) in enumerate(((core, held), (1 - core, held_mate))):
                for d, src in enumerate(pieces):
                    j = (y + GROUP - d) % GROUP
                    old = kept[pl.ds(pl.multiple_of(j * piece + skip, 8), count), :]
                    here = pl.ds(pl.multiple_of(whose * half + base + j * count, 8), count)
                    made[here, :] = jnp.where(takes, src[side * piece + skip : side * piece + skip + count], old)
                    copy = pltpu.make_async_copy(made.at[here, :], out_ref.at[here, :], sems.at[len(copies)])
                    copy.start()
                    copies.append(copy)
            base += GROUP * count
        for copy in copies:
            copy.wait()

    operands = [x for _, held, held_mate, pieces in parts for x in (held, held_mate, *pieces)]
    return pl.pallas_call(
        kernel,
        in_specs=[STAYS] * (len(operands) + 1),
        out_specs=pl.BlockSpec(memory_space=pl.ANY),
        out_shape=jax.ShapeDtypeStruct((size, width), f32),
        scratch_shapes=[pltpu.VMEM((size, width), f32), pltpu.SemaphoreType.DMA((2 * GROUP * len(parts),))],
        compiler_params=pltpu.CompilerParams(vmem_limit_bytes=8 << 20),
        name="finish",
    )(*in_vmem(*operands, facts))


def ring(step):
    size = lax.axis_size("col")
    return [(i, i - i % GROUP + (i + step) % GROUP) for i in range(size)]


def swap(bit):
    return [(i, i ^ bit) for i in range(lax.axis_size("row"))]


def to_mate(x):
    return lax.ppermute(x, "row", swap(1))


def to_far(x):
    return lax.ppermute(x, "row", swap(2))


def around(xs):
    got = {d: lax.ppermute(xs[d - 1], "col", ring(d)) for d in DISTANCES}
    return [got[d] for d in (1, 2, 3)]


def tie(*xs):
    return lax.optimization_barrier(xs)


def per_device(features, values, out_grad, query_weight, key_weight, query_mean, query_square, key_mean, key_square, members):
    f, v, o, wq, wk = [a[0, 0] for a in (features, values, out_grad, query_weight, key_weight)]
    mq, sq, mk, sk = [a[0, 0] for a in (query_mean, query_square, key_mean, key_square)]
    size = wq.shape[0]

    mine0, other0, query_mine, query_other, facts, ds, queries, ft = query_step(members[0, 0], f, v, o, wq, wk, mq, sq)
    theirs0 = to_mate(other0)
    part0, facts = chip_sum(mine0, theirs0, facts, True)
    part0, ds = tie(part0, ds)
    far0 = to_far(part0)
    mine1, other1 = key_step(ds, queries, ft, query_mine, query_other, wk, mk, sk)
    theirs1 = to_mate(other1)
    part1, _ = chip_sum(mine1, theirs1, facts, False)
    far0, part1 = tie(far0, part1)
    far1 = to_far(part1)

    def total_of(own, got, facts, first):
        me, mate, facts = col_mean(own, got, facts, first)
        return joined(me, to_mate(mate)), facts

    def gather(total):
        return [total] + around([total] * 3)

    own0, *send0, held0, held_mate0, facts = row_mean(mine0, theirs0, far0, facts, True)
    total0, facts = total_of(own0, around(send0), facts, True)
    held_mate0 = to_mate(held_mate0)
    far1, _ = tie(far1, total0)
    all0 = gather(total0)
    own1, *send1, held1, held_mate1, _ = row_mean(mine1, theirs1, far1, facts, False)
    got1 = around(send1)
    own1, *all0 = tie(own1, *all0)
    total1, _ = total_of(own1, got1, facts, False)
    held_mate1 = to_mate(held_mate1)
    all1 = gather(total1)
    zero, one = (0, held0, held_mate0, all0), (1, held1, held_mate1, all1)
    if CHUNKS[1][0]:
        query = finish(0, size, [zero, one], facts)
    else:
        query = finish(0, size, [zero], facts)
        all1[1], query = tie(all1[1], query)
    key = finish(1, size, [one], facts)
    return query[None, None], key[None, None]


def solution(mesh):
    mats = P("row", "col", None, None)
    return jax.shard_map(
        per_device,
        mesh=mesh,
        in_specs=(mats,) * 9 + (P("row", "col", None),),
        out_specs=(mats, mats),
        check_vma=False,
    )
```

time: 732 us -> 116 us (0.16)
  blocking collectives: 562 us -> 0 us
  starting transfers between devices: 101 us -> 26.5 us
  waiting for transfers between devices: 12.1 us -> 60.2 us
  local copies, waits for them, and re-layouts: 18.5 us -> 0.65 us
  other arithmetic: 13.3 us -> 0 us
    all_gather x1 -> x0, blocking collectives: 562 us -> none  [member_facts(): grid = lax.all_gather(members, ('row', 'col'))]
    ppermute x22 -> x20, starting transfers between devices: 101 us -> 26.5 us  [the longest x12 15.9 us: around(): got = {d: lax.ppermute(xs[d - 1], 'col', ring(d)) for d in DISTANCES}]
    ppermute x22 -> x20, waiting for transfers between devices: 12.1 us -> 60.2 us  [the longest x12 31.5 us: around(): got = {d: lax.ppermute(xs[d - 1], 'col', ring(d)) for d in DISTANCES}]
    unnamed x29 -> x2, local copies, waits for them, and re-layouts: 12 us -> 0.65 us
    pallas_call x1 -> x12, Pallas kernels: 22.4 us -> 27.5 us  [the longest x1 18.2 us: query_step(): pl.pallas_call(query_kernel, grid=(heads // QUAD,), in_specs=[SCALARS, fu...]
  transfers between devices with their start and end apart: 22 -> 20, of which waited for: 7 -> 12; matrix products, arithmetic and copies ran while one was open for 2% -> 0% of each run, Pallas kernels for 0% -> 7%
where the time goes in v2:
time: 116 us
  waiting for transfers between devices  60.2 us (52%)
  Pallas kernels  27.5 us (24%)
  starting transfers between devices  26.5 us (23%)
    ppermute x12, waiting for transfers between devices, around(): got = {d: lax.ppermute(xs[d - 1], 'col', ring(d)) for d in DISTANCES}  31.5 us
    ppermute x2, waiting for transfers between devices, to_far(): return lax.ppermute(x, 'row', swap(2))  23.7 us
    pallas_call x1, Pallas kernels, query_step(): pl.pallas_call(query_kernel, grid=(heads // QUAD,), in_specs=[SCALARS, fu...  18.2 us
    ppermute x12, starting transfers between devices, around(): got = {d: lax.ppermute(xs[d - 1], 'col', ring(d)) for d in DISTANCES}  15.9 us
    ppermute x6, starting transfers between devices, to_mate(): return lax.ppermute(x, 'row', swap(1))  9.32 us
    pallas_call x1, Pallas kernels, key_step(): pl.pallas_call(key_kernel, grid=(heads // QUAD,), in_specs=[STAYS] * 5 +...  6.33 us
    ppermute x6, waiting for transfers between devices, to_mate(): return lax.ppermute(x, 'row', swap(1))  5.08 us
  transfers between devices with their start and end apart: 20, of which 12 were waited for; matrix products, arithmetic and copies ran while one was open for 0% of the time, Pallas kernels for 7%

profile of v2, /device:TPU:1, one launch (start us, length us, event | category | flops | bytes accessed | tf_op | source)
XLA Modules:
  0.0 115.8 jit_solution(5273584897166262641)
XLA Ops:
  1.3 18.2 %query_step.1 = (f32[256,512]{1,0:T(8,128)S(1)}, f32[264,512]{1,0:T(8,128)S(1)}, f32[8,512]{1,0:T(8,128)S(1)}, f32[8,512]{1,0:T(8,128)S(1)}, f32[8,512]{1,0:T(8,...) custom-call(s32[2]{0:T(128)S(1)} %bitcast.12, ...), custom_call_target="tpu_custom_call" | custom-call | tf_op jit(solution)/shard_map/query_step/pallas_call | solution.py:202
  19.5 3.3 %collective-permute-start = (f32[264,512]{1,0:T(8,128)S(1)}, f32[264,512]{1,0:T(8,128)S(1)}, u32[]{:S(2)}, u32[]{:S(2)}) collective-permute-start(f32[264,512]{1,0:T(8,128)S(1)} %get-tuple-element.45), channel_id=1, source_target_pairs={{0,32},{32,0},{64,96},{96,64},{128,160},{160,128},{192,224},{224,1... | collective-permute-start | bytes 1622024 | tf_op jit(solution)/shard_map/ppermute | solution.py:399
  22.8 1.6 %collective-permute-done.theirs_ref = f32[264,512]{1,0:T(8,128)S(1)} collective-permute-done((f32[264,512]{1,0:T(8,128)S(1)}, f32[264,512]{1,0:T(8,128)S(1)}, u32[]{:S(2)}, u32[]{:S(2)}) %collective-permute-start) | collective-permute-done | bytes 540704 | tf_op jit(solution)/shard_map/ppermute | solution.py:399
  24.5 1.3 %collective-permute-start.2 = (f32[264,512]{1,0:T(8,128)S(1)}, f32[264,512]{1,0:T(8,128)S(1)}, u32[]{:S(2)}, u32[]{:S(2)}) collective-permute-start(f32[264,512]{1,0:T(8,128)S(1)} %get-tuple-element.56), channel_id=1, source_target_pairs={{0,64},{32,96},{64,0},{96,32},{128,192},{160,224},{192,128},{224,1... | collective-permute-start | bytes 1622024 | tf_op jit(solution)/shard_map/ppermute | solution.py:403
  25.8 6.3 %key_step.1 = (f32[256,512]{1,0:T(8,128)S(1)}, f32[256,512]{1,0:T(8,128)S(1)}) custom-call(bf16[8,1024,512]{2,1,0:T(8,128)(2,1)S(1)} %get-tuple-element.49.ds_ref, bf16[1024,512]{1,0:T(8,128)(2,1)S(1)} %get-tuple-element.50.q_ref, bf16[512,1024]{1,0:T(8,128)(2,1)S(1)} %get-tuple-element.51.ft_ref, f32[8,512]{1,0:T(8,128)S(1)} %get-tuple-element.52.query_mine, ...), custom_call_target="tpu_custom_call" | custom-call | tf_op jit(solution)/shard_map/key_step/pallas_call | solution.py:226
  32.9 1.5 %collective-permute-done.1.theirs_ref = f32[256,512]{1,0:T(8,128)S(1)} collective-permute-done((f32[256,512]{1,0:T(8,128)S(1)}, f32[256,512]{1,0:T(8,128)S(1)}, u32[]{:S(2)}, u32[]{:S(2)}) %collective-permute-start.1) | collective-permute-done | bytes 524320 | tf_op jit(solution)/shard_map/ppermute | solution.py:399
  34.5 16.5 %collective-permute-done.2.far_ref = f32[264,512]{1,0:T(8,128)S(1)} collective-permute-done((f32[264,512]{1,0:T(8,128)S(1)}, f32[264,512]{1,0:T(8,128)S(1)}, u32[]{:S(2)}, u32[]{:S(2)}) %collective-permute-start.2) | collective-permute-done | bytes 540704 | tf_op jit(solution)/shard_map/ppermute | solution.py:403
  51.4 2.6 %collective-permute-start.5 = (f32[136,512]{1,0:T(8,128)S(1)}, f32[136,512]{1,0:T(8,128)S(1)}, u32[]{:S(2)}, u32[]{:S(2)}) collective-permute-start(f32[136,512]{1,0:T(8,128)S(1)} %get-tuple-element.62), channel_id=1, source_target_pairs={{0,2},{1,3},{2,0},{3,1},{4,6},{5,7},{6,4},{7,5},{8,10},{9,11},{10,... | collective-permute-start | bytes 835592 | tf_op jit(solution)/shard_map/ppermute | solution.py:407
  54.0 1.1 collective-permute-start.6
  55.1 5.2 %collective-permute-done.4.g1 = f32[136,512]{1,0:T(8,128)S(1)} collective-permute-done((f32[136,512]{1,0:T(8,128)S(1)}, f32[136,512]{1,0:T(8,128)S(1)}, u32[]{:S(2)}, u32[]{:S(2)}) %collective-permute-start.4) | collective-permute-done | bytes 278560 | tf_op jit(solution)/shard_map/ppermute | solution.py:407
  60.2 5.6 %collective-permute-done.5.g2 = f32[136,512]{1,0:T(8,128)S(1)} collective-permute-done((f32[136,512]{1,0:T(8,128)S(1)}, f32[136,512]{1,0:T(8,128)S(1)}, u32[]{:S(2)}, u32[]{:S(2)}) %collective-permute-start.5) | collective-permute-done | bytes 278560 | tf_op jit(solution)/shard_map/ppermute | solution.py:407
  66.7 1.6 %collective-permute-start.7 = (f32[64,512]{1,0:T(8,128)S(1)}, f32[64,512]{1,0:T(8,128)S(1)}, u32[]{:S(2)}, u32[]{:S(2)}) collective-permute-start(f32[64,512]{1,0:T(8,128)S(1)} %get-tuple-element.66), channel_id=1, source_target_pairs={{0,32},{32,0},{64,96},{96,64},{128,160},{160,128},{192,224},{224,1... | collective-permute-start | bytes 393224 | tf_op jit(solution)/shard_map/ppermute | solution.py:399
  69.4 2.4 %collective-permute-start.10 = (f32[128,512]{1,0:T(8,128)S(1)}, f32[128,512]{1,0:T(8,128)S(1)}, u32[]{:S(2)}, u32[]{:S(2)}) collective-permute-start(f32[128,512]{1,0:T(8,128)S(1)} %joined.2.refs_2_), channel_id=1, source_target_pairs={{0,3},{1,0},{2,1},{3,2},{4,7},{5,4},{6,5},{7,6},{8,11},{9,8},{10,9... | collective-permute-start | bytes 786440 | tf_op jit(solution)/shard_map/ppermute | solution.py:407
  72.5 7.2 %collective-permute-done.3.far_ref = f32[256,512]{1,0:T(8,128)S(1)} collective-permute-done((f32[256,512]{1,0:T(8,128)S(1)}, f32[256,512]{1,0:T(8,128)S(1)}, u32[]{:S(2)}, u32[]{:S(2)}) %collective-permute-start.3) | collective-permute-done | bytes 524320 | tf_op jit(solution)/shard_map/ppermute | solution.py:403
  80.4 1.9 %collective-permute-start.12 = (f32[128,512]{1,0:T(8,128)S(1)}, f32[128,512]{1,0:T(8,128)S(1)}, u32[]{:S(2)}, u32[]{:S(2)}) collective-permute-start(f32[128,512]{1,0:T(8,128)S(1)} %get-tuple-element.72), channel_id=1, source_target_pairs={{0,2},{1,3},{2,0},{3,1},{4,6},{5,7},{6,4},{7,5},{8,10},{9,11},{10,... | collective-permute-start | bytes 786440 | tf_op jit(solution)/shard_map/ppermute | solution.py:407
  82.4 3.8 %collective-permute-start.13 = (f32[128,512]{1,0:T(8,128)S(1)}, f32[128,512]{1,0:T(8,128)S(1)}, u32[]{:S(2)}, u32[]{:S(2)}) collective-permute-start(f32[128,512]{1,0:T(8,128)S(1)} %get-tuple-element.73), channel_id=1, source_target_pairs={{0,3},{1,0},{2,1},{3,2},{4,7},{5,4},{6,5},{7,6},{8,11},{9,8},{10,9... | collective-permute-start | bytes 786440 | tf_op jit(solution)/shard_map/ppermute | solution.py:407
  86.2 1.9 %collective-permute-start.16 = (f32[256,512]{1,0:T(8,128)S(1)}, f32[256,512]{1,0:T(8,128)S(1)}, u32[]{:S(2)}, u32[]{:S(2)}) collective-permute-start(f32[256,512]{1,0:T(8,128)S(1)} %get-tuple-element.77), channel_id=1, source_target_pairs={{0,32},{32,0},{64,96},{96,64},{128,160},{160,128},{192,224},{224,1... | collective-permute-start | bytes 1572872 | tf_op jit(solution)/shard_map/ppermute | solution.py:399
  88.2 5.6 %collective-permute-done.11.g1 = f32[128,512]{1,0:T(8,128)S(1)} collective-permute-done((f32[128,512]{1,0:T(8,128)S(1)}, f32[128,512]{1,0:T(8,128)S(1)}, u32[]{:S(2)}, u32[]{:S(2)}) %collective-permute-start.11) | collective-permute-done | bytes 262176 | tf_op jit(solution)/shard_map/ppermute | solution.py:407
  93.7 3.7 %collective-permute-done.12.g2 = f32[128,512]{1,0:T(8,128)S(1)} collective-permute-done((f32[128,512]{1,0:T(8,128)S(1)}, f32[128,512]{1,0:T(8,128)S(1)}, u32[]{:S(2)}, u32[]{:S(2)}) %collective-permute-start.12) | collective-permute-done | bytes 262176 | tf_op jit(solution)/shard_map/ppermute | solution.py:407
  97.5 1.6 %collective-permute-start.14 = (f32[64,512]{1,0:T(8,128)S(1)}, f32[64,512]{1,0:T(8,128)S(1)}, u32[]{:S(2)}, u32[]{:S(2)}) collective-permute-start(f32[64,512]{1,0:T(8,128)S(1)} %get-tuple-element.75), channel_id=1, source_target_pairs={{0,32},{32,0},{64,96},{96,64},{128,160},{160,128},{192,224},{224,1... | collective-permute-start | bytes 393224 | tf_op jit(solution)/shard_map/ppermute | solution.py:399
  100.2 2.7 %collective-permute-start.19 = (f32[128,512]{1,0:T(8,128)S(1)}, f32[128,512]{1,0:T(8,128)S(1)}, u32[]{:S(2)}, u32[]{:S(2)}) collective-permute-start(f32[128,512]{1,0:T(8,128)S(1)} %joined.3.refs_2_), channel_id=1, source_target_pairs={{0,3},{1,0},{2,1},{3,2},{4,7},{5,4},{6,5},{7,6},{8,11},{9,8},{10,9... | collective-permute-start | bytes 786440 | tf_op jit(solution)/shard_map/ppermute | solution.py:407
  102.8 1.1 finish.2
  103.9 10.6 %collective-permute-done.15.refs_3_ = f32[128,512]{1,0:T(8,128)S(1)} collective-permute-done((f32[128,512]{1,0:T(8,128)S(1)}, f32[128,512]{1,0:T(8,128)S(1)}, u32[]{:S(2)}, u32[]{:S(2)}) %collective-permute-start.15) | collective-permute-done | bytes 262176 | tf_op jit(solution)/shard_map/ppermute | solution.py:407
  114.5 1.1 finish.3
  (30 shorter events, 6.5 us)
Async XLA Ops:
  0.6 0.7 copy-start
  19.5 4.9 %collective-permute-start = (f32[264,512]{1,0:T(8,128)S(1)}, f32[264,512]{1,0:T(8,128)S(1)}, u32[]{:S(2)}, u32[]{:S(2)}) collective-permute-start(f32[264,512]{1,0:T(8,128)S(1)} %get-tuple-element.45), channel_id=1, source_target_pairs={{0,32},{32,0},{64,96},{96,64},{128,160},{160,128},{192,224},{224,1... | collective-permute-start | bytes 1622024 | tf_op jit(solution)/shard_map/ppermute | solution.py:399
  24.5 26.5 %collective-permute-start.2 = (f32[264,512]{1,0:T(8,128)S(1)}, f32[264,512]{1,0:T(8,128)S(1)}, u32[]{:S(2)}, u32[]{:S(2)}) collective-permute-start(f32[264,512]{1,0:T(8,128)S(1)} %get-tuple-element.56), channel_id=1, source_target_pairs={{0,64},{32,96},{64,0},{96,32},{128,192},{160,224},{192,128},{224,1... | collective-permute-start | bytes 1622024 | tf_op jit(solution)/shard_map/ppermute | solution.py:403
  32.1 2.3 %collective-permute-start.1 = (f32[256,512]{1,0:T(8,128)S(1)}, f32[256,512]{1,0:T(8,128)S(1)}, u32[]{:S(2)}, u32[]{:S(2)}) collective-permute-start(f32[256,512]{1,0:T(8,128)S(1)} %get-tuple-element.55), channel_id=1, source_target_pairs={{0,32},{32,0},{64,96},{96,64},{128,160},{160,128},{192,224},{224,1... | collective-permute-start | bytes 1572872 | tf_op jit(solution)/shard_map/ppermute | solution.py:399
  51.3 9.0 %collective-permute-start.4 = (f32[136,512]{1,0:T(8,128)S(1)}, f32[136,512]{1,0:T(8,128)S(1)}, u32[]{:S(2)}, u32[]{:S(2)}) collective-permute-start(f32[136,512]{1,0:T(8,128)S(1)} %get-tuple-element.61), channel_id=1, source_target_pairs={{0,1},{1,2},{2,3},{3,0},{4,5},{5,6},{6,7},{7,4},{8,9},{9,10},{10,1... | collective-permute-start | bytes 835592 | tf_op jit(solution)/shard_map/ppermute | solution.py:407
  51.4 14.4 %collective-permute-start.5 = (f32[136,512]{1,0:T(8,128)S(1)}, f32[136,512]{1,0:T(8,128)S(1)}, u32[]{:S(2)}, u32[]{:S(2)}) collective-permute-start(f32[136,512]{1,0:T(8,128)S(1)} %get-tuple-element.62), channel_id=1, source_target_pairs={{0,2},{1,3},{2,0},{3,1},{4,6},{5,7},{6,4},{7,5},{8,10},{9,11},{10,... | collective-permute-start | bytes 835592 | tf_op jit(solution)/shard_map/ppermute | solution.py:407
  54.0 12.7 %collective-permute-start.6 = (f32[136,512]{1,0:T(8,128)S(1)}, f32[136,512]{1,0:T(8,128)S(1)}, u32[]{:S(2)}, u32[]{:S(2)}) collective-permute-start(f32[136,512]{1,0:T(8,128)S(1)} %get-tuple-element.63), channel_id=1, source_target_pairs={{0,3},{1,0},{2,1},{3,2},{4,7},{5,4},{6,5},{7,6},{8,11},{9,8},{10,9... | collective-permute-start | bytes 835592 | tf_op jit(solution)/shard_map/ppermute | solution.py:407
  55.1 24.6 %collective-permute-start.3 = (f32[256,512]{1,0:T(8,128)S(1)}, f32[256,512]{1,0:T(8,128)S(1)}, u32[]{:S(2)}, u32[]{:S(2)}) collective-permute-start(f32[256,512]{1,0:T(8,128)S(1)} %chip_sum.3), channel_id=1, source_target_pairs={{0,64},{32,96},{64,0},{96,32},{128,192},{160,224},{192,128},{224,1... | collective-permute-start | bytes 1572872 | tf_op jit(solution)/shard_map/ppermute | solution.py:403
  66.7 2.6 %collective-permute-start.7 = (f32[64,512]{1,0:T(8,128)S(1)}, f32[64,512]{1,0:T(8,128)S(1)}, u32[]{:S(2)}, u32[]{:S(2)}) collective-permute-start(f32[64,512]{1,0:T(8,128)S(1)} %get-tuple-element.66), channel_id=1, source_target_pairs={{0,32},{32,0},{64,96},{96,64},{128,160},{160,128},{192,224},{224,1... | collective-permute-start | bytes 393224 | tf_op jit(solution)/shard_map/ppermute | solution.py:399
  69.4 13.0 %collective-permute-start.10 = (f32[128,512]{1,0:T(8,128)S(1)}, f32[128,512]{1,0:T(8,128)S(1)}, u32[]{:S(2)}, u32[]{:S(2)}) collective-permute-start(f32[128,512]{1,0:T(8,128)S(1)} %joined.2.refs_2_), channel_id=1, source_target_pairs={{0,3},{1,0},{2,1},{3,2},{4,7},{5,4},{6,5},{7,6},{8,11},{9,8},{10,9... | collective-permute-start | bytes 786440 | tf_op jit(solution)/shard_map/ppermute | solution.py:407
  71.8 14.4 %collective-permute-start.9 = (f32[128,512]{1,0:T(8,128)S(1)}, f32[128,512]{1,0:T(8,128)S(1)}, u32[]{:S(2)}, u32[]{:S(2)}) collective-permute-start(f32[128,512]{1,0:T(8,128)S(1)} %joined.2.refs_2_), channel_id=1, source_target_pairs={{0,2},{1,3},{2,0},{3,1},{4,6},{5,7},{6,4},{7,5},{8,10},{9,11},{10,... | collective-permute-start | bytes 786440 | tf_op jit(solution)/shard_map/ppermute | solution.py:407
  72.2 15.8 %collective-permute-start.8 = (f32[128,512]{1,0:T(8,128)S(1)}, f32[128,512]{1,0:T(8,128)S(1)}, u32[]{:S(2)}, u32[]{:S(2)}) collective-permute-start(f32[128,512]{1,0:T(8,128)S(1)} %joined.2.refs_2_), channel_id=1, source_target_pairs={{0,1},{1,2},{2,3},{3,0},{4,5},{5,6},{6,7},{7,4},{8,9},{9,10},{10,1... | collective-permute-start | bytes 786440 | tf_op jit(solution)/shard_map/ppermute | solution.py:407
  79.9 13.8 %collective-permute-start.11 = (f32[128,512]{1,0:T(8,128)S(1)}, f32[128,512]{1,0:T(8,128)S(1)}, u32[]{:S(2)}, u32[]{:S(2)}) collective-permute-start(f32[128,512]{1,0:T(8,128)S(1)} %get-tuple-element.71), channel_id=1, source_target_pairs={{0,1},{1,2},{2,3},{3,0},{4,5},{5,6},{6,7},{7,4},{8,9},{9,10},{10,1... | collective-permute-start | bytes 786440 | tf_op jit(solution)/shard_map/ppermute | solution.py:407
  80.4 17.0 %collective-permute-start.12 = (f32[128,512]{1,0:T(8,128)S(1)}, f32[128,512]{1,0:T(8,128)S(1)}, u32[]{:S(2)}, u32[]{:S(2)}) collective-permute-start(f32[128,512]{1,0:T(8,128)S(1)} %get-tuple-element.72), channel_id=1, source_target_pairs={{0,2},{1,3},{2,0},{3,1},{4,6},{5,7},{6,4},{7,5},{8,10},{9,11},{10,... | collective-permute-start | bytes 786440 | tf_op jit(solution)/shard_map/ppermute | solution.py:407
  82.4 15.1 %collective-permute-start.13 = (f32[128,512]{1,0:T(8,128)S(1)}, f32[128,512]{1,0:T(8,128)S(1)}, u32[]{:S(2)}, u32[]{:S(2)}) collective-permute-start(f32[128,512]{1,0:T(8,128)S(1)} %get-tuple-element.73), channel_id=1, source_target_pairs={{0,3},{1,0},{2,1},{3,2},{4,7},{5,4},{6,5},{7,6},{8,11},{9,8},{10,9... | collective-permute-start | bytes 786440 | tf_op jit(solution)/shard_map/ppermute | solution.py:407
  86.2 16.7 %collective-permute-start.16 = (f32[256,512]{1,0:T(8,128)S(1)}, f32[256,512]{1,0:T(8,128)S(1)}, u32[]{:S(2)}, u32[]{:S(2)}) collective-permute-start(f32[256,512]{1,0:T(8,128)S(1)} %get-tuple-element.77), channel_id=1, source_target_pairs={{0,32},{32,0},{64,96},{96,64},{128,160},{160,128},{192,224},{224,1... | collective-permute-start | bytes 1572872 | tf_op jit(solution)/shard_map/ppermute | solution.py:399
  88.1 26.4 %collective-permute-start.17 = (f32[256,512]{1,0:T(8,128)S(1)}, f32[256,512]{1,0:T(8,128)S(1)}, u32[]{:S(2)}, u32[]{:S(2)}) collective-permute-start(f32[256,512]{1,0:T(8,128)S(1)} %get-tuple-element.84), channel_id=1, source_target_pairs={{0,32},{32,0},{64,96},{96,64},{128,160},{160,128},{192,224},{224,1... | collective-permute-start | bytes 1572872 | tf_op jit(solution)/shard_map/ppermute | solution.py:399
  97.5 2.6 %collective-permute-start.14 = (f32[64,512]{1,0:T(8,128)S(1)}, f32[64,512]{1,0:T(8,128)S(1)}, u32[]{:S(2)}, u32[]{:S(2)}) collective-permute-start(f32[64,512]{1,0:T(8,128)S(1)} %get-tuple-element.75), channel_id=1, source_target_pairs={{0,32},{32,0},{64,96},{96,64},{128,160},{160,128},{192,224},{224,1... | collective-permute-start | bytes 393224 | tf_op jit(solution)/shard_map/ppermute | solution.py:399
  100.1 14.4 %collective-permute-start.15 = (f32[128,512]{1,0:T(8,128)S(1)}, f32[128,512]{1,0:T(8,128)S(1)}, u32[]{:S(2)}, u32[]{:S(2)}) collective-permute-start(f32[128,512]{1,0:T(8,128)S(1)} %joined.3.refs_2_), channel_id=1, source_target_pairs={{0,1},{1,2},{2,3},{3,0},{4,5},{5,6},{6,7},{7,4},{8,9},{9,10},{10,1... | collective-permute-start | bytes 786440 | tf_op jit(solution)/shard_map/ppermute | solution.py:407
  100.2 14.4 %collective-permute-start.19 = (f32[128,512]{1,0:T(8,128)S(1)}, f32[128,512]{1,0:T(8,128)S(1)}, u32[]{:S(2)}, u32[]{:S(2)}) collective-permute-start(f32[128,512]{1,0:T(8,128)S(1)} %joined.3.refs_2_), channel_id=1, source_target_pairs={{0,3},{1,0},{2,1},{3,2},{4,7},{5,4},{6,5},{7,6},{8,11},{9,8},{10,9... | collective-permute-start | bytes 786440 | tf_op jit(solution)/shard_map/ppermute | solution.py:407
  102.8 11.7 %collective-permute-start.18 = (f32[128,512]{1,0:T(8,128)S(1)}, f32[128,512]{1,0:T(8,128)S(1)}, u32[]{:S(2)}, u32[]{:S(2)}) collective-permute-start(f32[128,512]{1,0:T(8,128)S(1)} %joined.3.refs_2_), channel_id=1, source_target_pairs={{0,2},{1,3},{2,0},{3,1},{4,6},{5,7},{6,4},{7,5},{8,10},{9,11},{10,... | collective-permute-start | bytes 786440 | tf_op jit(solution)/shard_map/ppermute | solution.py:407

commit v3 on v2

v3 whole, which is shorter than its diff:
```python
import functools
import math

import jax
import jax.numpy as jnp
from jax import lax
from jax.experimental import pallas as pl
from jax.experimental.pallas import tpu as pltpu
from jax.sharding import PartitionSpec as P

HD = 64
SEQ = 512
QUAD = 256
PAIR = 128
GROUP = 4
NOTE = 8
bf16 = jnp.bfloat16
f32 = jnp.float32

beta_one = 0.9
beta_two = 0.999
epsilon = 1e-06
decay_rate = 0.01
learn_rate = 0.1
correction_one = 1.0 - math.exp(100.0 * math.log(0.9))
correction_two = 1.0 - math.exp(100.0 * math.log(0.999))


def dot(a, b, ca=1, cb=0):
    return lax.dot_general(a, b, (((ca,), (cb,)), ((), ())), preferred_element_type=f32)


def lamb_direction(w, m, s, g):
    first = beta_one * m + (1.0 - beta_one) * g
    second = beta_two * s + (1.0 - beta_two) * g * g
    return first / correction_one / (jnp.sqrt(second / correction_two) + epsilon) + decay_rate * w


def lamb_ratio(norms):
    w2 = jnp.full((1, 1), norms[0], f32)
    u2 = jnp.full((1, 1), norms[1], f32)
    return learn_rate * jnp.sqrt(w2) / jnp.sqrt(u2 + epsilon)


def only_head(pair, h):
    lane = lax.broadcasted_iota(jnp.int32, (1, PAIR), 1)
    return jnp.where((lane >= h * HD) & (lane < (h + 1) * HD), pair, jnp.zeros((), pair.dtype))


def core_at():
    return lax.axis_index("row") % 2


def ring_at():
    return lax.axis_index("col") % GROUP


def deal(fill, size, mine, other):
    half = size // 2
    for side, out in ((core_at(), mine), (1 - core_at(), other)):
        out[:half] = fill(pl.ds(pl.multiple_of(side * half, 8), half))


def query_kernel(
    members, f_ref, v_ref, o_ref, wq_ref, wk_ref, m_ref, s_ref,
    mine_ref, other_ref, facts_ref, ds_ref, q_ref, ft_ref, ks, kt, gqt, u_all, w_all, norms,
):
    step = pl.program_id(0)
    last = pl.num_programs(0) - 1
    tokens, width = f_ref.shape
    in_scale = 1.0 / math.sqrt(width)
    soft_scale = math.log2(math.e) / math.sqrt(HD)
    cols = pl.ds(pl.multiple_of(step * QUAD, QUAD), QUAD)

    @pl.when(step == 0)
    def _():
        ft_ref[...] = f_ref[...].T
        norms[0] = 0.0
        norms[1] = 0.0

    feats = f_ref[...]
    queries = (dot(feats, wq_ref[...].astype(bf16)) * in_scale).astype(bf16)
    q_ref[:, cols] = queries
    keys = (dot(feats, wk_ref[...].astype(bf16)) * in_scale).astype(bf16)
    ks[...] = keys
    kt[...] = keys.T
    units = [(s, head) for s in range(tokens // SEQ) for head in range(0, QUAD, HD)]

    def products(s, head):
        rows = slice(s * SEQ, (s + 1) * SEQ)
        lanes = slice(head // PAIR * PAIR, head // PAIR * PAIR + PAIR)
        h = head % PAIR // HD
        o_head = only_head(o_ref[rows, lanes], h) * (1.0 / math.sqrt(HD))
        scores = dot(ks[rows, lanes], only_head(queries[rows, lanes], h), 1, 1)
        return scores, dot(v_ref[rows, lanes], o_head.astype(bf16), 1, 1)

    ready = products(*units[0])
    for i, (s, head) in enumerate(units):
        rows = slice(s * SEQ, (s + 1) * SEQ)
        scores, grad_prob = ready
        if i + 1 < len(units):
            ready = products(*units[i + 1])
        top = jnp.max(scores, axis=0, keepdims=True)
        e = jnp.exp2((scores - top) * soft_scale)
        prob = e * (1.0 / jnp.sum(e, axis=0, keepdims=True))
        prob_low = prob.astype(bf16).astype(f32)
        delta = jnp.sum(prob_low * grad_prob, axis=0, keepdims=True)
        grad_score = (prob * (grad_prob - delta)).astype(bf16)
        ds_ref[step * (QUAD // HD) + head // HD, rows, :] = grad_score
        gqt[head : head + HD, rows] = dot(kt[head : head + HD, rows], grad_score).astype(bf16)
    grad = dot(ft_ref[...], gqt[...], 1, 1) * in_scale
    w = wq_ref[...]
    u = lamb_direction(w, m_ref[...], s_ref[...], grad)
    u_all[:, cols] = u
    w_all[:, cols] = w
    norms[0] += jnp.sum(w * w)
    norms[1] += jnp.sum(u * u)

    @pl.when(step == last)
    def _():
        ratio = lamb_ratio(norms)
        new = lambda here: w_all[here, :] - ratio * u_all[here, :]
        deal(new, width, mine_ref, other_ref)
        at = lax.broadcasted_iota(jnp.int32, facts_ref.shape, 0)
        facts = jnp.where(at == 0, members[0, 0, 0], jnp.where(at == 1, members[0, 0, 1], 0)).astype(f32)
        facts_ref[...] = facts
        other_ref[width // 2 :] = facts


def key_kernel(
    ds_ref, q_ref, ft_ref, w_ref, m_ref, s_ref,
    mine_ref, other_ref, gks, u_all, w_all, norms,
):
    step = pl.program_id(0)
    last = pl.num_programs(0) - 1
    tokens, width = q_ref.shape
    in_scale = 1.0 / math.sqrt(width)
    cols = pl.ds(pl.multiple_of(step * QUAD, QUAD), QUAD)

    @pl.when(step == 0)
    def _():
        norms[0] = 0.0
        norms[1] = 0.0

    for s in range(tokens // SEQ):
        rows = slice(s * SEQ, (s + 1) * SEQ)
        for p in range(QUAD // PAIR):
            lanes = pl.ds(pl.multiple_of(step * QUAD + p * PAIR, PAIR), PAIR)
            pair = q_ref[rows, lanes]
            grad = jnp.zeros((SEQ, PAIR), f32)
            for h in range(PAIR // HD):
                unit = step * (QUAD // HD) + p * (PAIR // HD) + h
                grad = grad + dot(ds_ref[unit, rows, :], only_head(pair, h))
            gks[rows, p * PAIR : (p + 1) * PAIR] = grad.astype(bf16)
    grad = dot(ft_ref[...], gks[...]) * in_scale
    w = w_ref[...]
    u = lamb_direction(w, m_ref[...], s_ref[...], grad)
    u_all[:, cols] = u
    w_all[:, cols] = w
    norms[0] += jnp.sum(w * w)
    norms[1] += jnp.sum(u * u)

    @pl.when(step == last)
    def _():
        ratio = lamb_ratio(norms)
        new = lambda here: w_all[here, :] - ratio * u_all[here, :]
        deal(new, width, mine_ref, other_ref)


SCALARS = pl.BlockSpec(memory_space=pltpu.SMEM)
STAYS = pl.BlockSpec(memory_space=pltpu.VMEM)


def in_hbm(*xs):
    return [pltpu.with_memory_space_constraint(x, pltpu.HBM) for x in xs]


def in_vmem(*xs):
    return [pltpu.with_memory_space_constraint(x, pltpu.VMEM) for x in xs]


def query_step(members, f, v, o, wq, wk, m, s):
    tokens, width = f.shape
    heads = wq.shape[1]
    tok = pl.BlockSpec((tokens, QUAD), lambda i: (0, i))
    mat = pl.BlockSpec((width, QUAD), lambda i: (0, i))
    full = pl.BlockSpec((tokens, width), lambda i: (0, 0))
    shapes = [(width // 2, heads), (width // 2 + NOTE, heads), (NOTE, heads)]
    return pl.pallas_call(
        query_kernel,
        grid=(heads // QUAD,),
        in_specs=[SCALARS, full, tok, tok, mat, mat, mat, mat],
        out_specs=[STAYS] * 6,
        out_shape=[pltpu.VMEM(x, f32) for x in shapes]
        + [pltpu.VMEM(x, bf16) for x in ((heads // HD, tokens, SEQ), (tokens, heads), (width, tokens))],
        scratch_shapes=[
            pltpu.VMEM((tokens, QUAD), bf16),
            pltpu.VMEM((QUAD, tokens), bf16),
            pltpu.VMEM((QUAD, tokens), bf16),
            pltpu.VMEM((width, heads), f32),
            pltpu.VMEM((width, heads), f32),
            pltpu.SMEM((2,), f32),
        ],
        compiler_params=pltpu.CompilerParams(vmem_limit_bytes=36 << 20),
        name="query_step",
    )(*in_hbm(members, f, v, o, wq, wk, m, s))


def key_step(ds, q, ft, w, m, s):
    tokens, heads = q.shape
    width = ft.shape[0]
    mat = pl.BlockSpec((width, QUAD), lambda i: (0, i))
    return pl.pallas_call(
        key_kernel,
        grid=(heads // QUAD,),
        in_specs=[STAYS] * 3 + [mat, mat, mat],
        out_specs=[STAYS] * 2,
        out_shape=[pltpu.VMEM((width // 2, heads), f32)] * 2,
        scratch_shapes=[
            pltpu.VMEM((tokens, QUAD), bf16),
            pltpu.VMEM((width, heads), f32),
            pltpu.VMEM((width, heads), f32),
            pltpu.SMEM((2,), f32),
        ],
        compiler_params=pltpu.CompilerParams(vmem_limit_bytes=24 << 20),
        name="key_step",
    )(*in_vmem(ds, q, ft), *in_hbm(w, m, s))


A_ME, B_ME, A_MATE, B_MATE, A_CHIP, A_COUNT, B_COUNT, B_COUNT_MATE = range(8)
DISTANCES = (2, 1, 3)
NO_HBM = pl.CostEstimate(flops=0, transcendentals=0, bytes_accessed=0)


def small_call(kernel, name, shapes, *operands):
    got = pl.pallas_call(
        kernel,
        in_specs=[STAYS] * len(operands),
        out_specs=[STAYS] * len(shapes),
        out_shape=[pltpu.VMEM(s, f32) for s in shapes],
        compiler_params=pltpu.CompilerParams(vmem_limit_bytes=8 << 20),
        cost_estimate=NO_HBM,
        name=name,
    )(*in_vmem(*operands))
    return list(got)


def row(facts, i):
    return facts[i : i + 1, :]


def chip_sum(mine, theirs, facts, first):
    rows, width = mine.shape

    def kernel(mine_ref, theirs_ref, facts_ref, out_ref, facts_out):
        f = facts_ref[...]
        if first:
            got = theirs_ref[rows:]
            at = lax.broadcasted_iota(jnp.int32, f.shape, 0)
            f = jnp.where(at == A_MATE, row(got, 0), jnp.where(at == B_MATE, row(got, 1), f))
            f = jnp.where(at == A_CHIP, row(f, A_ME) + row(f, A_MATE), f)
        out_ref[rows:] = f
        facts_out[...] = f
        out_ref[:rows] = row(f, A_ME) * mine_ref[...] + row(f, A_MATE) * theirs_ref[:rows]

    return small_call(kernel, "chip_sum", [(rows + NOTE, width), facts.shape], mine, theirs, facts)


def row_mean(mine, theirs, far, facts, first):
    rows, width = mine.shape
    piece = rows // GROUP

    def kernel(mine_ref, theirs_ref, far_ref, facts_ref, own, s2, s1, s3, held, held_mate, *maybe_facts):
        f = facts_ref[...]
        if first:
            at = lax.broadcasted_iota(jnp.int32, f.shape, 0)
            count = row(f, A_CHIP) + row(far_ref[rows:], A_CHIP)
            f = jnp.where(at == A_COUNT, jnp.maximum(count, 1.0), f)
            maybe_facts[0][...] = f
        y = ring_at()
        for d, out in enumerate((own, s1, s2, s3)):
            here = pl.ds(pl.multiple_of((y + d) % GROUP * piece, 8), piece)
            m, t = mine_ref[here, :], theirs_ref[here, :]
            mean = (row(f, A_ME) * m + row(f, A_MATE) * t + far_ref[here, :]) / row(f, A_COUNT)
            m = jnp.where(row(f, A_ME) > 0, mean, m)
            t = jnp.where(row(f, A_MATE) > 0, mean, t)
            held[here, :] = m
            held_mate[here, :] = t
            out[:piece] = m * row(f, B_ME)
            out[piece : 2 * piece] = t * row(f, B_MATE)
            if first and d:
                out[2 * piece :] = f

    sent = (2 * piece + (NOTE if first else 0), width)
    shapes = [(2 * piece, width), sent, sent, sent, (rows, width), (rows, width)]
    if first:
        shapes = shapes + [facts.shape]
    got = small_call(kernel, "row_mean", shapes, mine, theirs, far, facts)
    return got if first else got + [facts]


def col_mean(own, got, facts, first):
    rows, width = own.shape
    piece = rows // 2

    def kernel(own_ref, g1, g2, g3, facts_ref, me, mate):
        f = facts_ref[...]
        if first:
            at = lax.broadcasted_iota(jnp.int32, f.shape, 0)
            notes = [g[rows:] for g in (g1, g2, g3)]
            count = sum([row(n, B_ME) for n in notes], row(f, B_ME))
            count_mate = sum([row(n, B_MATE) for n in notes], row(f, B_MATE))
            f = jnp.where(at == B_COUNT, jnp.maximum(count, 1.0), f)
            f = jnp.where(at == B_COUNT_MATE, jnp.maximum(count_mate, 1.0), f)
            mate[...] = f
        total = own_ref[...] + g1[:rows] + g2[:rows] + g3[:rows]
        me[:piece] = total[:piece] / row(f, B_COUNT)
        mate_out = me.at[piece:] if first else mate
        mate_out[...] = total[piece:] / row(f, B_COUNT_MATE)

    shapes = [(rows, width), facts.shape] if first else [(piece, width), (piece, width)]
    return small_call(kernel, "col_mean", shapes, own, *got, facts)


def joined(me, mate):
    piece, width = me.shape

    def kernel(me_ref, mate_ref, out):
        out[:piece] = me_ref[...]
        out[piece:] = mate_ref[...]

    return small_call(kernel, "joined", [(2 * piece, width)], me, mate)[0]


def choose(held, held_mate, p0, p3, p1, p2, facts):
    rows, width = held.shape
    piece = rows // GROUP

    def kernel(held_ref, held_mate_ref, b0, b3, b1, b2, facts_ref, me, mate):
        f = facts_ref[...]
        for d, src in enumerate((b0, b1, b2, b3)):
            here = pl.ds(pl.multiple_of((ring_at() + GROUP - d) % GROUP * piece, 8), piece)
            me[here, :] = jnp.where(row(f, B_ME) > 0, src[:piece], held_ref[here, :])
            mate[here, :] = jnp.where(row(f, B_MATE) > 0, src[piece:], held_mate_ref[here, :])

    return small_call(kernel, "choose", [(rows, width)] * 2, held, held_mate, p0, p3, p1, p2, facts)


def place(mine, other):
    rows, width = mine.shape

    def kernel(mine_ref, other_ref, out_ref, sems):
        copies = []
        for i, (src, side) in enumerate(((mine_ref, core_at()), (other_ref, 1 - core_at()))):
            to = out_ref.at[pl.ds(pl.multiple_of(side * rows, 8), rows), :]
            copies.append(pltpu.make_async_copy(src, to, sems.at[i]))
            copies[-1].start()
        for copy in copies:
            copy.wait()

    return pl.pallas_call(
        kernel,
        in_specs=[STAYS] * 2,
        out_specs=pl.BlockSpec(memory_space=pl.ANY),
        out_shape=jax.ShapeDtypeStruct((2 * rows, width), f32),
        scratch_shapes=[pltpu.SemaphoreType.DMA((2,))],
        name="place",
    )(*in_vmem(mine, other))


def finish(held, held_mate, p0, p2, p3, p1, facts):
    rows, width = held.shape
    piece = rows // GROUP
    blocks = 2 * GROUP

    def kernel(held_ref, mate_ref, b0, b2, b3, b1, facts_ref, out_ref, made, sems):
        takes = row(facts_ref[...], B_ME) > 0
        core, y = core_at(), ring_at()
        copies = []
        for side, (whose, kept) in enumerate(((core, held_ref), (1 - core, mate_ref))):
            for d, src in enumerate((b0, b1, b2, b3)):
                at = pl.multiple_of((y + GROUP - d) % GROUP * piece, 8)
                block = side * GROUP + d
                made[block] = jnp.where(takes, src[side * piece : (side + 1) * piece], kept[pl.ds(at, piece), :])
                to = out_ref.at[pl.ds(pl.multiple_of(whose * rows + at, 8), piece), :]
                copies.append(pltpu.make_async_copy(made.at[block], to, sems.at[block]))
                copies[-1].start()
        for copy in copies:
            copy.wait()

    return pl.pallas_call(
        kernel,
        in_specs=[STAYS] * 7,
        out_specs=pl.BlockSpec(memory_space=pl.ANY),
        out_shape=jax.ShapeDtypeStruct((2 * rows, width), f32),
        scratch_shapes=[pltpu.VMEM((blocks, piece, width), f32), pltpu.SemaphoreType.DMA((blocks,))],
        compiler_params=pltpu.CompilerParams(vmem_limit_bytes=8 << 20),
        name="finish",
    )(*in_vmem(held, held_mate, p0, p2, p3, p1, facts))


def ring(step):
    size = lax.axis_size("col")
    return [(i, i - i % GROUP + (i + step) % GROUP) for i in range(size)]


def swap(bit):
    return [(i, i ^ bit) for i in range(lax.axis_size("row"))]


def to_mate(x):
    return lax.ppermute(x, "row", swap(1))


def to_far(x):
    return lax.ppermute(x, "row", swap(2))


def around(x2, x1, x3):
    return [lax.ppermute(x, "col", ring(d)) for d, x in zip(DISTANCES, (x2, x1, x3))]


def after(x, *done):
    return lax.optimization_barrier((x, *done))[0]


def per_device(features, values, out_grad, query_weight, key_weight, query_mean, query_square, key_mean, key_square, members):
    f, v, o, wq, wk = [a[0, 0] for a in (features, values, out_grad, query_weight, key_weight)]
    mq, sq, mk, sk = [a[0, 0] for a in (query_mean, query_square, key_mean, key_square)]

    mine0, other0, facts, ds, queries, ft = query_step(members, f, v, o, wq, wk, mq, sq)
    theirs0 = to_mate(other0)
    part0, facts = chip_sum(mine0, theirs0, facts, True)
    far0 = to_far(part0)
    mine1, other1 = key_step(after(ds, part0), queries, ft, wk, mk, sk)
    theirs1 = to_mate(other1)
    part1, _ = chip_sum(mine1, theirs1, facts, False)
    far1 = to_far(after(part1, far0))

    own0, s2, s1, s3, held0, held_mate0, facts = row_mean(mine0, theirs0, far0, facts, True)
    total0, facts = col_mean(own0, around(s2, s1, s3), facts, True)
    p2, p1, p3 = around(total0, total0, total0)
    query_mine, query_mate = choose(held0, held_mate0, total0, p3, p1, p2, facts)
    query_other = to_mate(query_mate)

    own1, s2, s1, s3, held1, held_mate1, _ = row_mean(mine1, theirs1, after(far1, total0), facts, False)
    got1 = around(s2, s1, s3)
    held_mate1 = to_mate(held_mate1)
    me, mate = col_mean(after(own1, query_mine), got1, facts, False)
    total1 = joined(me, to_mate(mate))
    p2, p1, p3 = around(total1, total1, total1)
    query = place(query_mine, query_other)
    key = finish(held1, held_mate1, total1, after(p2, query), p3, p1, facts)
    return query[None, None], key[None, None]


def solution(mesh):
    mats = P("row", "col", None, None)
    return jax.shard_map(
        per_device,
        mesh=mesh,
        in_specs=(mats,) * 9 + (P("row", "col", None),),
        out_specs=(mats, mats),
        check_vma=False,
    )
```

time: 116 us -> 111 us (0.957)
  starting transfers between devices: 26.5 us -> 23.2 us
  waiting for transfers between devices: 60.2 us -> 58.9 us
    ppermute x6 -> x5, starting transfers between devices: 9.32 us -> 6.29 us  [to_mate(): return lax.ppermute(x, 'row', swap(1))]
    ppermute x2, waiting for transfers between devices: 23.7 us -> 22.1 us  [to_far(): return lax.ppermute(x, 'row', swap(2))]
    pallas_call x8, Pallas kernels: 0.8 us -> 2.19 us  [small_call(): pl.pallas_call(kernel, in_specs=[STAYS] * len(operands), out_specs=[STAYS...]
    ppermute x12, waiting for transfers between devices: 31.5 us -> 32.8 us  [around(): lax.ppermute(x, 'col', ring(d))]
    ppermute x6 -> x5, waiting for transfers between devices: 5.08 us -> 4.09 us  [to_mate(): return lax.ppermute(x, 'row', swap(1))]
  transfers between devices with their start and end apart: 20 -> 19, of which waited for: 12 -> 12; matrix products, arithmetic and copies ran while one was open for 0% -> 0% of each run, Pallas kernels for 7% -> 9%
where the time goes in v3:
time: 111 us
  waiting for transfers between devices  58.9 us (53%)
  Pallas kernels  27.8 us (25%)
  starting transfers between devices  23.2 us (21%)
    ppermute x12, waiting for transfers between devices, around(): lax.ppermute(x, 'col', ring(d))  32.8 us
    ppermute x2, waiting for transfers between devices, to_far(): return lax.ppermute(x, 'row', swap(2))  22.1 us
    pallas_call x1, Pallas kernels, query_step(): pl.pallas_call(query_kernel, grid=(heads // QUAD,), in_specs=[SCALARS, fu...  17.2 us
    ppermute x12, starting transfers between devices, around(): lax.ppermute(x, 'col', ring(d))  15.6 us
    pallas_call x1, Pallas kernels, key_step(): pl.pallas_call(key_kernel, grid=(heads // QUAD,), in_specs=[STAYS] * 3 +...  6.33 us
    ppermute x5, starting transfers between devices, to_mate(): return lax.ppermute(x, 'row', swap(1))  6.29 us
    ppermute x5, waiting for transfers between devices, to_mate(): return lax.ppermute(x, 'row', swap(1))  4.09 us
  transfers between devices with their start and end apart: 19, of which 12 were waited for; matrix products, arithmetic and copies ran while one was open for 0% of the time, Pallas kernels for 9%

profile of v3, /device:TPU:1, one launch (start us, length us, event | category | flops | bytes accessed | tf_op | source)
XLA Modules:
  0.0 110.8 jit_solution(17348662883260240715)
XLA Ops:
  0.6 17.2 %query_step.1 = (f32[256,512]{1,0:T(8,128)S(1)}, f32[264,512]{1,0:T(8,128)S(1)}, f32[8,512]{1,0:T(8,128)S(1)}, bf16[8,1024,512]{2,1,0:T(8,128)(2,1)S(1)}, bf16[1...) custom-call(s32[1,1,2]{2,1,0:T(1,128)} %members.1, bf16[1024,512]{1,0:T(8,128)(2,1)} %bitcast.15, ...), custom_call_target="tpu_custom_call" | custom-call | tf_op jit(solution)/shard_map/query_step/pallas_call | solution.py:189
  17.8 3.3 %collective-permute-start = (f32[264,512]{1,0:T(8,128)S(1)}, f32[264,512]{1,0:T(8,128)S(1)}, u32[]{:S(2)}, u32[]{:S(2)}) collective-permute-start(f32[264,512]{1,0:T(8,128)S(1)} %get-tuple-element.38), channel_id=1, source_target_pairs={{0,32},{32,0},{64,96},{96,64},{128,160},{160,128},{192,224},{224,1... | collective-permute-start | bytes 1622024 | tf_op jit(solution)/shard_map/ppermute | solution.py:412
  21.2 1.6 %collective-permute-done.theirs_ref = f32[264,512]{1,0:T(8,128)S(1)} collective-permute-done((f32[264,512]{1,0:T(8,128)S(1)}, f32[264,512]{1,0:T(8,128)S(1)}, u32[]{:S(2)}, u32[]{:S(2)}) %collective-permute-start) | collective-permute-done | bytes 540704 | tf_op jit(solution)/shard_map/ppermute | solution.py:412
  22.8 1.3 %collective-permute-start.1 = (f32[264,512]{1,0:T(8,128)S(1)}, f32[264,512]{1,0:T(8,128)S(1)}, u32[]{:S(2)}, u32[]{:S(2)}) collective-permute-start(f32[264,512]{1,0:T(8,128)S(1)} %get-tuple-element.40), channel_id=1, source_target_pairs={{0,64},{32,96},{64,0},{96,32},{128,192},{160,224},{192,128},{224,1... | collective-permute-start | bytes 1622024 | tf_op jit(solution)/shard_map/ppermute | solution.py:416
  24.1 6.3 %key_step.1 = (f32[256,512]{1,0:T(8,128)S(1)}, f32[256,512]{1,0:T(8,128)S(1)}) custom-call(bf16[8,1024,512]{2,1,0:T(8,128)(2,1)S(1)} %get-tuple-element.54.ds_ref, bf16[1024,512]{1,0:T(8,128)(2,1)S(1)} %get-tuple-element.55.q_ref, bf16[512,1024]{1,0:T(8,128)(2,1)S(1)} %get-tuple-element.56.ft_ref, f32[512,512]{1,0:T(8,128)} %bitcast.12, ...), custom_call_target="tpu_custom_call" | custom-call | tf_op jit(solution)/shard_map/key_step/pallas_call | solution.py:213
  31.2 1.5 %collective-permute-done.9.theirs_ref = f32[256,512]{1,0:T(8,128)S(1)} collective-permute-done((f32[256,512]{1,0:T(8,128)S(1)}, f32[256,512]{1,0:T(8,128)S(1)}, u32[]{:S(2)}, u32[]{:S(2)}) %collective-permute-start.9) | collective-permute-done | bytes 524320 | tf_op jit(solution)/shard_map/ppermute | solution.py:412
  33.4 15.9 %collective-permute-done.1.far_ref = f32[264,512]{1,0:T(8,128)S(1)} collective-permute-done((f32[264,512]{1,0:T(8,128)S(1)}, f32[264,512]{1,0:T(8,128)S(1)}, u32[]{:S(2)}, u32[]{:S(2)}) %collective-permute-start.1) | collective-permute-done | bytes 540704 | tf_op jit(solution)/shard_map/ppermute | solution.py:416
  49.6 1.7 %collective-permute-start.2 = (f32[136,512]{1,0:T(8,128)S(1)}, f32[136,512]{1,0:T(8,128)S(1)}, u32[]{:S(2)}, u32[]{:S(2)}) collective-permute-start(f32[136,512]{1,0:T(8,128)S(1)} %get-tuple-element.45), channel_id=1, source_target_pairs={{0,2},{1,3},{2,0},{3,1},{4,6},{5,7},{6,4},{7,5},{8,10},{9,11},{10,... | collective-permute-start | bytes 835592 | tf_op jit(solution)/shard_map/ppermute | solution.py:420
  51.7 2.3 %collective-permute-start.4 = (f32[136,512]{1,0:T(8,128)S(1)}, f32[136,512]{1,0:T(8,128)S(1)}, u32[]{:S(2)}, u32[]{:S(2)}) collective-permute-start(f32[136,512]{1,0:T(8,128)S(1)} %get-tuple-element.47), channel_id=1, source_target_pairs={{0,3},{1,0},{2,1},{3,2},{4,7},{5,4},{6,5},{7,6},{8,11},{9,8},{10,9... | collective-permute-start | bytes 835592 | tf_op jit(solution)/shard_map/ppermute | solution.py:420
  54.0 4.7 %collective-permute-done.2.g1 = f32[136,512]{1,0:T(8,128)S(1)} collective-permute-done((f32[136,512]{1,0:T(8,128)S(1)}, f32[136,512]{1,0:T(8,128)S(1)}, u32[]{:S(2)}, u32[]{:S(2)}) %collective-permute-start.2) | collective-permute-done | bytes 278560 | tf_op jit(solution)/shard_map/ppermute | solution.py:420
  58.7 7.0 %collective-permute-done.3.g2 = f32[136,512]{1,0:T(8,128)S(1)} collective-permute-done((f32[136,512]{1,0:T(8,128)S(1)}, f32[136,512]{1,0:T(8,128)S(1)}, u32[]{:S(2)}, u32[]{:S(2)}) %collective-permute-start.3) | collective-permute-done | bytes 278560 | tf_op jit(solution)/shard_map/ppermute | solution.py:420
  65.8 1.4 %collective-permute-start.7 = (f32[128,512]{1,0:T(8,128)S(1)}, f32[128,512]{1,0:T(8,128)S(1)}, u32[]{:S(2)}, u32[]{:S(2)}) collective-permute-start(f32[128,512]{1,0:T(8,128)S(1)} %get-tuple-element.49.b0), channel_id=1, source_target_pairs={{0,2},{1,3},{2,0},{3,1},{4,6},{5,7},{6,4},{7,5},{8,10},{9,11},{10,... | collective-permute-start | bytes 786440 | tf_op jit(solution)/shard_map/ppermute | solution.py:420
  67.9 1.9 %collective-permute-start.5 = (f32[128,512]{1,0:T(8,128)S(1)}, f32[128,512]{1,0:T(8,128)S(1)}, u32[]{:S(2)}, u32[]{:S(2)}) collective-permute-start(f32[128,512]{1,0:T(8,128)S(1)} %get-tuple-element.49.b0), channel_id=1, source_target_pairs={{0,3},{1,0},{2,1},{3,2},{4,7},{5,4},{6,5},{7,6},{8,11},{9,8},{10,9... | collective-permute-start | bytes 786440 | tf_op jit(solution)/shard_map/ppermute | solution.py:420
  69.9 6.1 %collective-permute-done.10.far_ref = f32[264,512]{1,0:T(8,128)S(1)} collective-permute-done((f32[264,512]{1,0:T(8,128)S(1)}, f32[264,512]{1,0:T(8,128)S(1)}, u32[]{:S(2)}, u32[]{:S(2)}) %collective-permute-start.10) | collective-permute-done | bytes 540704 | tf_op jit(solution)/shard_map/ppermute | solution.py:416
  77.8 2.3 %collective-permute-start.14 = (f32[128,512]{1,0:T(8,128)S(1)}, f32[128,512]{1,0:T(8,128)S(1)}, u32[]{:S(2)}, u32[]{:S(2)}) collective-permute-start(f32[128,512]{1,0:T(8,128)S(1)} %get-tuple-element.68), channel_id=1, source_target_pairs={{0,3},{1,0},{2,1},{3,2},{4,7},{5,4},{6,5},{7,6},{8,11},{9,8},{10,9... | collective-permute-start | bytes 786440 | tf_op jit(solution)/shard_map/ppermute | solution.py:420
  80.0 1.2 %collective-permute-done.6.b1 = f32[128,512]{1,0:T(8,128)S(1)} collective-permute-done((f32[128,512]{1,0:T(8,128)S(1)}, f32[128,512]{1,0:T(8,128)S(1)}, u32[]{:S(2)}, u32[]{:S(2)}) %collective-permute-start.6) | collective-permute-done | bytes 262176 | tf_op jit(solution)/shard_map/ppermute | solution.py:420
  81.4 1.5 %collective-permute-start.8 = (f32[256,512]{1,0:T(8,128)S(1)}, f32[256,512]{1,0:T(8,128)S(1)}, u32[]{:S(2)}, u32[]{:S(2)}) collective-permute-start(f32[256,512]{1,0:T(8,128)S(1)} %get-tuple-element.52), channel_id=1, source_target_pairs={{0,32},{32,0},{64,96},{96,64},{128,160},{160,128},{192,224},{224,1... | collective-permute-start | bytes 1572872 | tf_op jit(solution)/shard_map/ppermute | solution.py:412
  83.0 3.3 %collective-permute-done.12.g1 = f32[128,512]{1,0:T(8,128)S(1)} collective-permute-done((f32[128,512]{1,0:T(8,128)S(1)}, f32[128,512]{1,0:T(8,128)S(1)}, u32[]{:S(2)}, u32[]{:S(2)}) %collective-permute-start.12) | collective-permute-done | bytes 262176 | tf_op jit(solution)/shard_map/ppermute | solution.py:420
  86.3 6.2 %collective-permute-done.13.g2 = f32[128,512]{1,0:T(8,128)S(1)} collective-permute-done((f32[128,512]{1,0:T(8,128)S(1)}, f32[128,512]{1,0:T(8,128)S(1)}, u32[]{:S(2)}, u32[]{:S(2)}) %collective-permute-start.13) | collective-permute-done | bytes 262176 | tf_op jit(solution)/shard_map/ppermute | solution.py:420
  94.1 1.4 %collective-permute-start.16 = (f32[128,512]{1,0:T(8,128)S(1)}, f32[128,512]{1,0:T(8,128)S(1)}, u32[]{:S(2)}, u32[]{:S(2)}) collective-permute-start(f32[128,512]{1,0:T(8,128)S(1)} %joined.1.b0), channel_id=1, source_target_pairs={{0,2},{1,3},{2,0},{3,1},{4,6},{5,7},{6,4},{7,5},{8,10},{9,11},{10,... | collective-permute-start | bytes 786440 | tf_op jit(solution)/shard_map/ppermute | solution.py:420
  96.3 1.9 %collective-permute-start.17 = (f32[128,512]{1,0:T(8,128)S(1)}, f32[128,512]{1,0:T(8,128)S(1)}, u32[]{:S(2)}, u32[]{:S(2)}) collective-permute-start(f32[128,512]{1,0:T(8,128)S(1)} %joined.1.b0), channel_id=1, source_target_pairs={{0,3},{1,0},{2,1},{3,2},{4,7},{5,4},{6,5},{7,6},{8,11},{9,8},{10,9... | collective-permute-start | bytes 786440 | tf_op jit(solution)/shard_map/ppermute | solution.py:420
  99.2 4.1 %collective-permute-done.16.b2 = f32[128,512]{1,0:T(8,128)S(1)} collective-permute-done((f32[128,512]{1,0:T(8,128)S(1)}, f32[128,512]{1,0:T(8,128)S(1)}, u32[]{:S(2)}, u32[]{:S(2)}) %collective-permute-start.16) | collective-permute-done | bytes 262176 | tf_op jit(solution)/shard_map/ppermute | solution.py:420
  103.3 6.3 %collective-permute-done.18.b1 = f32[128,512]{1,0:T(8,128)S(1)} collective-permute-done((f32[128,512]{1,0:T(8,128)S(1)}, f32[128,512]{1,0:T(8,128)S(1)}, u32[]{:S(2)}, u32[]{:S(2)}) %collective-permute-start.18) | collective-permute-done | bytes 262176 | tf_op jit(solution)/shard_map/ppermute | solution.py:420
  109.6 1.1 finish.1
  (26 shorter events, 8.4 us)
Async XLA Ops:
  17.8 4.9 %collective-permute-start = (f32[264,512]{1,0:T(8,128)S(1)}, f32[264,512]{1,0:T(8,128)S(1)}, u32[]{:S(2)}, u32[]{:S(2)}) collective-permute-start(f32[264,512]{1,0:T(8,128)S(1)} %get-tuple-element.38), channel_id=1, source_target_pairs={{0,32},{32,0},{64,96},{96,64},{128,160},{160,128},{192,224},{224,1... | collective-permute-start | bytes 1622024 | tf_op jit(solution)/shard_map/ppermute | solution.py:412
  22.8 26.5 %collective-permute-start.1 = (f32[264,512]{1,0:T(8,128)S(1)}, f32[264,512]{1,0:T(8,128)S(1)}, u32[]{:S(2)}, u32[]{:S(2)}) collective-permute-start(f32[264,512]{1,0:T(8,128)S(1)} %get-tuple-element.40), channel_id=1, source_target_pairs={{0,64},{32,96},{64,0},{96,32},{128,192},{160,224},{192,128},{224,1... | collective-permute-start | bytes 1622024 | tf_op jit(solution)/shard_map/ppermute | solution.py:416
  30.5 2.3 %collective-permute-start.9 = (f32[256,512]{1,0:T(8,128)S(1)}, f32[256,512]{1,0:T(8,128)S(1)}, u32[]{:S(2)}, u32[]{:S(2)}) collective-permute-start(f32[256,512]{1,0:T(8,128)S(1)} %get-tuple-element.58), channel_id=1, source_target_pairs={{0,32},{32,0},{64,96},{96,64},{128,160},{160,128},{192,224},{224,1... | collective-permute-start | bytes 1572872 | tf_op jit(solution)/shard_map/ppermute | solution.py:412
  49.3 26.6 %collective-permute-start.10 = (f32[264,512]{1,0:T(8,128)S(1)}, f32[264,512]{1,0:T(8,128)S(1)}, u32[]{:S(2)}, u32[]{:S(2)}) collective-permute-start(f32[264,512]{1,0:T(8,128)S(1)} %get-tuple-element.60), channel_id=1, source_target_pairs={{0,64},{32,96},{64,0},{96,32},{128,192},{160,224},{192,128},{224,1... | collective-permute-start | bytes 1622024 | tf_op jit(solution)/shard_map/ppermute | solution.py:416
  49.6 9.1 %collective-permute-start.2 = (f32[136,512]{1,0:T(8,128)S(1)}, f32[136,512]{1,0:T(8,128)S(1)}, u32[]{:S(2)}, u32[]{:S(2)}) collective-permute-start(f32[136,512]{1,0:T(8,128)S(1)} %get-tuple-element.45), channel_id=1, source_target_pairs={{0,2},{1,3},{2,0},{3,1},{4,6},{5,7},{6,4},{7,5},{8,10},{9,11},{10,... | collective-permute-start | bytes 835592 | tf_op jit(solution)/shard_map/ppermute | solution.py:420
  51.3 14.4 %collective-permute-start.3 = (f32[136,512]{1,0:T(8,128)S(1)}, f32[136,512]{1,0:T(8,128)S(1)}, u32[]{:S(2)}, u32[]{:S(2)}) collective-permute-start(f32[136,512]{1,0:T(8,128)S(1)} %get-tuple-element.46), channel_id=1, source_target_pairs={{0,1},{1,2},{2,3},{3,0},{4,5},{5,6},{6,7},{7,4},{8,9},{9,10},{10,1... | collective-permute-start | bytes 835592 | tf_op jit(solution)/shard_map/ppermute | solution.py:420
  51.7 14.0 %collective-permute-start.4 = (f32[136,512]{1,0:T(8,128)S(1)}, f32[136,512]{1,0:T(8,128)S(1)}, u32[]{:S(2)}, u32[]{:S(2)}) collective-permute-start(f32[136,512]{1,0:T(8,128)S(1)} %get-tuple-element.47), channel_id=1, source_target_pairs={{0,3},{1,0},{2,1},{3,2},{4,7},{5,4},{6,5},{7,6},{8,11},{9,8},{10,9... | collective-permute-start | bytes 835592 | tf_op jit(solution)/shard_map/ppermute | solution.py:420
  65.8 12.0 %collective-permute-start.7 = (f32[128,512]{1,0:T(8,128)S(1)}, f32[128,512]{1,0:T(8,128)S(1)}, u32[]{:S(2)}, u32[]{:S(2)}) collective-permute-start(f32[128,512]{1,0:T(8,128)S(1)} %get-tuple-element.49.b0), channel_id=1, source_target_pairs={{0,2},{1,3},{2,0},{3,1},{4,6},{5,7},{6,4},{7,5},{8,10},{9,11},{10,... | collective-permute-start | bytes 786440 | tf_op jit(solution)/shard_map/ppermute | solution.py:420
  67.2 14.1 %collective-permute-start.6 = (f32[128,512]{1,0:T(8,128)S(1)}, f32[128,512]{1,0:T(8,128)S(1)}, u32[]{:S(2)}, u32[]{:S(2)}) collective-permute-start(f32[128,512]{1,0:T(8,128)S(1)} %get-tuple-element.49.b0), channel_id=1, source_target_pairs={{0,1},{1,2},{2,3},{3,0},{4,5},{5,6},{6,7},{7,4},{8,9},{9,10},{10,1... | collective-permute-start | bytes 786440 | tf_op jit(solution)/shard_map/ppermute | solution.py:420
  67.9 13.3 %collective-permute-start.5 = (f32[128,512]{1,0:T(8,128)S(1)}, f32[128,512]{1,0:T(8,128)S(1)}, u32[]{:S(2)}, u32[]{:S(2)}) collective-permute-start(f32[128,512]{1,0:T(8,128)S(1)} %get-tuple-element.49.b0), channel_id=1, source_target_pairs={{0,3},{1,0},{2,1},{3,2},{4,7},{5,4},{6,5},{7,6},{8,11},{9,8},{10,9... | collective-permute-start | bytes 786440 | tf_op jit(solution)/shard_map/ppermute | solution.py:420
  77.0 9.3 %collective-permute-start.12 = (f32[128,512]{1,0:T(8,128)S(1)}, f32[128,512]{1,0:T(8,128)S(1)}, u32[]{:S(2)}, u32[]{:S(2)}) collective-permute-start(f32[128,512]{1,0:T(8,128)S(1)} %get-tuple-element.66), channel_id=1, source_target_pairs={{0,2},{1,3},{2,0},{3,1},{4,6},{5,7},{6,4},{7,5},{8,10},{9,11},{10,... | collective-permute-start | bytes 786440 | tf_op jit(solution)/shard_map/ppermute | solution.py:420
  77.4 15.1 %collective-permute-start.13 = (f32[128,512]{1,0:T(8,128)S(1)}, f32[128,512]{1,0:T(8,128)S(1)}, u32[]{:S(2)}, u32[]{:S(2)}) collective-permute-start(f32[128,512]{1,0:T(8,128)S(1)} %get-tuple-element.67), channel_id=1, source_target_pairs={{0,1},{1,2},{2,3},{3,0},{4,5},{5,6},{6,7},{7,4},{8,9},{9,10},{10,1... | collective-permute-start | bytes 786440 | tf_op jit(solution)/shard_map/ppermute | solution.py:420
  77.8 14.7 %collective-permute-start.14 = (f32[128,512]{1,0:T(8,128)S(1)}, f32[128,512]{1,0:T(8,128)S(1)}, u32[]{:S(2)}, u32[]{:S(2)}) collective-permute-start(f32[128,512]{1,0:T(8,128)S(1)} %get-tuple-element.68), channel_id=1, source_target_pairs={{0,3},{1,0},{2,1},{3,2},{4,7},{5,4},{6,5},{7,6},{8,11},{9,8},{10,9... | collective-permute-start | bytes 786440 | tf_op jit(solution)/shard_map/ppermute | solution.py:420
  81.4 16.8 %collective-permute-start.8 = (f32[256,512]{1,0:T(8,128)S(1)}, f32[256,512]{1,0:T(8,128)S(1)}, u32[]{:S(2)}, u32[]{:S(2)}) collective-permute-start(f32[256,512]{1,0:T(8,128)S(1)} %get-tuple-element.52), channel_id=1, source_target_pairs={{0,32},{32,0},{64,96},{96,64},{128,160},{160,128},{192,224},{224,1... | collective-permute-start | bytes 1572872 | tf_op jit(solution)/shard_map/ppermute | solution.py:412
  82.9 20.4 %collective-permute-start.11 = (f32[256,512]{1,0:T(8,128)}, f32[256,512]{1,0:T(8,128)S(1)}, u32[]{:S(2)}, u32[]{:S(2)}) collective-permute-start(f32[256,512]{1,0:T(8,128)} %get-tuple-element.63), channel_id=1, source_target_pairs={{0,32},{32,0},{64,96},{96,64},{128,160},{160,128},{192,224},{224,1... | collective-permute-start | bytes 1572872 | tf_op jit(solution)/shard_map/ppermute | solution.py:412
  92.5 1.6 %collective-permute-start.15 = (f32[64,512]{1,0:T(8,128)S(1)}, f32[64,512]{1,0:T(8,128)S(1)}, u32[]{:S(2)}, u32[]{:S(2)}) collective-permute-start(f32[64,512]{1,0:T(8,128)S(1)} %get-tuple-element.70), channel_id=1, source_target_pairs={{0,32},{32,0},{64,96},{96,64},{128,160},{160,128},{192,224},{224,1... | collective-permute-start | bytes 393224 | tf_op jit(solution)/shard_map/ppermute | solution.py:412
  94.1 9.2 %collective-permute-start.16 = (f32[128,512]{1,0:T(8,128)S(1)}, f32[128,512]{1,0:T(8,128)S(1)}, u32[]{:S(2)}, u32[]{:S(2)}) collective-permute-start(f32[128,512]{1,0:T(8,128)S(1)} %joined.1.b0), channel_id=1, source_target_pairs={{0,2},{1,3},{2,0},{3,1},{4,6},{5,7},{6,4},{7,5},{8,10},{9,11},{10,... | collective-permute-start | bytes 786440 | tf_op jit(solution)/shard_map/ppermute | solution.py:420
  95.5 14.1 %collective-permute-start.18 = (f32[128,512]{1,0:T(8,128)S(1)}, f32[128,512]{1,0:T(8,128)S(1)}, u32[]{:S(2)}, u32[]{:S(2)}) collective-permute-start(f32[128,512]{1,0:T(8,128)S(1)} %joined.1.b0), channel_id=1, source_target_pairs={{0,1},{1,2},{2,3},{3,0},{4,5},{5,6},{6,7},{7,4},{8,9},{9,10},{10,1... | collective-permute-start | bytes 786440 | tf_op jit(solution)/shard_map/ppermute | solution.py:420
  96.3 13.3 %collective-permute-start.17 = (f32[128,512]{1,0:T(8,128)S(1)}, f32[128,512]{1,0:T(8,128)S(1)}, u32[]{:S(2)}, u32[]{:S(2)}) collective-permute-start(f32[128,512]{1,0:T(8,128)S(1)} %joined.1.b0), channel_id=1, source_target_pairs={{0,3},{1,0},{2,1},{3,2},{4,7},{5,4},{6,5},{7,6},{8,11},{9,8},{10,9... | collective-permute-start | bytes 786440 | tf_op jit(solution)/shard_map/ppermute | solution.py:420

commit v4 on v3

--- a/solution.py
+++ b/solution.py
@@ -14,6 +14,7 @@
 PAIR = 128
 GROUP = 4
 NOTE = 8
+FIRST, TURN, LAST = 160, 96, 192
 bf16 = jnp.bfloat16
 f32 = jnp.float32
 
@@ -55,15 +56,17 @@
     return lax.axis_index("col") % GROUP
 
 
-def deal(fill, size, mine, other):
-    half = size // 2
-    for side, out in ((core_at(), mine), (1 - core_at(), other)):
-        out[:half] = fill(pl.ds(pl.multiple_of(side * half, 8), half))
+def deal(fill, size, mines, others):
+    for side, outs in ((core_at(), mines), (1 - core_at(), others)):
+        at = side * (size // 2)
+        for out, count in outs:
+            out[:count] = fill(pl.ds(pl.multiple_of(at, 8), count))
+            at = at + count
 
 
 def query_kernel(
     members, f_ref, v_ref, o_ref, wq_ref, wk_ref, m_ref, s_ref,
-    mine_ref, other_ref, facts_ref, ds_ref, q_ref, ft_ref, ks, kt, gqt, u_all, w_all, norms,
+    mine_ref, turn_ref, other_ref, facts_ref, ds_ref, q_ref, ft_ref, ks, kt, gqt, u_all, w_all, norms,
 ):
     step = pl.program_id(0)
     last = pl.num_programs(0) - 1
@@ -120,7 +123,7 @@
     def _():
         ratio = lamb_ratio(norms)
         new = lambda here: w_all[here, :] - ratio * u_all[here, :]
-        deal(new, width, mine_ref, other_ref)
+        deal(new, width, ((mine_ref, FIRST), (turn_ref, TURN)), ((other_ref, width // 2),))
         at = lax.broadcasted_iota(jnp.int32, facts_ref.shape, 0)
         facts = jnp.where(at == 0, members[0, 0, 0], jnp.where(at == 1, members[0, 0, 1], 0)).astype(f32)
         facts_ref[...] = facts
@@ -128,8 +131,8 @@
 
 
 def key_kernel(
-    ds_ref, q_ref, ft_ref, w_ref, m_ref, s_ref,
-    mine_ref, other_ref, gks, u_all, w_all, norms,
+    ds_ref, q_ref, ft_ref, turn_ref, w_ref, m_ref, s_ref,
+    turned_ref, mine_ref, turned_other, other_ref, gks, u_all, w_all, norms,
 ):
     step = pl.program_id(0)
     last = pl.num_programs(0) - 1
@@ -164,7 +167,10 @@
     def _():
         ratio = lamb_ratio(norms)
         new = lambda here: w_all[here, :] - ratio * u_all[here, :]
-        deal(new, width, mine_ref, other_ref)
+        turned_ref[:TURN] = turn_ref[...]
+        keys = width // 2 - LAST
+        mines = ((turned_ref.at[TURN:], keys), (mine_ref, LAST))
+        deal(new, width, mines, ((turned_other, keys), (other_ref, LAST)))
 
 
 SCALARS = pl.BlockSpec(memory_space=pltpu.SMEM)
@@ -185,12 +191,12 @@
     tok = pl.BlockSpec((tokens, QUAD), lambda i: (0, i))
     mat = pl.BlockSpec((width, QUAD), lambda i: (0, i))
     full = pl.BlockSpec((tokens, width), lambda i: (0, 0))
-    shapes = [(width // 2, heads), (width // 2 + NOTE, heads), (NOTE, heads)]
+    shapes = [(FIRST, heads), (TURN, heads), (width // 2 + NOTE, heads), (NOTE, heads)]
     return pl.pallas_call(
         query_kernel,
         grid=(heads // QUAD,),
         in_specs=[SCALARS, full, tok, tok, mat, mat, mat, mat],
-        out_specs=[STAYS] * 6,
+        out_specs=[STAYS] * 7,
         out_shape=[pltpu.VMEM(x, f32) for x in shapes]
         + [pltpu.VMEM(x, bf16) for x in ((heads // HD, tokens, SEQ), (tokens, heads), (width, tokens))],
         scratch_shapes=[
@@ -206,16 +212,17 @@
     )(*in_hbm(members, f, v, o, wq, wk, m, s))
 
 
-def key_step(ds, q, ft, w, m, s):
+def key_step(ds, q, ft, turn, w, m, s):
     tokens, heads = q.shape
     width = ft.shape[0]
+    keys = width // 2 - LAST
     mat = pl.BlockSpec((width, QUAD), lambda i: (0, i))
     return pl.pallas_call(
         key_kernel,
         grid=(heads // QUAD,),
-        in_specs=[STAYS] * 3 + [mat, mat, mat],
-        out_specs=[STAYS] * 2,
-        out_shape=[pltpu.VMEM((width // 2, heads), f32)] * 2,
+        in_specs=[STAYS] * 4 + [mat, mat, mat],
+        out_specs=[STAYS] * 4,
+        out_shape=[pltpu.VMEM((r, heads), f32) for r in (TURN + keys, LAST, keys, LAST)],
         scratch_shapes=[
             pltpu.VMEM((tokens, QUAD), bf16),
             pltpu.VMEM((width, heads), f32),
@@ -224,7 +231,7 @@
         ],
         compiler_params=pltpu.CompilerParams(vmem_limit_bytes=24 << 20),
         name="key_step",
-    )(*in_vmem(ds, q, ft), *in_hbm(w, m, s))
+    )(*in_vmem(ds, q, ft, turn), *in_hbm(w, m, s))
 
 
 A_ME, B_ME, A_MATE, B_MATE, A_CHIP, A_COUNT, B_COUNT, B_COUNT_MATE = range(8)
@@ -249,21 +256,46 @@
     return facts[i : i + 1, :]
 
 
-def chip_sum(mine, theirs, facts, first):
+def chip_sum(mine, theirs, facts):
     rows, width = mine.shape
 
     def kernel(mine_ref, theirs_ref, facts_ref, out_ref, facts_out):
         f = facts_ref[...]
-        if first:
-            got = theirs_ref[rows:]
-            at = lax.broadcasted_iota(jnp.int32, f.shape, 0)
-            f = jnp.where(at == A_MATE, row(got, 0), jnp.where(at == B_MATE, row(got, 1), f))
-            f = jnp.where(at == A_CHIP, row(f, A_ME) + row(f, A_MATE), f)
+        got = theirs_ref[theirs_ref.shape[0] - NOTE :]
+        at = lax.broadcasted_iota(jnp.int32, f.shape, 0)
+        f = jnp.where(at == A_MATE, row(got, 0), jnp.where(at == B_MATE, row(got, 1), f))
+        f = jnp.where(at == A_CHIP, row(f, A_ME) + row(f, A_MATE), f)
         out_ref[rows:] = f
         facts_out[...] = f
         out_ref[:rows] = row(f, A_ME) * mine_ref[...] + row(f, A_MATE) * theirs_ref[:rows]
 
     return small_call(kernel, "chip_sum", [(rows + NOTE, width), facts.shape], mine, theirs, facts)
+
+
+def chip_sum_turned(turned, theirs_query, theirs_key, facts):
+    rows, width = turned.shape
+
+    def kernel(turned_ref, tq_ref, tk_ref, facts_ref, out_ref, theirs_out):
+        f = facts_ref[...]
+        theirs_out[:TURN] = tq_ref[FIRST : FIRST + TURN]
+        theirs_out[TURN:] = tk_ref[...]
+        out_ref[:rows] = row(f, A_ME) * turned_ref[...] + row(f, A_MATE) * theirs_out[...]
+        out_ref[rows : rows + NOTE] = f
+        out_ref[rows + NOTE :] = f
+
+    shapes = [(rows + 2 * NOTE, width), (rows, width)]
+    return small_call(kernel, "chip_sum_turned", shapes, turned, theirs_query, theirs_key, facts)
+
+
+def chip_sum_last(mine, theirs, facts):
+    rows, width = mine.shape
+
+    def kernel(mine_ref, theirs_ref, facts_ref, out_ref):
+        f = facts_ref[...]
+        out_ref[:rows] = row(f, A_ME) * mine_ref[...] + row(f, A_MATE) * theirs_ref[...]
+        out_ref[rows:] = f
+
+    return small_call(kernel, "chip_sum_last", [(rows + NOTE, width)], mine, theirs, facts)[0]
 
 
 def row_mean(mine, theirs, far, facts, first):
@@ -274,7 +306,7 @@
         f = facts_ref[...]
         if first:
             at = lax.broadcasted_iota(jnp.int32, f.shape, 0)
-            count = row(f, A_CHIP) + row(far_ref[rows:], A_CHIP)
+            count = row(f, A_CHIP) + row(far_ref[rows : rows + NOTE], A_CHIP)
             f = jnp.where(at == A_COUNT, jnp.maximum(count, 1.0), f)
             maybe_facts[0][...] = f
         y = ring_at()
@@ -299,11 +331,11 @@
     return got if first else got + [facts]
 
 
-def col_mean(own, got, facts, first):
+def col_mean(own, got, facts, first=False, split=False):
     rows, width = own.shape
     piece = rows // 2
 
-    def kernel(own_ref, g1, g2, g3, facts_ref, me, mate):
+    def kernel(own_ref, g1, g2, g3, facts_ref, *outs):
         f = facts_ref[...]
         if first:
             at = lax.broadcasted_iota(jnp.int32, f.shape, 0)
@@ -312,14 +344,14 @@
             count_mate = sum([row(n, B_MATE) for n in notes], row(f, B_MATE))
             f = jnp.where(at == B_COUNT, jnp.maximum(count, 1.0), f)
             f = jnp.where(at == B_COUNT_MATE, jnp.maximum(count_mate, 1.0), f)
-            mate[...] = f
+            outs[1][...] = f
         total = own_ref[...] + g1[:rows] + g2[:rows] + g3[:rows]
-        me[:piece] = total[:piece] / row(f, B_COUNT)
-        mate_out = me.at[piece:] if first else mate
-        mate_out[...] = total[piece:] / row(f, B_COUNT_MATE)
-
-    shapes = [(rows, width), facts.shape] if first else [(piece, width), (piece, width)]
-    return small_call(kernel, "col_mean", shapes, own, *got, facts)
+        mate = outs[1] if split else outs[0].at[piece:]
+        outs[0][:piece] = total[:piece] / row(f, B_COUNT)
+        mate[...] = total[piece:] / row(f, B_COUNT_MATE)
+
+    shapes = [(piece, width)] * 2 if split else [(rows, width)]
+    return small_call(kernel, "col_mean", shapes + ([facts.shape] if first else []), own, *got, facts)
 
 
 def joined(me, mate):
@@ -346,57 +378,64 @@
     return small_call(kernel, "choose", [(rows, width)] * 2, held, held_mate, p0, p3, p1, p2, facts)
 
 
-def place(mine, other):
-    rows, width = mine.shape
-
-    def kernel(mine_ref, other_ref, out_ref, sems):
+def place(size, mine, other, turned, turned_other):
+    width = mine.shape[1]
+
+    def kernel(mine_ref, other_ref, turned_ref, turned_other_ref, out_ref, sems):
         copies = []
-        for i, (src, side) in enumerate(((mine_ref, core_at()), (other_ref, 1 - core_at()))):
-            to = out_ref.at[pl.ds(pl.multiple_of(side * rows, 8), rows), :]
-            copies.append(pltpu.make_async_copy(src, to, sems.at[i]))
-            copies[-1].start()
+        for a, b, side in ((mine_ref, turned_ref, core_at()), (other_ref, turned_other_ref, 1 - core_at())):
+            for src, skip, count in ((a, 0, FIRST), (b, FIRST, TURN)):
+                to = out_ref.at[pl.ds(pl.multiple_of(side * (size // 2) + skip, 8), count), :]
+                copies.append(pltpu.make_async_copy(src.at[:count], to, sems.at[len(copies)]))
+                copies[-1].start()
         for copy in copies:
             copy.wait()
 
     return pl.pallas_call(
         kernel,
-        in_specs=[STAYS] * 2,
+        in_specs=[STAYS] * 4,
         out_specs=pl.BlockSpec(memory_space=pl.ANY),
-        out_shape=jax.ShapeDtypeStruct((2 * rows, width), f32),
-        scratch_shapes=[pltpu.SemaphoreType.DMA((2,))],
+        out_shape=jax.ShapeDtypeStruct((size, width), f32),
+        scratch_shapes=[pltpu.SemaphoreType.DMA((4,))],
         name="place",
-    )(*in_vmem(mine, other))
-
-
-def finish(held, held_mate, p0, p2, p3, p1, facts):
+    )(*in_vmem(mine, other, turned, turned_other))
+
+
+def finish(size, turned, turned_other, held, held_mate, p0, p2, p3, p1, facts):
     rows, width = held.shape
     piece = rows // GROUP
     blocks = 2 * GROUP
-
-    def kernel(held_ref, mate_ref, b0, b2, b3, b1, facts_ref, out_ref, made, sems):
+    keys = size // 2 - rows
+
+    def kernel(turned_ref, turned_other_ref, held_ref, mate_ref, b0, b2, b3, b1, facts_ref, out_ref, made, sems):
         takes = row(facts_ref[...], B_ME) > 0
-        core, y = core_at(), ring_at()
+        y = ring_at()
         copies = []
-        for side, (whose, kept) in enumerate(((core, held_ref), (1 - core, mate_ref))):
+        sides = ((core_at(), turned_ref, held_ref), (1 - core_at(), turned_other_ref, mate_ref))
+        for side, (whose, early, kept) in enumerate(sides):
+            base = whose * (size // 2)
+            to = out_ref.at[pl.ds(pl.multiple_of(base, 8), keys), :]
+            copies.append(pltpu.make_async_copy(early.at[TURN:], to, sems.at[len(copies)]))
+            copies[-1].start()
             for d, src in enumerate((b0, b1, b2, b3)):
                 at = pl.multiple_of((y + GROUP - d) % GROUP * piece, 8)
                 block = side * GROUP + d
                 made[block] = jnp.where(takes, src[side * piece : (side + 1) * piece], kept[pl.ds(at, piece), :])
-                to = out_ref.at[pl.ds(pl.multiple_of(whose * rows + at, 8), piece), :]
-                copies.append(pltpu.make_async_copy(made.at[block], to, sems.at[block]))
+                to = out_ref.at[pl.ds(pl.multiple_of(base + keys + at, 8), piece), :]
+                copies.append(pltpu.make_async_copy(made.at[block], to, sems.at[len(copies)]))
                 copies[-1].start()
         for copy in copies:
             copy.wait()
 
     return pl.pallas_call(
         kernel,
-        in_specs=[STAYS] * 7,
+        in_specs=[STAYS] * 9,
         out_specs=pl.BlockSpec(memory_space=pl.ANY),
-        out_shape=jax.ShapeDtypeStruct((2 * rows, width), f32),
-        scratch_shapes=[pltpu.VMEM((blocks, piece, width), f32), pltpu.SemaphoreType.DMA((blocks,))],
+        out_shape=jax.ShapeDtypeStruct((size, width), f32),
+        scratch_shapes=[pltpu.VMEM((blocks, piece, width), f32), pltpu.SemaphoreType.DMA((blocks + 2,))],
         compiler_params=pltpu.CompilerParams(vmem_limit_bytes=8 << 20),
         name="finish",
-    )(*in_vmem(held, held_mate, p0, p2, p3, p1, facts))
+    )(*in_vmem(turned, turned_other, held, held_mate, p0, p2, p3, p1, facts))
 
 
 def ring(step):
@@ -428,29 +467,39 @@
     f, v, o, wq, wk = [a[0, 0] for a in (features, values, out_grad, query_weight, key_weight)]
     mq, sq, mk, sk = [a[0, 0] for a in (query_mean, query_square, key_mean, key_square)]
 
-    mine0, other0, facts, ds, queries, ft = query_step(members, f, v, o, wq, wk, mq, sq)
+    size = wq.shape[0]
+    mine0, turn, other0, facts, ds, queries, ft = query_step(members, f, v, o, wq, wk, mq, sq)
     theirs0 = to_mate(other0)
-    part0, facts = chip_sum(mine0, theirs0, facts, True)
+    part0, facts = chip_sum(mine0, theirs0, facts)
     far0 = to_far(part0)
-    mine1, other1 = key_step(after(ds, part0), queries, ft, wk, mk, sk)
-    theirs1 = to_mate(other1)
-    part1, _ = chip_sum(mine1, theirs1, facts, False)
+    mine1, mine2, other1, other2 = key_step(after(ds, part0), queries, ft, turn, wk, mk, sk)
+    part1, theirs1 = chip_sum_turned(mine1, theirs0, to_mate(other1), facts)
     far1 = to_far(after(part1, far0))
+    theirs2 = to_mate(after(other2, far0))
+    part2 = chip_sum_last(mine2, theirs2, facts)
+    far2 = to_far(after(part2, far1))
 
     own0, s2, s1, s3, held0, held_mate0, facts = row_mean(mine0, theirs0, far0, facts, True)
-    total0, facts = col_mean(own0, around(s2, s1, s3), facts, True)
+    total0, facts = col_mean(own0, around(s2, s1, s3), facts, first=True)
     p2, p1, p3 = around(total0, total0, total0)
-    query_mine, query_mate = choose(held0, held_mate0, total0, p3, p1, p2, facts)
-    query_other = to_mate(query_mate)
+    me0, mate0 = choose(held0, held_mate0, total0, p3, p1, p2, facts)
+    other0 = to_mate(mate0)
 
     own1, s2, s1, s3, held1, held_mate1, _ = row_mean(mine1, theirs1, after(far1, total0), facts, False)
     got1 = around(s2, s1, s3)
-    held_mate1 = to_mate(held_mate1)
-    me, mate = col_mean(after(own1, query_mine), got1, facts, False)
-    total1 = joined(me, to_mate(mate))
+    total1 = col_mean(after(own1, me0), got1, facts)[0]
     p2, p1, p3 = around(total1, total1, total1)
-    query = place(query_mine, query_other)
-    key = finish(held1, held_mate1, total1, after(p2, query), p3, p1, facts)
+    me1, mate1 = choose(held1, held_mate1, total1, p3, p1, p2, facts)
+    other1 = to_mate(mate1)
+
+    own2, s2, s1, s3, held2, held_mate2, _ = row_mean(mine2, theirs2, after(far2, total1), facts, False)
+    got2 = around(s2, s1, s3)
+    held_mate2 = to_mate(held_mate2)
+    me2, mate2 = col_mean(after(own2, me1), got2, facts, split=True)
+    total2 = joined(me2, to_mate(mate2))
+    p2, p1, p3 = around(total2, total2, total2)
+    query = place(size, me0, other0, me1, other1)
+    key = finish(size, me1, other1, held2, held_mate2, total2, after(p2, query), p3, p1, facts)
     return query[None, None], key[None, None]
 
 

time: 111 us -> 109 us (0.982)
  waiting for transfers between devices: 58.9 us -> 49.3 us
  starting transfers between devices: 23.2 us -> 32 us
    ppermute x12 -> x18, starting transfers between devices: 15.6 us -> 21.6 us  [around(): lax.ppermute(x, 'col', ring(d))]
    ppermute x2 -> x3, waiting for transfers between devices: 22.1 us -> 17.3 us  [to_far(): return lax.ppermute(x, 'row', swap(2))]
    ppermute x12 -> x18, waiting for transfers between devices: 32.8 us -> 29.5 us  [around(): lax.ppermute(x, 'col', ring(d))]
    ppermute x5 -> x7, starting transfers between devices: 6.29 us -> 8.9 us  [to_mate(): return lax.ppermute(x, 'row', swap(1))]
    ppermute x5 -> x7, waiting for transfers between devices: 4.09 us -> 2.52 us  [to_mate(): return lax.ppermute(x, 'row', swap(1))]
  transfers between devices with their start and end apart: 19 -> 28, of which waited for: 12 -> 16; matrix products, arithmetic and copies ran while one was open for 0% -> 0% of each run, Pallas kernels for 9% -> 8%
where the time goes in v4:
time: 109 us
  waiting for transfers between devices  49.3 us (45%)
  starting transfers between devices  32 us (29%)
  Pallas kernels  26.7 us (24%)
    ppermute x18, waiting for transfers between devices, around(): lax.ppermute(x, 'col', ring(d))  29.5 us
    ppermute x18, starting transfers between devices, around(): lax.ppermute(x, 'col', ring(d))  21.6 us
    ppermute x3, waiting for transfers between devices, to_far(): return lax.ppermute(x, 'row', swap(2))  17.3 us
    pallas_call x1, Pallas kernels, query_step(): pl.pallas_call(query_kernel, grid=(heads // QUAD,), in_specs=[SCALARS, fu...  17.2 us
    ppermute x7, starting transfers between devices, to_mate(): return lax.ppermute(x, 'row', swap(1))  8.9 us
    pallas_call x1, Pallas kernels, key_step(): pl.pallas_call(key_kernel, grid=(heads // QUAD,), in_specs=[STAYS] * 4 +...  6.29 us
    ppermute x7, waiting for transfers between devices, to_mate(): return lax.ppermute(x, 'row', swap(1))  2.52 us
  transfers between devices with their start and end apart: 28, of which 16 were waited for; matrix products, arithmetic and copies ran while one was open for 0% of the time, Pallas kernels for 8%

profile of v4, /device:TPU:1, one launch (start us, length us, event | category | flops | bytes accessed | tf_op | source)
XLA Modules:
  0.0 108.9 jit_solution(14859645382171470805)
XLA Ops:
  0.6 17.2 %query_step.1 = (f32[160,512]{1,0:T(8,128)S(1)}, f32[96,512]{1,0:T(8,128)S(1)}, f32[264,512]{1,0:T(8,128)S(1)}, f32[8,512]{1,0:T(8,128)S(1)}, bf16[8,1024,512]{2...) custom-call(s32[1,1,2]{2,1,0:T(1,128)} %members.1, bf16[1024,512]{1,0:T(8,128)(2,1)} %bitcast.15, ...), custom_call_target="tpu_custom_call" | custom-call | tf_op jit(solution)/shard_map/query_step/pallas_call | solution.py:195
  17.8 3.3 %collective-permute-start = (f32[264,512]{1,0:T(8,128)S(1)}, f32[264,512]{1,0:T(8,128)S(1)}, u32[]{:S(2)}, u32[]{:S(2)}) collective-permute-start(f32[264,512]{1,0:T(8,128)S(1)} %get-tuple-element.54), channel_id=1, source_target_pairs={{0,32},{32,0},{64,96},{96,64},{128,160},{160,128},{192,224},{224,1... | collective-permute-start | bytes 1622024 | tf_op jit(solution)/shard_map/ppermute | solution.py:451
  21.2 1.6 %collective-permute-done.theirs_ref.tq_ref = f32[264,512]{1,0:T(8,128)S(1)} collective-permute-done((f32[264,512]{1,0:T(8,128)S(1)}, f32[264,512]{1,0:T(8,128)S(1)}, u32[]{:S(2)}, u32[]{:S(2)}) %collective-permute-start) | collective-permute-done | bytes 540704 | tf_op jit(solution)/shard_map/ppermute | solution.py:451
  24.1 6.3 %key_step.1 = (f32[160,512]{1,0:T(8,128)S(1)}, f32[192,512]{1,0:T(8,128)S(1)}, f32[64,512]{1,0:T(8,128)S(1)}, f32[192,512]{1,0:T(8,128)S(1)}) custom-call(bf16[8,1024,512]{2,1,0:T(8,128)(2,1)S(1)} %get-tuple-element.70.ds_ref, bf16[1024,512]{1,0:T(8,128)(2,1)S(1)} %get-tuple-element.71.q_ref, bf16[512,1024]{1,0:T(8,128)(2,1)S(1)} %get-tuple-element.72.ft_ref, ...), custom_call_target="tpu_custom_call" | custom-call | tf_op jit(solution)/shard_map/key_step/pallas_call | solution.py:220
  31.2 9.7 %collective-permute-done.1.far_ref = f32[168,512]{1,0:T(8,128)S(1)} collective-permute-done((f32[168,512]{1,0:T(8,128)S(1)}, f32[168,512]{1,0:T(8,128)S(1)}, u32[]{:S(2)}, u32[]{:S(2)}) %collective-permute-start.1) | collective-permute-done | bytes 344096 | tf_op jit(solution)/shard_map/ppermute | solution.py:455
  42.0 2.1 %collective-permute-start.2 = (f32[88,512]{1,0:T(8,128)S(1)}, f32[88,512]{1,0:T(8,128)S(1)}, u32[]{:S(2)}, u32[]{:S(2)}) collective-permute-start(f32[88,512]{1,0:T(8,128)S(1)} %get-tuple-element.61), channel_id=1, source_target_pairs={{0,2},{1,3},{2,0},{3,1},{4,6},{5,7},{6,4},{7,5},{8,10},{9,11},{10,... | collective-permute-start | bytes 540680 | tf_op jit(solution)/shard_map/ppermute | solution.py:459
  44.5 2.3 %collective-permute-start.4 = (f32[88,512]{1,0:T(8,128)S(1)}, f32[88,512]{1,0:T(8,128)S(1)}, u32[]{:S(2)}, u32[]{:S(2)}) collective-permute-start(f32[88,512]{1,0:T(8,128)S(1)} %get-tuple-element.63), channel_id=1, source_target_pairs={{0,3},{1,0},{2,1},{3,2},{4,7},{5,4},{6,5},{7,6},{8,11},{9,8},{10,9... | collective-permute-start | bytes 540680 | tf_op jit(solution)/shard_map/ppermute | solution.py:459
  46.8 3.2 %collective-permute-done.2.g1 = f32[88,512]{1,0:T(8,128)S(1)} collective-permute-done((f32[88,512]{1,0:T(8,128)S(1)}, f32[88,512]{1,0:T(8,128)S(1)}, u32[]{:S(2)}, u32[]{:S(2)}) %collective-permute-start.2) | collective-permute-done | bytes 180256 | tf_op jit(solution)/shard_map/ppermute | solution.py:459
  50.0 4.1 %collective-permute-done.3.g2 = f32[88,512]{1,0:T(8,128)S(1)} collective-permute-done((f32[88,512]{1,0:T(8,128)S(1)}, f32[88,512]{1,0:T(8,128)S(1)}, u32[]{:S(2)}, u32[]{:S(2)}) %collective-permute-start.3) | collective-permute-done | bytes 180256 | tf_op jit(solution)/shard_map/ppermute | solution.py:459
  56.5 4.1 %collective-permute-done.10.far_ref = f32[176,512]{1,0:T(8,128)S(1)} collective-permute-done((f32[176,512]{1,0:T(8,128)S(1)}, f32[176,512]{1,0:T(8,128)S(1)}, u32[]{:S(2)}, u32[]{:S(2)}) %collective-permute-start.10) | collective-permute-done | bytes 360480 | tf_op jit(solution)/shard_map/ppermute | solution.py:455
  60.6 1.5 %collective-permute-start.5 = (f32[80,512]{1,0:T(8,128)S(1)}, f32[80,512]{1,0:T(8,128)S(1)}, u32[]{:S(2)}, u32[]{:S(2)}) collective-permute-start(f32[80,512]{1,0:T(8,128)S(1)} %get-tuple-element.65.b0), channel_id=1, source_target_pairs={{0,3},{1,0},{2,1},{3,2},{4,7},{5,4},{6,5},{7,6},{8,11},{9,8},{10,9... | collective-permute-start | bytes 491528 | tf_op jit(solution)/shard_map/ppermute | solution.py:459
  63.4 2.0 %collective-permute-done.6.b1 = f32[80,512]{1,0:T(8,128)S(1)} collective-permute-done((f32[80,512]{1,0:T(8,128)S(1)}, f32[80,512]{1,0:T(8,128)S(1)}, u32[]{:S(2)}, u32[]{:S(2)}) %collective-permute-start.6) | collective-permute-done | bytes 163872 | tf_op jit(solution)/shard_map/ppermute | solution.py:459
  66.1 2.5 %collective-permute-done.11.g1 = f32[80,512]{1,0:T(8,128)S(1)} collective-permute-done((f32[80,512]{1,0:T(8,128)S(1)}, f32[80,512]{1,0:T(8,128)S(1)}, u32[]{:S(2)}, u32[]{:S(2)}) %collective-permute-start.11) | collective-permute-done | bytes 163872 | tf_op jit(solution)/shard_map/ppermute | solution.py:459
  68.6 5.0 %collective-permute-done.12.g2 = f32[80,512]{1,0:T(8,128)S(1)} collective-permute-done((f32[80,512]{1,0:T(8,128)S(1)}, f32[80,512]{1,0:T(8,128)S(1)}, u32[]{:S(2)}, u32[]{:S(2)}) %collective-permute-start.12) | collective-permute-done | bytes 163872 | tf_op jit(solution)/shard_map/ppermute | solution.py:459
  74.4 2.2 %collective-permute-start.15 = (f32[80,512]{1,0:T(8,128)S(1)}, f32[80,512]{1,0:T(8,128)S(1)}, u32[]{:S(2)}, u32[]{:S(2)}) collective-permute-start(f32[80,512]{1,0:T(8,128)S(1)} %col_mean.4.b0), channel_id=1, source_target_pairs={{0,1},{1,2},{2,3},{3,0},{4,5},{5,6},{6,7},{7,4},{8,9},{9,10},{10,1... | collective-permute-start | bytes 491528 | tf_op jit(solution)/shard_map/ppermute | solution.py:459
  77.1 3.5 %collective-permute-done.19.far_ref = f32[200,512]{1,0:T(8,128)S(1)} collective-permute-done((f32[200,512]{1,0:T(8,128)S(1)}, f32[200,512]{1,0:T(8,128)S(1)}, u32[]{:S(2)}, u32[]{:S(2)}) %collective-permute-start.19) | collective-permute-done | bytes 409632 | tf_op jit(solution)/shard_map/ppermute | solution.py:455
  80.8 2.0 %collective-permute-start.21 = (f32[96,512]{1,0:T(8,128)S(1)}, f32[96,512]{1,0:T(8,128)S(1)}, u32[]{:S(2)}, u32[]{:S(2)}) collective-permute-start(f32[96,512]{1,0:T(8,128)S(1)} %get-tuple-element.98), channel_id=1, source_target_pairs={{0,2},{1,3},{2,0},{3,1},{4,6},{5,7},{6,4},{7,5},{8,10},{9,11},{10,... | collective-permute-start | bytes 589832 | tf_op jit(solution)/shard_map/ppermute | solution.py:459
  84.6 1.7 %collective-permute-start.23 = (f32[96,512]{1,0:T(8,128)S(1)}, f32[96,512]{1,0:T(8,128)S(1)}, u32[]{:S(2)}, u32[]{:S(2)}) collective-permute-start(f32[96,512]{1,0:T(8,128)S(1)} %get-tuple-element.100), channel_id=1, source_target_pairs={{0,3},{1,0},{2,1},{3,2},{4,7},{5,4},{6,5},{7,6},{8,11},{9,8},{10,9... | collective-permute-start | bytes 589832 | tf_op jit(solution)/shard_map/ppermute | solution.py:459
  88.4 2.3 %collective-permute-start.17 = (f32[160,512]{1,0:T(8,128)S(1)}, f32[160,512]{1,0:T(8,128)S(1)}, u32[]{:S(2)}, u32[]{:S(2)}) collective-permute-start(f32[160,512]{1,0:T(8,128)S(1)} %get-tuple-element.88), channel_id=1, source_target_pairs={{0,32},{32,0},{64,96},{96,64},{128,160},{160,128},{192,224},{224,1... | collective-permute-start | bytes 983048 | tf_op jit(solution)/shard_map/ppermute | solution.py:451
  90.7 2.8 %collective-permute-done.22.g2 = f32[96,512]{1,0:T(8,128)S(1)} collective-permute-done((f32[96,512]{1,0:T(8,128)S(1)}, f32[96,512]{1,0:T(8,128)S(1)}, u32[]{:S(2)}, u32[]{:S(2)}) %collective-permute-start.22) | collective-permute-done | bytes 196640 | tf_op jit(solution)/shard_map/ppermute | solution.py:459
  95.0 2.0 %collective-permute-start.25 = (f32[96,512]{1,0:T(8,128)S(1)}, f32[96,512]{1,0:T(8,128)S(1)}, u32[]{:S(2)}, u32[]{:S(2)}) collective-permute-start(f32[96,512]{1,0:T(8,128)S(1)} %joined.1.b0), channel_id=1, source_target_pairs={{0,2},{1,3},{2,0},{3,1},{4,6},{5,7},{6,4},{7,5},{8,10},{9,11},{10,... | collective-permute-start | bytes 589832 | tf_op jit(solution)/shard_map/ppermute | solution.py:459
  97.9 1.8 %collective-permute-start.26 = (f32[96,512]{1,0:T(8,128)S(1)}, f32[96,512]{1,0:T(8,128)S(1)}, u32[]{:S(2)}, u32[]{:S(2)}) collective-permute-start(f32[96,512]{1,0:T(8,128)S(1)} %joined.1.b0), channel_id=1, source_target_pairs={{0,3},{1,0},{2,1},{3,2},{4,7},{5,4},{6,5},{7,6},{8,11},{9,8},{10,9... | collective-permute-start | bytes 589832 | tf_op jit(solution)/shard_map/ppermute | solution.py:459
  100.7 2.1 %collective-permute-done.25.b2 = f32[96,512]{1,0:T(8,128)S(1)} collective-permute-done((f32[96,512]{1,0:T(8,128)S(1)}, f32[96,512]{1,0:T(8,128)S(1)}, u32[]{:S(2)}, u32[]{:S(2)}) %collective-permute-start.25) | collective-permute-done | bytes 196640 | tf_op jit(solution)/shard_map/ppermute | solution.py:459
  102.8 4.9 %collective-permute-done.27.b1 = f32[96,512]{1,0:T(8,128)S(1)} collective-permute-done((f32[96,512]{1,0:T(8,128)S(1)}, f32[96,512]{1,0:T(8,128)S(1)}, u32[]{:S(2)}, u32[]{:S(2)}) %collective-permute-start.27) | collective-permute-done | bytes 196640 | tf_op jit(solution)/shard_map/ppermute | solution.py:459
  (48 shorter events, 17.8 us)
Async XLA Ops:
  22.8 18.1 %collective-permute-start.1 = (f32[168,512]{1,0:T(8,128)S(1)}, f32[168,512]{1,0:T(8,128)S(1)}, u32[]{:S(2)}, u32[]{:S(2)}) collective-permute-start(f32[168,512]{1,0:T(8,128)S(1)} %get-tuple-element.56), channel_id=1, source_target_pairs={{0,64},{32,96},{64,0},{96,32},{128,192},{160,224},{192,128},{224,1... | collective-permute-start | bytes 1032200 | tf_op jit(solution)/shard_map/ppermute | solution.py:455
  30.4 11.2 %collective-permute-start.9 = (f32[64,512]{1,0:T(8,128)S(1)}, f32[64,512]{1,0:T(8,128)S(1)}, u32[]{:S(2)}, u32[]{:S(2)}) collective-permute-start(f32[64,512]{1,0:T(8,128)S(1)} %get-tuple-element.75), channel_id=1, source_target_pairs={{0,32},{32,0},{64,96},{96,64},{128,160},{160,128},{192,224},{224,1... | collective-permute-start | bytes 393224 | tf_op jit(solution)/shard_map/ppermute | solution.py:451
  40.9 15.6 %collective-permute-start.18 = (f32[192,512]{1,0:T(8,128)S(1)}, f32[192,512]{1,0:T(8,128)S(1)}, u32[]{:S(2)}, u32[]{:S(2)}) collective-permute-start(f32[192,512]{1,0:T(8,128)S(1)} %get-tuple-element.91), channel_id=1, source_target_pairs={{0,32},{32,0},{64,96},{96,64},{128,160},{160,128},{192,224},{224,1... | collective-permute-start | bytes 1179656 | tf_op jit(solution)/shard_map/ppermute | solution.py:451
  41.7 18.9 %collective-permute-start.10 = (f32[176,512]{1,0:T(8,128)S(1)}, f32[176,512]{1,0:T(8,128)S(1)}, u32[]{:S(2)}, u32[]{:S(2)}) collective-permute-start(f32[176,512]{1,0:T(8,128)S(1)} %get-tuple-element.78), channel_id=1, source_target_pairs={{0,64},{32,96},{64,0},{96,32},{128,192},{160,224},{192,128},{224,1... | collective-permute-start | bytes 1081352 | tf_op jit(solution)/shard_map/ppermute | solution.py:455
  42.0 8.0 %collective-permute-start.2 = (f32[88,512]{1,0:T(8,128)S(1)}, f32[88,512]{1,0:T(8,128)S(1)}, u32[]{:S(2)}, u32[]{:S(2)}) collective-permute-start(f32[88,512]{1,0:T(8,128)S(1)} %get-tuple-element.61), channel_id=1, source_target_pairs={{0,2},{1,3},{2,0},{3,1},{4,6},{5,7},{6,4},{7,5},{8,10},{9,11},{10,... | collective-permute-start | bytes 540680 | tf_op jit(solution)/shard_map/ppermute | solution.py:459
  44.1 10.1 %collective-permute-start.3 = (f32[88,512]{1,0:T(8,128)S(1)}, f32[88,512]{1,0:T(8,128)S(1)}, u32[]{:S(2)}, u32[]{:S(2)}) collective-permute-start(f32[88,512]{1,0:T(8,128)S(1)} %get-tuple-element.62), channel_id=1, source_target_pairs={{0,1},{1,2},{2,3},{3,0},{4,5},{5,6},{6,7},{7,4},{8,9},{9,10},{10,1... | collective-permute-start | bytes 540680 | tf_op jit(solution)/shard_map/ppermute | solution.py:459
  44.5 9.7 %collective-permute-start.4 = (f32[88,512]{1,0:T(8,128)S(1)}, f32[88,512]{1,0:T(8,128)S(1)}, u32[]{:S(2)}, u32[]{:S(2)}) collective-permute-start(f32[88,512]{1,0:T(8,128)S(1)} %get-tuple-element.63), channel_id=1, source_target_pairs={{0,3},{1,0},{2,1},{3,2},{4,7},{5,4},{6,5},{7,6},{8,11},{9,8},{10,9... | collective-permute-start | bytes 540680 | tf_op jit(solution)/shard_map/ppermute | solution.py:459
  54.2 8.5 %collective-permute-start.7 = (f32[80,512]{1,0:T(8,128)S(1)}, f32[80,512]{1,0:T(8,128)S(1)}, u32[]{:S(2)}, u32[]{:S(2)}) collective-permute-start(f32[80,512]{1,0:T(8,128)S(1)} %get-tuple-element.65.b0), channel_id=1, source_target_pairs={{0,2},{1,3},{2,0},{3,1},{4,6},{5,7},{6,4},{7,5},{8,10},{9,11},{10,... | collective-permute-start | bytes 491528 | tf_op jit(solution)/shard_map/ppermute | solution.py:459
  55.4 10.0 %collective-permute-start.6 = (f32[80,512]{1,0:T(8,128)S(1)}, f32[80,512]{1,0:T(8,128)S(1)}, u32[]{:S(2)}, u32[]{:S(2)}) collective-permute-start(f32[80,512]{1,0:T(8,128)S(1)} %get-tuple-element.65.b0), channel_id=1, source_target_pairs={{0,1},{1,2},{2,3},{3,0},{4,5},{5,6},{6,7},{7,4},{8,9},{9,10},{10,1... | collective-permute-start | bytes 491528 | tf_op jit(solution)/shard_map/ppermute | solution.py:459
  60.6 20.0 %collective-permute-start.19 = (f32[200,512]{1,0:T(8,128)S(1)}, f32[200,512]{1,0:T(8,128)S(1)}, u32[]{:S(2)}, u32[]{:S(2)}) collective-permute-start(f32[200,512]{1,0:T(8,128)S(1)} %chip_sum_last.1), channel_id=1, source_target_pairs={{0,64},{32,96},{64,0},{96,32},{128,192},{160,224},{192,128},{224,1... | collective-permute-start | bytes 1228808 | tf_op jit(solution)/shard_map/ppermute | solution.py:455
  62.7 10.8 %collective-permute-start.12 = (f32[80,512]{1,0:T(8,128)S(1)}, f32[80,512]{1,0:T(8,128)S(1)}, u32[]{:S(2)}, u32[]{:S(2)}) collective-permute-start(f32[80,512]{1,0:T(8,128)S(1)} %get-tuple-element.85), channel_id=1, source_target_pairs={{0,1},{1,2},{2,3},{3,0},{4,5},{5,6},{6,7},{7,4},{8,9},{9,10},{10,1... | collective-permute-start | bytes 491528 | tf_op jit(solution)/shard_map/ppermute | solution.py:459
  65.4 8.1 %collective-permute-start.13 = (f32[80,512]{1,0:T(8,128)S(1)}, f32[80,512]{1,0:T(8,128)S(1)}, u32[]{:S(2)}, u32[]{:S(2)}) collective-permute-start(f32[80,512]{1,0:T(8,128)S(1)} %get-tuple-element.86), channel_id=1, source_target_pairs={{0,3},{1,0},{2,1},{3,2},{4,7},{5,4},{6,5},{7,6},{8,11},{9,8},{10,9... | collective-permute-start | bytes 491528 | tf_op jit(solution)/shard_map/ppermute | solution.py:459
  73.6 10.0 %collective-permute-start.16 = (f32[80,512]{1,0:T(8,128)S(1)}, f32[80,512]{1,0:T(8,128)S(1)}, u32[]{:S(2)}, u32[]{:S(2)}) collective-permute-start(f32[80,512]{1,0:T(8,128)S(1)} %col_mean.4.b0), channel_id=1, source_target_pairs={{0,2},{1,3},{2,0},{3,1},{4,6},{5,7},{6,4},{7,5},{8,10},{9,11},{10,... | collective-permute-start | bytes 491528 | tf_op jit(solution)/shard_map/ppermute | solution.py:459
  74.4 10.1 %collective-permute-start.15 = (f32[80,512]{1,0:T(8,128)S(1)}, f32[80,512]{1,0:T(8,128)S(1)}, u32[]{:S(2)}, u32[]{:S(2)}) collective-permute-start(f32[80,512]{1,0:T(8,128)S(1)} %col_mean.4.b0), channel_id=1, source_target_pairs={{0,1},{1,2},{2,3},{3,0},{4,5},{5,6},{6,7},{7,4},{8,9},{9,10},{10,1... | collective-permute-start | bytes 491528 | tf_op jit(solution)/shard_map/ppermute | solution.py:459
  76.6 9.6 %collective-permute-start.14 = (f32[80,512]{1,0:T(8,128)S(1)}, f32[80,512]{1,0:T(8,128)S(1)}, u32[]{:S(2)}, u32[]{:S(2)}) collective-permute-start(f32[80,512]{1,0:T(8,128)S(1)} %col_mean.4.b0), channel_id=1, source_target_pairs={{0,3},{1,0},{2,1},{3,2},{4,7},{5,4},{6,5},{7,6},{8,11},{9,8},{10,9... | collective-permute-start | bytes 491528 | tf_op jit(solution)/shard_map/ppermute | solution.py:459
  80.8 7.6 %collective-permute-start.21 = (f32[96,512]{1,0:T(8,128)S(1)}, f32[96,512]{1,0:T(8,128)S(1)}, u32[]{:S(2)}, u32[]{:S(2)}) collective-permute-start(f32[96,512]{1,0:T(8,128)S(1)} %get-tuple-element.98), channel_id=1, source_target_pairs={{0,2},{1,3},{2,0},{3,1},{4,6},{5,7},{6,4},{7,5},{8,10},{9,11},{10,... | collective-permute-start | bytes 589832 | tf_op jit(solution)/shard_map/ppermute | solution.py:459
  82.8 15.1 %collective-permute-start.8 = (f32[160,512]{1,0:T(8,128)S(1)}, f32[160,512]{1,0:T(8,128)S(1)}, u32[]{:S(2)}, u32[]{:S(2)}) collective-permute-start(f32[160,512]{1,0:T(8,128)S(1)} %get-tuple-element.68), channel_id=1, source_target_pairs={{0,32},{32,0},{64,96},{96,64},{128,160},{160,128},{192,224},{224,1... | collective-permute-start | bytes 983048 | tf_op jit(solution)/shard_map/ppermute | solution.py:451
  83.6 9.9 %collective-permute-start.22 = (f32[96,512]{1,0:T(8,128)S(1)}, f32[96,512]{1,0:T(8,128)S(1)}, u32[]{:S(2)}, u32[]{:S(2)}) collective-permute-start(f32[96,512]{1,0:T(8,128)S(1)} %get-tuple-element.99), channel_id=1, source_target_pairs={{0,1},{1,2},{2,3},{3,0},{4,5},{5,6},{6,7},{7,4},{8,9},{9,10},{10,1... | collective-permute-start | bytes 589832 | tf_op jit(solution)/shard_map/ppermute | solution.py:459
  84.6 9.0 %collective-permute-start.23 = (f32[96,512]{1,0:T(8,128)S(1)}, f32[96,512]{1,0:T(8,128)S(1)}, u32[]{:S(2)}, u32[]{:S(2)}) collective-permute-start(f32[96,512]{1,0:T(8,128)S(1)} %get-tuple-element.100), channel_id=1, source_target_pairs={{0,3},{1,0},{2,1},{3,2},{4,7},{5,4},{6,5},{7,6},{8,11},{9,8},{10,9... | collective-permute-start | bytes 589832 | tf_op jit(solution)/shard_map/ppermute | solution.py:459
  86.3 16.6 %collective-permute-start.20 = (f32[192,512]{1,0:T(8,128)S(1)}, f32[192,512]{1,0:T(8,128)S(1)}, u32[]{:S(2)}, u32[]{:S(2)}) collective-permute-start(f32[192,512]{1,0:T(8,128)S(1)} %get-tuple-element.95), channel_id=1, source_target_pairs={{0,32},{32,0},{64,96},{96,64},{128,160},{160,128},{192,224},{224,1... | collective-permute-start | bytes 1179656 | tf_op jit(solution)/shard_map/ppermute | solution.py:451
  88.4 11.3 %collective-permute-start.17 = (f32[160,512]{1,0:T(8,128)S(1)}, f32[160,512]{1,0:T(8,128)S(1)}, u32[]{:S(2)}, u32[]{:S(2)}) collective-permute-start(f32[160,512]{1,0:T(8,128)S(1)} %get-tuple-element.88), channel_id=1, source_target_pairs={{0,32},{32,0},{64,96},{96,64},{128,160},{160,128},{192,224},{224,1... | collective-permute-start | bytes 983048 | tf_op jit(solution)/shard_map/ppermute | solution.py:451
  95.0 7.8 %collective-permute-start.25 = (f32[96,512]{1,0:T(8,128)S(1)}, f32[96,512]{1,0:T(8,128)S(1)}, u32[]{:S(2)}, u32[]{:S(2)}) collective-permute-start(f32[96,512]{1,0:T(8,128)S(1)} %joined.1.b0), channel_id=1, source_target_pairs={{0,2},{1,3},{2,0},{3,1},{4,6},{5,7},{6,4},{7,5},{8,10},{9,11},{10,... | collective-permute-start | bytes 589832 | tf_op jit(solution)/shard_map/ppermute | solution.py:459
  97.0 10.7 %collective-permute-start.27 = (f32[96,512]{1,0:T(8,128)S(1)}, f32[96,512]{1,0:T(8,128)S(1)}, u32[]{:S(2)}, u32[]{:S(2)}) collective-permute-start(f32[96,512]{1,0:T(8,128)S(1)} %joined.1.b0), channel_id=1, source_target_pairs={{0,1},{1,2},{2,3},{3,0},{4,5},{5,6},{6,7},{7,4},{8,9},{9,10},{10,1... | collective-permute-start | bytes 589832 | tf_op jit(solution)/shard_map/ppermute | solution.py:459
  97.9 9.8 %collective-permute-start.26 = (f32[96,512]{1,0:T(8,128)S(1)}, f32[96,512]{1,0:T(8,128)S(1)}, u32[]{:S(2)}, u32[]{:S(2)}) collective-permute-start(f32[96,512]{1,0:T(8,128)S(1)} %joined.1.b0), channel_id=1, source_target_pairs={{0,3},{1,0},{2,1},{3,2},{4,7},{5,4},{6,5},{7,6},{8,11},{9,8},{10,9... | collective-permute-start | bytes 589832 | tf_op jit(solution)/shard_map/ppermute | solution.py:459
  (4 other events, 18.0 us)

commit v5 on v4

--- a/solution.py
+++ b/solution.py
@@ -279,11 +279,9 @@
         f = facts_ref[...]
         theirs_out[:TURN] = tq_ref[FIRST : FIRST + TURN]
         theirs_out[TURN:] = tk_ref[...]
-        out_ref[:rows] = row(f, A_ME) * turned_ref[...] + row(f, A_MATE) * theirs_out[...]
-        out_ref[rows : rows + NOTE] = f
-        out_ref[rows + NOTE :] = f
-
-    shapes = [(rows + 2 * NOTE, width), (rows, width)]
+        out_ref[...] = row(f, A_ME) * turned_ref[...] + row(f, A_MATE) * theirs_out[...]
+
+    shapes = [(rows, width), (rows, width)]
     return small_call(kernel, "chip_sum_turned", shapes, turned, theirs_query, theirs_key, facts)
 
 
@@ -292,10 +290,9 @@
 
     def kernel(mine_ref, theirs_ref, facts_ref, out_ref):
         f = facts_ref[...]
-        out_ref[:rows] = row(f, A_ME) * mine_ref[...] + row(f, A_MATE) * theirs_ref[...]
-        out_ref[rows:] = f
-
-    return small_call(kernel, "chip_sum_last", [(rows + NOTE, width)], mine, theirs, facts)[0]
+        out_ref[...] = row(f, A_ME) * mine_ref[...] + row(f, A_MATE) * theirs_ref[...]
+
+    return small_call(kernel, "chip_sum_last", [(rows, width)], mine, theirs, facts)[0]
 
 
 def row_mean(mine, theirs, far, facts, first):
@@ -319,39 +316,38 @@
             held[here, :] = m
             held_mate[here, :] = t
             out[:piece] = m * row(f, B_ME)
-            out[piece : 2 * piece] = t * row(f, B_MATE)
-            if first and d:
-                out[2 * piece :] = f
-
-    sent = (2 * piece + (NOTE if first else 0), width)
-    shapes = [(2 * piece, width), sent, sent, sent, (rows, width), (rows, width)]
+            out[piece:] = t * row(f, B_MATE)
+
+    shapes = [(2 * piece, width)] * 4 + [(rows, width)] * 2
     if first:
         shapes = shapes + [facts.shape]
     got = small_call(kernel, "row_mean", shapes, mine, theirs, far, facts)
     return got if first else got + [facts]
 
 
-def col_mean(own, got, facts, first=False, split=False):
+def col_sum(own, got, facts):
+    rows, width = own.shape
+
+    def kernel(own_ref, g1, g2, g3, facts_ref, out):
+        out[:rows] = own_ref[...] + g1[...] + g2[...] + g3[...]
+        out[rows:] = facts_ref[...]
+
+    return small_call(kernel, "col_sum", [(rows + NOTE, width)], own, *got, facts)[0]
+
+
+def col_mean(own, got, facts, split=False):
     rows, width = own.shape
     piece = rows // 2
 
     def kernel(own_ref, g1, g2, g3, facts_ref, *outs):
         f = facts_ref[...]
-        if first:
-            at = lax.broadcasted_iota(jnp.int32, f.shape, 0)
-            notes = [g[rows:] for g in (g1, g2, g3)]
-            count = sum([row(n, B_ME) for n in notes], row(f, B_ME))
-            count_mate = sum([row(n, B_MATE) for n in notes], row(f, B_MATE))
-            f = jnp.where(at == B_COUNT, jnp.maximum(count, 1.0), f)
-            f = jnp.where(at == B_COUNT_MATE, jnp.maximum(count_mate, 1.0), f)
-            outs[1][...] = f
-        total = own_ref[...] + g1[:rows] + g2[:rows] + g3[:rows]
+        total = own_ref[...] + g1[...] + g2[...] + g3[...]
         mate = outs[1] if split else outs[0].at[piece:]
         outs[0][:piece] = total[:piece] / row(f, B_COUNT)
         mate[...] = total[piece:] / row(f, B_COUNT_MATE)
 
     shapes = [(piece, width)] * 2 if split else [(rows, width)]
-    return small_call(kernel, "col_mean", shapes + ([facts.shape] if first else []), own, *got, facts)
+    return small_call(kernel, "col_mean", shapes, own, *got, facts)
 
 
 def joined(me, mate):
@@ -364,18 +360,29 @@
     return small_call(kernel, "joined", [(2 * piece, width)], me, mate)[0]
 
 
-def choose(held, held_mate, p0, p3, p1, p2, facts):
+def choose(held, held_mate, p0, p3, p1, p2, facts, first):
     rows, width = held.shape
     piece = rows // GROUP
 
-    def kernel(held_ref, held_mate_ref, b0, b3, b1, b2, facts_ref, me, mate):
+    def kernel(held_ref, held_mate_ref, b0, b3, b1, b2, facts_ref, me, mate, *maybe_facts):
         f = facts_ref[...]
+        if first:
+            notes = [b[2 * piece :] for b in (b1, b2, b3)]
+            count = sum([row(n, B_ME) for n in notes], row(f, B_ME))
+            count_mate = sum([row(n, B_MATE) for n in notes], row(f, B_MATE))
+            over, over_mate = jnp.maximum(count, 1.0), jnp.maximum(count_mate, 1.0)
+            at = lax.broadcasted_iota(jnp.int32, f.shape, 0)
+            maybe_facts[0][...] = jnp.where(at == B_COUNT, over, jnp.where(at == B_COUNT_MATE, over_mate, f))
         for d, src in enumerate((b0, b1, b2, b3)):
             here = pl.ds(pl.multiple_of((ring_at() + GROUP - d) % GROUP * piece, 8), piece)
-            me[here, :] = jnp.where(row(f, B_ME) > 0, src[:piece], held_ref[here, :])
-            mate[here, :] = jnp.where(row(f, B_MATE) > 0, src[piece:], held_mate_ref[here, :])
-
-    return small_call(kernel, "choose", [(rows, width)] * 2, held, held_mate, p0, p3, p1, p2, facts)
+            mine, theirs = src[:piece], src[piece : 2 * piece]
+            if first:
+                mine, theirs = mine / over, theirs / over_mate
+            me[here, :] = jnp.where(row(f, B_ME) > 0, mine, held_ref[here, :])
+            mate[here, :] = jnp.where(row(f, B_MATE) > 0, theirs, held_mate_ref[here, :])
+
+    shapes = [(rows, width)] * 2 + ([facts.shape] if first else [])
+    return small_call(kernel, "choose", shapes, held, held_mate, p0, p3, p1, p2, facts)
 
 
 def place(size, mine, other, turned, turned_other):
@@ -480,22 +487,22 @@
     far2 = to_far(after(part2, far1))
 
     own0, s2, s1, s3, held0, held_mate0, facts = row_mean(mine0, theirs0, far0, facts, True)
-    total0, facts = col_mean(own0, around(s2, s1, s3), facts, first=True)
+    total0 = col_sum(own0, around(s2, s1, s3), facts)
     p2, p1, p3 = around(total0, total0, total0)
-    me0, mate0 = choose(held0, held_mate0, total0, p3, p1, p2, facts)
+    me0, mate0, counted = choose(held0, held_mate0, total0, p3, p1, p2, facts, True)
     other0 = to_mate(mate0)
 
     own1, s2, s1, s3, held1, held_mate1, _ = row_mean(mine1, theirs1, after(far1, total0), facts, False)
     got1 = around(s2, s1, s3)
-    total1 = col_mean(after(own1, me0), got1, facts)[0]
+    total1 = col_mean(after(own1, me0), got1, counted)[0]
     p2, p1, p3 = around(total1, total1, total1)
-    me1, mate1 = choose(held1, held_mate1, total1, p3, p1, p2, facts)
+    me1, mate1 = choose(held1, held_mate1, total1, p3, p1, p2, facts, False)
     other1 = to_mate(mate1)
 
     own2, s2, s1, s3, held2, held_mate2, _ = row_mean(mine2, theirs2, after(far2, total1), facts, False)
     got2 = around(s2, s1, s3)
     held_mate2 = to_mate(held_mate2)
-    me2, mate2 = col_mean(after(own2, me1), got2, facts, split=True)
+    me2, mate2 = col_mean(after(own2, me1), got2, counted, split=True)
     total2 = joined(me2, to_mate(mate2))
     p2, p1, p3 = around(total2, total2, total2)
     query = place(size, me0, other0, me1, other1)

time: 109 us -> 108 us (level)
  waiting for transfers between devices: 49.3 us -> 47.8 us
    ppermute x3, waiting for transfers between devices: 17.3 us -> 15.7 us  [to_far(): return lax.ppermute(x, 'row', swap(2))]
  transfers between devices with their start and end apart: 28 -> 28, of which waited for: 16 -> 15; matrix products, arithmetic and copies ran while one was open for 0% -> 0% of each run, Pallas kernels for 8% -> 8%
where the time goes in v5:
time: 108 us
  waiting for transfers between devices  47.8 us (44%)
  starting transfers between devices  32.7 us (30%)
  Pallas kernels  26.7 us (25%)
    ppermute x18, waiting for transfers between devices, around(): lax.ppermute(x, 'col', ring(d))  29.6 us
    ppermute x18, starting transfers between devices, around(): lax.ppermute(x, 'col', ring(d))  21.7 us
    pallas_call x1, Pallas kernels, query_step(): pl.pallas_call(query_kernel, grid=(heads // QUAD,), in_specs=[SCALARS, fu...  17.2 us
    ppermute x3, waiting for transfers between devices, to_far(): return lax.ppermute(x, 'row', swap(2))  15.7 us
    ppermute x7, starting transfers between devices, to_mate(): return lax.ppermute(x, 'row', swap(1))  9.57 us
    pallas_call x1, Pallas kernels, key_step(): pl.pallas_call(key_kernel, grid=(heads // QUAD,), in_specs=[STAYS] * 4 +...  6.29 us
    ppermute x7, waiting for transfers between devices, to_mate(): return lax.ppermute(x, 'row', swap(1))  2.52 us
  transfers between devices with their start and end apart: 28, of which 15 were waited for; matrix products, arithmetic and copies ran while one was open for 0% of the time, Pallas kernels for 8%

profile of v5, /device:TPU:1, one launch (start us, length us, event | category | flops | bytes accessed | tf_op | source)
XLA Modules:
  0.0 108.1 jit_solution(8752994818157305923)
XLA Ops:
  0.6 17.2 %query_step.1 = (f32[160,512]{1,0:T(8,128)S(1)}, f32[96,512]{1,0:T(8,128)S(1)}, f32[264,512]{1,0:T(8,128)S(1)}, f32[8,512]{1,0:T(8,128)S(1)}, bf16[8,1024,512]{2...) custom-call(s32[1,1,2]{2,1,0:T(1,128)} %members.1, bf16[1024,512]{1,0:T(8,128)(2,1)} %bitcast.15, ...), custom_call_target="tpu_custom_call" | custom-call | tf_op jit(solution)/shard_map/query_step/pallas_call | solution.py:195
  17.8 3.3 %collective-permute-start = (f32[264,512]{1,0:T(8,128)S(1)}, f32[264,512]{1,0:T(8,128)S(1)}, u32[]{:S(2)}, u32[]{:S(2)}) collective-permute-start(f32[264,512]{1,0:T(8,128)S(1)} %get-tuple-element.53), channel_id=1, source_target_pairs={{0,32},{32,0},{64,96},{96,64},{128,160},{160,128},{192,224},{224,1... | collective-permute-start | bytes 1622024 | tf_op jit(solution)/shard_map/ppermute | solution.py:458
  21.2 1.6 %collective-permute-done.theirs_ref.tq_ref = f32[264,512]{1,0:T(8,128)S(1)} collective-permute-done((f32[264,512]{1,0:T(8,128)S(1)}, f32[264,512]{1,0:T(8,128)S(1)}, u32[]{:S(2)}, u32[]{:S(2)}) %collective-permute-start) | collective-permute-done | bytes 540704 | tf_op jit(solution)/shard_map/ppermute | solution.py:458
  24.1 6.3 %key_step.1 = (f32[160,512]{1,0:T(8,128)S(1)}, f32[192,512]{1,0:T(8,128)S(1)}, f32[64,512]{1,0:T(8,128)S(1)}, f32[192,512]{1,0:T(8,128)S(1)}) custom-call(bf16[8,1024,512]{2,1,0:T(8,128)(2,1)S(1)} %get-tuple-element.67.ds_ref, bf16[1024,512]{1,0:T(8,128)(2,1)S(1)} %get-tuple-element.68.q_ref, bf16[512,1024]{1,0:T(8,128)(2,1)S(1)} %get-tuple-element.69.ft_ref, ...), custom_call_target="tpu_custom_call" | custom-call | tf_op jit(solution)/shard_map/key_step/pallas_call | solution.py:220
  31.2 9.7 %collective-permute-done.1.far_ref = f32[168,512]{1,0:T(8,128)S(1)} collective-permute-done((f32[168,512]{1,0:T(8,128)S(1)}, f32[168,512]{1,0:T(8,128)S(1)}, u32[]{:S(2)}, u32[]{:S(2)}) %collective-permute-start.1) | collective-permute-done | bytes 344096 | tf_op jit(solution)/shard_map/ppermute | solution.py:462
  42.0 2.1 %collective-permute-start.2 = (f32[80,512]{1,0:T(8,128)S(1)}, f32[80,512]{1,0:T(8,128)S(1)}, u32[]{:S(2)}, u32[]{:S(2)}) collective-permute-start(f32[80,512]{1,0:T(8,128)S(1)} %get-tuple-element.60), channel_id=1, source_target_pairs={{0,2},{1,3},{2,0},{3,1},{4,6},{5,7},{6,4},{7,5},{8,10},{9,11},{10,... | collective-permute-start | bytes 491528 | tf_op jit(solution)/shard_map/ppermute | solution.py:466
  44.5 2.3 %collective-permute-start.4 = (f32[80,512]{1,0:T(8,128)S(1)}, f32[80,512]{1,0:T(8,128)S(1)}, u32[]{:S(2)}, u32[]{:S(2)}) collective-permute-start(f32[80,512]{1,0:T(8,128)S(1)} %get-tuple-element.62), channel_id=1, source_target_pairs={{0,3},{1,0},{2,1},{3,2},{4,7},{5,4},{6,5},{7,6},{8,11},{9,8},{10,9... | collective-permute-start | bytes 491528 | tf_op jit(solution)/shard_map/ppermute | solution.py:466
  46.8 2.9 %collective-permute-done.2.g1 = f32[80,512]{1,0:T(8,128)S(1)} collective-permute-done((f32[80,512]{1,0:T(8,128)S(1)}, f32[80,512]{1,0:T(8,128)S(1)}, u32[]{:S(2)}, u32[]{:S(2)}) %collective-permute-start.2) | collective-permute-done | bytes 163872 | tf_op jit(solution)/shard_map/ppermute | solution.py:466
  49.6 3.8 %collective-permute-done.3.g2 = f32[80,512]{1,0:T(8,128)S(1)} collective-permute-done((f32[80,512]{1,0:T(8,128)S(1)}, f32[80,512]{1,0:T(8,128)S(1)}, u32[]{:S(2)}, u32[]{:S(2)}) %collective-permute-start.3) | collective-permute-done | bytes 163872 | tf_op jit(solution)/shard_map/ppermute | solution.py:466
  55.7 3.5 %collective-permute-done.10.far_ref = f32[160,512]{1,0:T(8,128)S(1)} collective-permute-done((f32[160,512]{1,0:T(8,128)S(1)}, f32[160,512]{1,0:T(8,128)S(1)}, u32[]{:S(2)}, u32[]{:S(2)}) %collective-permute-start.10) | collective-permute-done | bytes 327712 | tf_op jit(solution)/shard_map/ppermute | solution.py:462
  62.0 3.6 %collective-permute-done.6.b1 = f32[88,512]{1,0:T(8,128)S(1)} collective-permute-done((f32[88,512]{1,0:T(8,128)S(1)}, f32[88,512]{1,0:T(8,128)S(1)}, u32[]{:S(2)}, u32[]{:S(2)}) %collective-permute-start.6) | collective-permute-done | bytes 180256 | tf_op jit(solution)/shard_map/ppermute | solution.py:466
  65.7 2.1 %collective-permute-done.11.g1 = f32[80,512]{1,0:T(8,128)S(1)} collective-permute-done((f32[80,512]{1,0:T(8,128)S(1)}, f32[80,512]{1,0:T(8,128)S(1)}, u32[]{:S(2)}, u32[]{:S(2)}) %collective-permute-start.11) | collective-permute-done | bytes 163872 | tf_op jit(solution)/shard_map/ppermute | solution.py:466
  67.8 4.5 %collective-permute-done.12.g2 = f32[80,512]{1,0:T(8,128)S(1)} collective-permute-done((f32[80,512]{1,0:T(8,128)S(1)}, f32[80,512]{1,0:T(8,128)S(1)}, u32[]{:S(2)}, u32[]{:S(2)}) %collective-permute-start.12) | collective-permute-done | bytes 163872 | tf_op jit(solution)/shard_map/ppermute | solution.py:466
  72.4 1.5 %collective-permute-start.16 = (f32[80,512]{1,0:T(8,128)S(1)}, f32[80,512]{1,0:T(8,128)S(1)}, u32[]{:S(2)}, u32[]{:S(2)}) collective-permute-start(f32[80,512]{1,0:T(8,128)S(1)} %col_mean.2.b0), channel_id=1, source_target_pairs={{0,2},{1,3},{2,0},{3,1},{4,6},{5,7},{6,4},{7,5},{8,10},{9,11},{10,... | collective-permute-start | bytes 491528 | tf_op jit(solution)/shard_map/ppermute | solution.py:466
  73.9 2.2 %collective-permute-start.15 = (f32[80,512]{1,0:T(8,128)S(1)}, f32[80,512]{1,0:T(8,128)S(1)}, u32[]{:S(2)}, u32[]{:S(2)}) collective-permute-start(f32[80,512]{1,0:T(8,128)S(1)} %col_mean.2.b0), channel_id=1, source_target_pairs={{0,1},{1,2},{2,3},{3,0},{4,5},{5,6},{6,7},{7,4},{8,9},{9,10},{10,1... | collective-permute-start | bytes 491528 | tf_op jit(solution)/shard_map/ppermute | solution.py:466
  76.6 2.4 %collective-permute-done.19.far_ref = f32[192,512]{1,0:T(8,128)S(1)} collective-permute-done((f32[192,512]{1,0:T(8,128)S(1)}, f32[192,512]{1,0:T(8,128)S(1)}, u32[]{:S(2)}, u32[]{:S(2)}) %collective-permute-start.19) | collective-permute-done | bytes 393248 | tf_op jit(solution)/shard_map/ppermute | solution.py:462
  79.2 2.1 %collective-permute-start.21 = (f32[96,512]{1,0:T(8,128)S(1)}, f32[96,512]{1,0:T(8,128)S(1)}, u32[]{:S(2)}, u32[]{:S(2)}) collective-permute-start(f32[96,512]{1,0:T(8,128)S(1)} %get-tuple-element.96), channel_id=1, source_target_pairs={{0,2},{1,3},{2,0},{3,1},{4,6},{5,7},{6,4},{7,5},{8,10},{9,11},{10,... | collective-permute-start | bytes 589832 | tf_op jit(solution)/shard_map/ppermute | solution.py:466
  83.2 1.7 %collective-permute-start.23 = (f32[96,512]{1,0:T(8,128)S(1)}, f32[96,512]{1,0:T(8,128)S(1)}, u32[]{:S(2)}, u32[]{:S(2)}) collective-permute-start(f32[96,512]{1,0:T(8,128)S(1)} %get-tuple-element.98), channel_id=1, source_target_pairs={{0,3},{1,0},{2,1},{3,2},{4,7},{5,4},{6,5},{7,6},{8,11},{9,8},{10,9... | collective-permute-start | bytes 589832 | tf_op jit(solution)/shard_map/ppermute | solution.py:466
  87.1 1.9 %collective-permute-start.17 = (f32[160,512]{1,0:T(8,128)S(1)}, f32[160,512]{1,0:T(8,128)S(1)}, u32[]{:S(2)}, u32[]{:S(2)}) collective-permute-start(f32[160,512]{1,0:T(8,128)S(1)} %get-tuple-element.86), channel_id=1, source_target_pairs={{0,32},{32,0},{64,96},{96,64},{128,160},{160,128},{192,224},{224,1... | collective-permute-start | bytes 983048 | tf_op jit(solution)/shard_map/ppermute | solution.py:458
  89.1 3.0 %collective-permute-done.22.g2 = f32[96,512]{1,0:T(8,128)S(1)} collective-permute-done((f32[96,512]{1,0:T(8,128)S(1)}, f32[96,512]{1,0:T(8,128)S(1)}, u32[]{:S(2)}, u32[]{:S(2)}) %collective-permute-start.22) | collective-permute-done | bytes 196640 | tf_op jit(solution)/shard_map/ppermute | solution.py:466
  94.3 1.5 %collective-permute-start.25 = (f32[96,512]{1,0:T(8,128)S(1)}, f32[96,512]{1,0:T(8,128)S(1)}, u32[]{:S(2)}, u32[]{:S(2)}) collective-permute-start(f32[96,512]{1,0:T(8,128)S(1)} %joined.1.b0), channel_id=1, source_target_pairs={{0,2},{1,3},{2,0},{3,1},{4,6},{5,7},{6,4},{7,5},{8,10},{9,11},{10,... | collective-permute-start | bytes 589832 | tf_op jit(solution)/shard_map/ppermute | solution.py:466
  95.8 1.5 %collective-permute-start.27 = (f32[96,512]{1,0:T(8,128)S(1)}, f32[96,512]{1,0:T(8,128)S(1)}, u32[]{:S(2)}, u32[]{:S(2)}) collective-permute-start(f32[96,512]{1,0:T(8,128)S(1)} %joined.1.b0), channel_id=1, source_target_pairs={{0,1},{1,2},{2,3},{3,0},{4,5},{5,6},{6,7},{7,4},{8,9},{9,10},{10,1... | collective-permute-start | bytes 589832 | tf_op jit(solution)/shard_map/ppermute | solution.py:466
  99.5 2.5 %collective-permute-done.25.b2 = f32[96,512]{1,0:T(8,128)S(1)} collective-permute-done((f32[96,512]{1,0:T(8,128)S(1)}, f32[96,512]{1,0:T(8,128)S(1)}, u32[]{:S(2)}, u32[]{:S(2)}) %collective-permute-start.25) | collective-permute-done | bytes 196640 | tf_op jit(solution)/shard_map/ppermute | solution.py:466
  102.0 4.9 %collective-permute-done.27.b1 = f32[96,512]{1,0:T(8,128)S(1)} collective-permute-done((f32[96,512]{1,0:T(8,128)S(1)}, f32[96,512]{1,0:T(8,128)S(1)}, u32[]{:S(2)}, u32[]{:S(2)}) %collective-permute-start.27) | collective-permute-done | bytes 196640 | tf_op jit(solution)/shard_map/ppermute | solution.py:466
  (48 shorter events, 19.0 us)
Async XLA Ops:
  22.8 18.1 %collective-permute-start.1 = (f32[168,512]{1,0:T(8,128)S(1)}, f32[168,512]{1,0:T(8,128)S(1)}, u32[]{:S(2)}, u32[]{:S(2)}) collective-permute-start(f32[168,512]{1,0:T(8,128)S(1)} %get-tuple-element.55), channel_id=1, source_target_pairs={{0,64},{32,96},{64,0},{96,32},{128,192},{160,224},{192,128},{224,1... | collective-permute-start | bytes 1032200 | tf_op jit(solution)/shard_map/ppermute | solution.py:462
  30.4 11.2 %collective-permute-start.9 = (f32[64,512]{1,0:T(8,128)S(1)}, f32[64,512]{1,0:T(8,128)S(1)}, u32[]{:S(2)}, u32[]{:S(2)}) collective-permute-start(f32[64,512]{1,0:T(8,128)S(1)} %get-tuple-element.72), channel_id=1, source_target_pairs={{0,32},{32,0},{64,96},{96,64},{128,160},{160,128},{192,224},{224,1... | collective-permute-start | bytes 393224 | tf_op jit(solution)/shard_map/ppermute | solution.py:458
  40.9 14.7 %collective-permute-start.18 = (f32[192,512]{1,0:T(8,128)S(1)}, f32[192,512]{1,0:T(8,128)S(1)}, u32[]{:S(2)}, u32[]{:S(2)}) collective-permute-start(f32[192,512]{1,0:T(8,128)S(1)} %get-tuple-element.89), channel_id=1, source_target_pairs={{0,32},{32,0},{64,96},{96,64},{128,160},{160,128},{192,224},{224,1... | collective-permute-start | bytes 1179656 | tf_op jit(solution)/shard_map/ppermute | solution.py:458
  41.7 17.5 %collective-permute-start.10 = (f32[160,512]{1,0:T(8,128)S(1)}, f32[160,512]{1,0:T(8,128)S(1)}, u32[]{:S(2)}, u32[]{:S(2)}) collective-permute-start(f32[160,512]{1,0:T(8,128)S(1)} %get-tuple-element.75), channel_id=1, source_target_pairs={{0,64},{32,96},{64,0},{96,32},{128,192},{160,224},{192,128},{224,1... | collective-permute-start | bytes 983048 | tf_op jit(solution)/shard_map/ppermute | solution.py:462
  42.0 7.6 %collective-permute-start.2 = (f32[80,512]{1,0:T(8,128)S(1)}, f32[80,512]{1,0:T(8,128)S(1)}, u32[]{:S(2)}, u32[]{:S(2)}) collective-permute-start(f32[80,512]{1,0:T(8,128)S(1)} %get-tuple-element.60), channel_id=1, source_target_pairs={{0,2},{1,3},{2,0},{3,1},{4,6},{5,7},{6,4},{7,5},{8,10},{9,11},{10,... | collective-permute-start | bytes 491528 | tf_op jit(solution)/shard_map/ppermute | solution.py:466
  44.1 9.4 %collective-permute-start.3 = (f32[80,512]{1,0:T(8,128)S(1)}, f32[80,512]{1,0:T(8,128)S(1)}, u32[]{:S(2)}, u32[]{:S(2)}) collective-permute-start(f32[80,512]{1,0:T(8,128)S(1)} %get-tuple-element.61), channel_id=1, source_target_pairs={{0,1},{1,2},{2,3},{3,0},{4,5},{5,6},{6,7},{7,4},{8,9},{9,10},{10,1... | collective-permute-start | bytes 491528 | tf_op jit(solution)/shard_map/ppermute | solution.py:466
  44.5 9.0 %collective-permute-start.4 = (f32[80,512]{1,0:T(8,128)S(1)}, f32[80,512]{1,0:T(8,128)S(1)}, u32[]{:S(2)}, u32[]{:S(2)}) collective-permute-start(f32[80,512]{1,0:T(8,128)S(1)} %get-tuple-element.62), channel_id=1, source_target_pairs={{0,3},{1,0},{2,1},{3,2},{4,7},{5,4},{6,5},{7,6},{8,11},{9,8},{10,9... | collective-permute-start | bytes 491528 | tf_op jit(solution)/shard_map/ppermute | solution.py:466
  53.5 7.8 %collective-permute-start.7 = (f32[88,512]{1,0:T(8,128)S(1)}, f32[88,512]{1,0:T(8,128)S(1)}, u32[]{:S(2)}, u32[]{:S(2)}) collective-permute-start(f32[88,512]{1,0:T(8,128)S(1)} %col_sum.1.b0), channel_id=1, source_target_pairs={{0,2},{1,3},{2,0},{3,1},{4,6},{5,7},{6,4},{7,5},{8,10},{9,11},{10,... | collective-permute-start | bytes 540680 | tf_op jit(solution)/shard_map/ppermute | solution.py:466
  54.7 10.9 %collective-permute-start.6 = (f32[88,512]{1,0:T(8,128)S(1)}, f32[88,512]{1,0:T(8,128)S(1)}, u32[]{:S(2)}, u32[]{:S(2)}) collective-permute-start(f32[88,512]{1,0:T(8,128)S(1)} %col_sum.1.b0), channel_id=1, source_target_pairs={{0,1},{1,2},{2,3},{3,0},{4,5},{5,6},{6,7},{7,4},{8,9},{9,10},{10,1... | collective-permute-start | bytes 540680 | tf_op jit(solution)/shard_map/ppermute | solution.py:466
  59.2 19.8 %collective-permute-start.19 = (f32[192,512]{1,0:T(8,128)S(1)}, f32[192,512]{1,0:T(8,128)S(1)}, u32[]{:S(2)}, u32[]{:S(2)}) collective-permute-start(f32[192,512]{1,0:T(8,128)S(1)} %chip_sum_last.1), channel_id=1, source_target_pairs={{0,64},{32,96},{64,0},{96,32},{128,192},{160,224},{192,128},{224,1... | collective-permute-start | bytes 1179656 | tf_op jit(solution)/shard_map/ppermute | solution.py:462
  60.9 7.0 %collective-permute-start.11 = (f32[80,512]{1,0:T(8,128)S(1)}, f32[80,512]{1,0:T(8,128)S(1)}, u32[]{:S(2)}, u32[]{:S(2)}) collective-permute-start(f32[80,512]{1,0:T(8,128)S(1)} %get-tuple-element.81), channel_id=1, source_target_pairs={{0,2},{1,3},{2,0},{3,1},{4,6},{5,7},{6,4},{7,5},{8,10},{9,11},{10,... | collective-permute-start | bytes 491528 | tf_op jit(solution)/shard_map/ppermute | solution.py:466
  61.3 11.0 %collective-permute-start.12 = (f32[80,512]{1,0:T(8,128)S(1)}, f32[80,512]{1,0:T(8,128)S(1)}, u32[]{:S(2)}, u32[]{:S(2)}) collective-permute-start(f32[80,512]{1,0:T(8,128)S(1)} %get-tuple-element.82), channel_id=1, source_target_pairs={{0,1},{1,2},{2,3},{3,0},{4,5},{5,6},{6,7},{7,4},{8,9},{9,10},{10,1... | collective-permute-start | bytes 491528 | tf_op jit(solution)/shard_map/ppermute | solution.py:466
  72.4 9.8 %collective-permute-start.16 = (f32[80,512]{1,0:T(8,128)S(1)}, f32[80,512]{1,0:T(8,128)S(1)}, u32[]{:S(2)}, u32[]{:S(2)}) collective-permute-start(f32[80,512]{1,0:T(8,128)S(1)} %col_mean.2.b0), channel_id=1, source_target_pairs={{0,2},{1,3},{2,0},{3,1},{4,6},{5,7},{6,4},{7,5},{8,10},{9,11},{10,... | collective-permute-start | bytes 491528 | tf_op jit(solution)/shard_map/ppermute | solution.py:466
  73.9 9.3 %collective-permute-start.15 = (f32[80,512]{1,0:T(8,128)S(1)}, f32[80,512]{1,0:T(8,128)S(1)}, u32[]{:S(2)}, u32[]{:S(2)}) collective-permute-start(f32[80,512]{1,0:T(8,128)S(1)} %col_mean.2.b0), channel_id=1, source_target_pairs={{0,1},{1,2},{2,3},{3,0},{4,5},{5,6},{6,7},{7,4},{8,9},{9,10},{10,1... | collective-permute-start | bytes 491528 | tf_op jit(solution)/shard_map/ppermute | solution.py:466
  76.1 8.8 %collective-permute-start.14 = (f32[80,512]{1,0:T(8,128)S(1)}, f32[80,512]{1,0:T(8,128)S(1)}, u32[]{:S(2)}, u32[]{:S(2)}) collective-permute-start(f32[80,512]{1,0:T(8,128)S(1)} %col_mean.2.b0), channel_id=1, source_target_pairs={{0,3},{1,0},{2,1},{3,2},{4,7},{5,4},{6,5},{7,6},{8,11},{9,8},{10,9... | collective-permute-start | bytes 491528 | tf_op jit(solution)/shard_map/ppermute | solution.py:466
  79.2 7.9 %collective-permute-start.21 = (f32[96,512]{1,0:T(8,128)S(1)}, f32[96,512]{1,0:T(8,128)S(1)}, u32[]{:S(2)}, u32[]{:S(2)}) collective-permute-start(f32[96,512]{1,0:T(8,128)S(1)} %get-tuple-element.96), channel_id=1, source_target_pairs={{0,2},{1,3},{2,0},{3,1},{4,6},{5,7},{6,4},{7,5},{8,10},{9,11},{10,... | collective-permute-start | bytes 589832 | tf_op jit(solution)/shard_map/ppermute | solution.py:466
  81.4 15.9 %collective-permute-start.8 = (f32[160,512]{1,0:T(8,128)S(1)}, f32[160,512]{1,0:T(8,128)S(1)}, u32[]{:S(2)}, u32[]{:S(2)}) collective-permute-start(f32[160,512]{1,0:T(8,128)S(1)} %get-tuple-element.65), channel_id=1, source_target_pairs={{0,32},{32,0},{64,96},{96,64},{128,160},{160,128},{192,224},{224,1... | collective-permute-start | bytes 983048 | tf_op jit(solution)/shard_map/ppermute | solution.py:458
  82.2 9.9 %collective-permute-start.22 = (f32[96,512]{1,0:T(8,128)S(1)}, f32[96,512]{1,0:T(8,128)S(1)}, u32[]{:S(2)}, u32[]{:S(2)}) collective-permute-start(f32[96,512]{1,0:T(8,128)S(1)} %get-tuple-element.97), channel_id=1, source_target_pairs={{0,1},{1,2},{2,3},{3,0},{4,5},{5,6},{6,7},{7,4},{8,9},{9,10},{10,1... | collective-permute-start | bytes 589832 | tf_op jit(solution)/shard_map/ppermute | solution.py:466
  83.2 8.9 %collective-permute-start.23 = (f32[96,512]{1,0:T(8,128)S(1)}, f32[96,512]{1,0:T(8,128)S(1)}, u32[]{:S(2)}, u32[]{:S(2)}) collective-permute-start(f32[96,512]{1,0:T(8,128)S(1)} %get-tuple-element.98), channel_id=1, source_target_pairs={{0,3},{1,0},{2,1},{3,2},{4,7},{5,4},{6,5},{7,6},{8,11},{9,8},{10,9... | collective-permute-start | bytes 589832 | tf_op jit(solution)/shard_map/ppermute | solution.py:466
  84.8 17.2 %collective-permute-start.20 = (f32[192,512]{1,0:T(8,128)S(1)}, f32[192,512]{1,0:T(8,128)S(1)}, u32[]{:S(2)}, u32[]{:S(2)}) collective-permute-start(f32[192,512]{1,0:T(8,128)S(1)} %get-tuple-element.93), channel_id=1, source_target_pairs={{0,32},{32,0},{64,96},{96,64},{128,160},{160,128},{192,224},{224,1... | collective-permute-start | bytes 1179656 | tf_op jit(solution)/shard_map/ppermute | solution.py:458
  87.1 11.4 %collective-permute-start.17 = (f32[160,512]{1,0:T(8,128)S(1)}, f32[160,512]{1,0:T(8,128)S(1)}, u32[]{:S(2)}, u32[]{:S(2)}) collective-permute-start(f32[160,512]{1,0:T(8,128)S(1)} %get-tuple-element.86), channel_id=1, source_target_pairs={{0,32},{32,0},{64,96},{96,64},{128,160},{160,128},{192,224},{224,1... | collective-permute-start | bytes 983048 | tf_op jit(solution)/shard_map/ppermute | solution.py:458
  94.3 7.8 %collective-permute-start.25 = (f32[96,512]{1,0:T(8,128)S(1)}, f32[96,512]{1,0:T(8,128)S(1)}, u32[]{:S(2)}, u32[]{:S(2)}) collective-permute-start(f32[96,512]{1,0:T(8,128)S(1)} %joined.1.b0), channel_id=1, source_target_pairs={{0,2},{1,3},{2,0},{3,1},{4,6},{5,7},{6,4},{7,5},{8,10},{9,11},{10,... | collective-permute-start | bytes 589832 | tf_op jit(solution)/shard_map/ppermute | solution.py:466
  95.8 11.1 %collective-permute-start.27 = (f32[96,512]{1,0:T(8,128)S(1)}, f32[96,512]{1,0:T(8,128)S(1)}, u32[]{:S(2)}, u32[]{:S(2)}) collective-permute-start(f32[96,512]{1,0:T(8,128)S(1)} %joined.1.b0), channel_id=1, source_target_pairs={{0,1},{1,2},{2,3},{3,0},{4,5},{5,6},{6,7},{7,4},{8,9},{9,10},{10,1... | collective-permute-start | bytes 589832 | tf_op jit(solution)/shard_map/ppermute | solution.py:466
  97.3 9.6 %collective-permute-start.26 = (f32[96,512]{1,0:T(8,128)S(1)}, f32[96,512]{1,0:T(8,128)S(1)}, u32[]{:S(2)}, u32[]{:S(2)}) collective-permute-start(f32[96,512]{1,0:T(8,128)S(1)} %joined.1.b0), channel_id=1, source_target_pairs={{0,3},{1,0},{2,1},{3,2},{4,7},{5,4},{6,5},{7,6},{8,11},{9,8},{10,9... | collective-permute-start | bytes 589832 | tf_op jit(solution)/shard_map/ppermute | solution.py:466
  (4 other events, 20.1 us)

commit v6 on v5

--- a/solution.py
+++ b/solution.py
@@ -66,7 +66,7 @@
 
 def query_kernel(
     members, f_ref, v_ref, o_ref, wq_ref, wk_ref, m_ref, s_ref,
-    mine_ref, turn_ref, other_ref, facts_ref, ds_ref, q_ref, ft_ref, ks, kt, gqt, u_all, w_all, norms,
+    mine_ref, turn_ref, other_ref, facts_ref, ds_ref, q_ref, ft_ref, ks, kt, gqt, u_all, w_all, norms, qt, ot,
 ):
     step = pl.program_id(0)
     last = pl.num_programs(0) - 1
@@ -89,13 +89,16 @@
     kt[...] = keys.T
     units = [(s, head) for s in range(tokens // SEQ) for head in range(0, QUAD, HD)]
 
+    qt[...] = queries.T
+    ot[...] = (o_ref[...] * (1.0 / math.sqrt(HD))).astype(bf16).T
+    none = jnp.zeros((HD, SEQ), bf16)
+
     def products(s, head):
         rows = slice(s * SEQ, (s + 1) * SEQ)
         lanes = slice(head // PAIR * PAIR, head // PAIR * PAIR + PAIR)
-        h = head % PAIR // HD
-        o_head = only_head(o_ref[rows, lanes], h) * (1.0 / math.sqrt(HD))
-        scores = dot(ks[rows, lanes], only_head(queries[rows, lanes], h), 1, 1)
-        return scores, dot(v_ref[rows, lanes], o_head.astype(bf16), 1, 1)
+        wide = lambda x: jnp.concatenate([none, x] if head % PAIR else [x, none])
+        scores = dot(ks[rows, lanes], wide(qt[head : head + HD, rows]))
+        return scores, dot(v_ref[rows, lanes], wide(ot[head : head + HD, rows]))
 
     ready = products(*units[0])
     for i, (s, head) in enumerate(units):
@@ -206,6 +209,8 @@
             pltpu.VMEM((width, heads), f32),
             pltpu.VMEM((width, heads), f32),
             pltpu.SMEM((2,), f32),
+            pltpu.VMEM((QUAD, tokens), bf16),
+            pltpu.VMEM((QUAD, tokens), bf16),
         ],
         compiler_params=pltpu.CompilerParams(vmem_limit_bytes=36 << 20),
         name="query_step",

time: 108 us -> 108 us (level)
  no operation moved by 1% of the time
where the time goes in v6:
time: 108 us
  waiting for transfers between devices  47.8 us (44%)
  starting transfers between devices  32.7 us (30%)
  Pallas kernels  26.2 us (24%)
    ppermute x18, waiting for transfers between devices, around(): lax.ppermute(x, 'col', ring(d))  29.6 us
    ppermute x18, starting transfers between devices, around(): lax.ppermute(x, 'col', ring(d))  21.7 us
    pallas_call x1, Pallas kernels, query_step(): pl.pallas_call(query_kernel, grid=(heads // QUAD,), in_specs=[SCALARS, fu...  16.7 us
    ppermute x3, waiting for transfers between devices, to_far(): return lax.ppermute(x, 'row', swap(2))  15.7 us
    ppermute x7, starting transfers between devices, to_mate(): return lax.ppermute(x, 'row', swap(1))  9.56 us
    pallas_call x1, Pallas kernels, key_step(): pl.pallas_call(key_kernel, grid=(heads // QUAD,), in_specs=[STAYS] * 4 +...  6.29 us
    ppermute x7, waiting for transfers between devices, to_mate(): return lax.ppermute(x, 'row', swap(1))  2.52 us
  transfers between devices with their start and end apart: 28, of which 15 were waited for; matrix products, arithmetic and copies ran while one was open for 0% of the time, Pallas kernels for 8%

profile of v6, /device:TPU:1, one launch (start us, length us, event | category | flops | bytes accessed | tf_op | source)
XLA Modules:
  0.0 107.7 jit_solution(10219299467835180928)
XLA Ops:
  0.6 16.7 %query_step.1 = (f32[160,512]{1,0:T(8,128)S(1)}, f32[96,512]{1,0:T(8,128)S(1)}, f32[264,512]{1,0:T(8,128)S(1)}, f32[8,512]{1,0:T(8,128)S(1)}, bf16[8,1024,512]{2...) custom-call(s32[1,1,2]{2,1,0:T(1,128)} %members.1, bf16[1024,512]{1,0:T(8,128)(2,1)} %bitcast.15, ...), custom_call_target="tpu_custom_call" | custom-call | tf_op jit(solution)/shard_map/query_step/pallas_call | solution.py:198
  17.4 3.3 %collective-permute-start = (f32[264,512]{1,0:T(8,128)S(1)}, f32[264,512]{1,0:T(8,128)S(1)}, u32[]{:S(2)}, u32[]{:S(2)}) collective-permute-start(f32[264,512]{1,0:T(8,128)S(1)} %get-tuple-element.53), channel_id=1, source_target_pairs={{0,32},{32,0},{64,96},{96,64},{128,160},{160,128},{192,224},{224,1... | collective-permute-start | bytes 1622024 | tf_op jit(solution)/shard_map/ppermute | solution.py:463
  20.7 1.6 %collective-permute-done.theirs_ref.tq_ref = f32[264,512]{1,0:T(8,128)S(1)} collective-permute-done((f32[264,512]{1,0:T(8,128)S(1)}, f32[264,512]{1,0:T(8,128)S(1)}, u32[]{:S(2)}, u32[]{:S(2)}) %collective-permute-start) | collective-permute-done | bytes 540704 | tf_op jit(solution)/shard_map/ppermute | solution.py:463
  23.6 6.3 %key_step.1 = (f32[160,512]{1,0:T(8,128)S(1)}, f32[192,512]{1,0:T(8,128)S(1)}, f32[64,512]{1,0:T(8,128)S(1)}, f32[192,512]{1,0:T(8,128)S(1)}) custom-call(bf16[8,1024,512]{2,1,0:T(8,128)(2,1)S(1)} %get-tuple-element.67.ds_ref, bf16[1024,512]{1,0:T(8,128)(2,1)S(1)} %get-tuple-element.68.q_ref, bf16[512,1024]{1,0:T(8,128)(2,1)S(1)} %get-tuple-element.69.ft_ref, ...), custom_call_target="tpu_custom_call" | custom-call | tf_op jit(solution)/shard_map/key_step/pallas_call | solution.py:225
  30.7 9.7 %collective-permute-done.1.far_ref = f32[168,512]{1,0:T(8,128)S(1)} collective-permute-done((f32[168,512]{1,0:T(8,128)S(1)}, f32[168,512]{1,0:T(8,128)S(1)}, u32[]{:S(2)}, u32[]{:S(2)}) %collective-permute-start.1) | collective-permute-done | bytes 344096 | tf_op jit(solution)/shard_map/ppermute | solution.py:467
  41.6 2.1 %collective-permute-start.2 = (f32[80,512]{1,0:T(8,128)S(1)}, f32[80,512]{1,0:T(8,128)S(1)}, u32[]{:S(2)}, u32[]{:S(2)}) collective-permute-start(f32[80,512]{1,0:T(8,128)S(1)} %get-tuple-element.60), channel_id=1, source_target_pairs={{0,2},{1,3},{2,0},{3,1},{4,6},{5,7},{6,4},{7,5},{8,10},{9,11},{10,... | collective-permute-start | bytes 491528 | tf_op jit(solution)/shard_map/ppermute | solution.py:471
  44.0 2.3 %collective-permute-start.4 = (f32[80,512]{1,0:T(8,128)S(1)}, f32[80,512]{1,0:T(8,128)S(1)}, u32[]{:S(2)}, u32[]{:S(2)}) collective-permute-start(f32[80,512]{1,0:T(8,128)S(1)} %get-tuple-element.62), channel_id=1, source_target_pairs={{0,3},{1,0},{2,1},{3,2},{4,7},{5,4},{6,5},{7,6},{8,11},{9,8},{10,9... | collective-permute-start | bytes 491528 | tf_op jit(solution)/shard_map/ppermute | solution.py:471
  46.3 2.9 %collective-permute-done.2.g1 = f32[80,512]{1,0:T(8,128)S(1)} collective-permute-done((f32[80,512]{1,0:T(8,128)S(1)}, f32[80,512]{1,0:T(8,128)S(1)}, u32[]{:S(2)}, u32[]{:S(2)}) %collective-permute-start.2) | collective-permute-done | bytes 163872 | tf_op jit(solution)/shard_map/ppermute | solution.py:471
  49.2 3.8 %collective-permute-done.3.g2 = f32[80,512]{1,0:T(8,128)S(1)} collective-permute-done((f32[80,512]{1,0:T(8,128)S(1)}, f32[80,512]{1,0:T(8,128)S(1)}, u32[]{:S(2)}, u32[]{:S(2)}) %collective-permute-start.3) | collective-permute-done | bytes 163872 | tf_op jit(solution)/shard_map/ppermute | solution.py:471
  55.2 3.5 %collective-permute-done.10.far_ref = f32[160,512]{1,0:T(8,128)S(1)} collective-permute-done((f32[160,512]{1,0:T(8,128)S(1)}, f32[160,512]{1,0:T(8,128)S(1)}, u32[]{:S(2)}, u32[]{:S(2)}) %collective-permute-start.10) | collective-permute-done | bytes 327712 | tf_op jit(solution)/shard_map/ppermute | solution.py:467
  61.6 3.6 %collective-permute-done.6.b1 = f32[88,512]{1,0:T(8,128)S(1)} collective-permute-done((f32[88,512]{1,0:T(8,128)S(1)}, f32[88,512]{1,0:T(8,128)S(1)}, u32[]{:S(2)}, u32[]{:S(2)}) %collective-permute-start.6) | collective-permute-done | bytes 180256 | tf_op jit(solution)/shard_map/ppermute | solution.py:471
  65.2 2.1 %collective-permute-done.11.g1 = f32[80,512]{1,0:T(8,128)S(1)} collective-permute-done((f32[80,512]{1,0:T(8,128)S(1)}, f32[80,512]{1,0:T(8,128)S(1)}, u32[]{:S(2)}, u32[]{:S(2)}) %collective-permute-start.11) | collective-permute-done | bytes 163872 | tf_op jit(solution)/shard_map/ppermute | solution.py:471
  67.4 4.5 %collective-permute-done.12.g2 = f32[80,512]{1,0:T(8,128)S(1)} collective-permute-done((f32[80,512]{1,0:T(8,128)S(1)}, f32[80,512]{1,0:T(8,128)S(1)}, u32[]{:S(2)}, u32[]{:S(2)}) %collective-permute-start.12) | collective-permute-done | bytes 163872 | tf_op jit(solution)/shard_map/ppermute | solution.py:471
  71.9 1.5 %collective-permute-start.16 = (f32[80,512]{1,0:T(8,128)S(1)}, f32[80,512]{1,0:T(8,128)S(1)}, u32[]{:S(2)}, u32[]{:S(2)}) collective-permute-start(f32[80,512]{1,0:T(8,128)S(1)} %col_mean.2.b0), channel_id=1, source_target_pairs={{0,2},{1,3},{2,0},{3,1},{4,6},{5,7},{6,4},{7,5},{8,10},{9,11},{10,... | collective-permute-start | bytes 491528 | tf_op jit(solution)/shard_map/ppermute | solution.py:471
  73.4 2.1 %collective-permute-start.15 = (f32[80,512]{1,0:T(8,128)S(1)}, f32[80,512]{1,0:T(8,128)S(1)}, u32[]{:S(2)}, u32[]{:S(2)}) collective-permute-start(f32[80,512]{1,0:T(8,128)S(1)} %col_mean.2.b0), channel_id=1, source_target_pairs={{0,1},{1,2},{2,3},{3,0},{4,5},{5,6},{6,7},{7,4},{8,9},{9,10},{10,1... | collective-permute-start | bytes 491528 | tf_op jit(solution)/shard_map/ppermute | solution.py:471
  76.1 2.4 %collective-permute-done.19.far_ref = f32[192,512]{1,0:T(8,128)S(1)} collective-permute-done((f32[192,512]{1,0:T(8,128)S(1)}, f32[192,512]{1,0:T(8,128)S(1)}, u32[]{:S(2)}, u32[]{:S(2)}) %collective-permute-start.19) | collective-permute-done | bytes 393248 | tf_op jit(solution)/shard_map/ppermute | solution.py:467
  78.8 2.1 %collective-permute-start.21 = (f32[96,512]{1,0:T(8,128)S(1)}, f32[96,512]{1,0:T(8,128)S(1)}, u32[]{:S(2)}, u32[]{:S(2)}) collective-permute-start(f32[96,512]{1,0:T(8,128)S(1)} %get-tuple-element.96), channel_id=1, source_target_pairs={{0,2},{1,3},{2,0},{3,1},{4,6},{5,7},{6,4},{7,5},{8,10},{9,11},{10,... | collective-permute-start | bytes 589832 | tf_op jit(solution)/shard_map/ppermute | solution.py:471
  82.7 1.6 %collective-permute-start.23 = (f32[96,512]{1,0:T(8,128)S(1)}, f32[96,512]{1,0:T(8,128)S(1)}, u32[]{:S(2)}, u32[]{:S(2)}) collective-permute-start(f32[96,512]{1,0:T(8,128)S(1)} %get-tuple-element.98), channel_id=1, source_target_pairs={{0,3},{1,0},{2,1},{3,2},{4,7},{5,4},{6,5},{7,6},{8,11},{9,8},{10,9... | collective-permute-start | bytes 589832 | tf_op jit(solution)/shard_map/ppermute | solution.py:471
  86.7 1.9 %collective-permute-start.17 = (f32[160,512]{1,0:T(8,128)S(1)}, f32[160,512]{1,0:T(8,128)S(1)}, u32[]{:S(2)}, u32[]{:S(2)}) collective-permute-start(f32[160,512]{1,0:T(8,128)S(1)} %get-tuple-element.86), channel_id=1, source_target_pairs={{0,32},{32,0},{64,96},{96,64},{128,160},{160,128},{192,224},{224,1... | collective-permute-start | bytes 983048 | tf_op jit(solution)/shard_map/ppermute | solution.py:463
  88.6 3.0 %collective-permute-done.22.g2 = f32[96,512]{1,0:T(8,128)S(1)} collective-permute-done((f32[96,512]{1,0:T(8,128)S(1)}, f32[96,512]{1,0:T(8,128)S(1)}, u32[]{:S(2)}, u32[]{:S(2)}) %collective-permute-start.22) | collective-permute-done | bytes 196640 | tf_op jit(solution)/shard_map/ppermute | solution.py:471
  93.8 1.6 %collective-permute-start.25 = (f32[96,512]{1,0:T(8,128)S(1)}, f32[96,512]{1,0:T(8,128)S(1)}, u32[]{:S(2)}, u32[]{:S(2)}) collective-permute-start(f32[96,512]{1,0:T(8,128)S(1)} %joined.1.b0), channel_id=1, source_target_pairs={{0,2},{1,3},{2,0},{3,1},{4,6},{5,7},{6,4},{7,5},{8,10},{9,11},{10,... | collective-permute-start | bytes 589832 | tf_op jit(solution)/shard_map/ppermute | solution.py:471
  95.3 1.5 %collective-permute-start.27 = (f32[96,512]{1,0:T(8,128)S(1)}, f32[96,512]{1,0:T(8,128)S(1)}, u32[]{:S(2)}, u32[]{:S(2)}) collective-permute-start(f32[96,512]{1,0:T(8,128)S(1)} %joined.1.b0), channel_id=1, source_target_pairs={{0,1},{1,2},{2,3},{3,0},{4,5},{5,6},{6,7},{7,4},{8,9},{9,10},{10,1... | collective-permute-start | bytes 589832 | tf_op jit(solution)/shard_map/ppermute | solution.py:471
  99.0 2.5 %collective-permute-done.25.b2 = f32[96,512]{1,0:T(8,128)S(1)} collective-permute-done((f32[96,512]{1,0:T(8,128)S(1)}, f32[96,512]{1,0:T(8,128)S(1)}, u32[]{:S(2)}, u32[]{:S(2)}) %collective-permute-start.25) | collective-permute-done | bytes 196640 | tf_op jit(solution)/shard_map/ppermute | solution.py:471
  101.6 4.9 %collective-permute-done.27.b1 = f32[96,512]{1,0:T(8,128)S(1)} collective-permute-done((f32[96,512]{1,0:T(8,128)S(1)}, f32[96,512]{1,0:T(8,128)S(1)}, u32[]{:S(2)}, u32[]{:S(2)}) %collective-permute-start.27) | collective-permute-done | bytes 196640 | tf_op jit(solution)/shard_map/ppermute | solution.py:471
  (48 shorter events, 19.1 us)
Async XLA Ops:
  22.3 18.1 %collective-permute-start.1 = (f32[168,512]{1,0:T(8,128)S(1)}, f32[168,512]{1,0:T(8,128)S(1)}, u32[]{:S(2)}, u32[]{:S(2)}) collective-permute-start(f32[168,512]{1,0:T(8,128)S(1)} %get-tuple-element.55), channel_id=1, source_target_pairs={{0,64},{32,96},{64,0},{96,32},{128,192},{160,224},{192,128},{224,1... | collective-permute-start | bytes 1032200 | tf_op jit(solution)/shard_map/ppermute | solution.py:467
  29.9 11.2 %collective-permute-start.9 = (f32[64,512]{1,0:T(8,128)S(1)}, f32[64,512]{1,0:T(8,128)S(1)}, u32[]{:S(2)}, u32[]{:S(2)}) collective-permute-start(f32[64,512]{1,0:T(8,128)S(1)} %get-tuple-element.72), channel_id=1, source_target_pairs={{0,32},{32,0},{64,96},{96,64},{128,160},{160,128},{192,224},{224,1... | collective-permute-start | bytes 393224 | tf_op jit(solution)/shard_map/ppermute | solution.py:463
  40.4 14.7 %collective-permute-start.18 = (f32[192,512]{1,0:T(8,128)S(1)}, f32[192,512]{1,0:T(8,128)S(1)}, u32[]{:S(2)}, u32[]{:S(2)}) collective-permute-start(f32[192,512]{1,0:T(8,128)S(1)} %get-tuple-element.89), channel_id=1, source_target_pairs={{0,32},{32,0},{64,96},{96,64},{128,160},{160,128},{192,224},{224,1... | collective-permute-start | bytes 1179656 | tf_op jit(solution)/shard_map/ppermute | solution.py:463
  41.2 17.5 %collective-permute-start.10 = (f32[160,512]{1,0:T(8,128)S(1)}, f32[160,512]{1,0:T(8,128)S(1)}, u32[]{:S(2)}, u32[]{:S(2)}) collective-permute-start(f32[160,512]{1,0:T(8,128)S(1)} %get-tuple-element.75), channel_id=1, source_target_pairs={{0,64},{32,96},{64,0},{96,32},{128,192},{160,224},{192,128},{224,1... | collective-permute-start | bytes 983048 | tf_op jit(solution)/shard_map/ppermute | solution.py:467
  41.6 7.6 %collective-permute-start.2 = (f32[80,512]{1,0:T(8,128)S(1)}, f32[80,512]{1,0:T(8,128)S(1)}, u32[]{:S(2)}, u32[]{:S(2)}) collective-permute-start(f32[80,512]{1,0:T(8,128)S(1)} %get-tuple-element.60), channel_id=1, source_target_pairs={{0,2},{1,3},{2,0},{3,1},{4,6},{5,7},{6,4},{7,5},{8,10},{9,11},{10,... | collective-permute-start | bytes 491528 | tf_op jit(solution)/shard_map/ppermute | solution.py:471
  43.6 9.4 %collective-permute-start.3 = (f32[80,512]{1,0:T(8,128)S(1)}, f32[80,512]{1,0:T(8,128)S(1)}, u32[]{:S(2)}, u32[]{:S(2)}) collective-permute-start(f32[80,512]{1,0:T(8,128)S(1)} %get-tuple-element.61), channel_id=1, source_target_pairs={{0,1},{1,2},{2,3},{3,0},{4,5},{5,6},{6,7},{7,4},{8,9},{9,10},{10,1... | collective-permute-start | bytes 491528 | tf_op jit(solution)/shard_map/ppermute | solution.py:471
  44.0 9.0 %collective-permute-start.4 = (f32[80,512]{1,0:T(8,128)S(1)}, f32[80,512]{1,0:T(8,128)S(1)}, u32[]{:S(2)}, u32[]{:S(2)}) collective-permute-start(f32[80,512]{1,0:T(8,128)S(1)} %get-tuple-element.62), channel_id=1, source_target_pairs={{0,3},{1,0},{2,1},{3,2},{4,7},{5,4},{6,5},{7,6},{8,11},{9,8},{10,9... | collective-permute-start | bytes 491528 | tf_op jit(solution)/shard_map/ppermute | solution.py:471
  53.0 7.8 %collective-permute-start.7 = (f32[88,512]{1,0:T(8,128)S(1)}, f32[88,512]{1,0:T(8,128)S(1)}, u32[]{:S(2)}, u32[]{:S(2)}) collective-permute-start(f32[88,512]{1,0:T(8,128)S(1)} %col_sum.1.b0), channel_id=1, source_target_pairs={{0,2},{1,3},{2,0},{3,1},{4,6},{5,7},{6,4},{7,5},{8,10},{9,11},{10,... | collective-permute-start | bytes 540680 | tf_op jit(solution)/shard_map/ppermute | solution.py:471
  54.2 10.9 %collective-permute-start.6 = (f32[88,512]{1,0:T(8,128)S(1)}, f32[88,512]{1,0:T(8,128)S(1)}, u32[]{:S(2)}, u32[]{:S(2)}) collective-permute-start(f32[88,512]{1,0:T(8,128)S(1)} %col_sum.1.b0), channel_id=1, source_target_pairs={{0,1},{1,2},{2,3},{3,0},{4,5},{5,6},{6,7},{7,4},{8,9},{9,10},{10,1... | collective-permute-start | bytes 540680 | tf_op jit(solution)/shard_map/ppermute | solution.py:471
  58.7 19.8 %collective-permute-start.19 = (f32[192,512]{1,0:T(8,128)S(1)}, f32[192,512]{1,0:T(8,128)S(1)}, u32[]{:S(2)}, u32[]{:S(2)}) collective-permute-start(f32[192,512]{1,0:T(8,128)S(1)} %chip_sum_last.1), channel_id=1, source_target_pairs={{0,64},{32,96},{64,0},{96,32},{128,192},{160,224},{192,128},{224,1... | collective-permute-start | bytes 1179656 | tf_op jit(solution)/shard_map/ppermute | solution.py:467
  60.4 7.0 %collective-permute-start.11 = (f32[80,512]{1,0:T(8,128)S(1)}, f32[80,512]{1,0:T(8,128)S(1)}, u32[]{:S(2)}, u32[]{:S(2)}) collective-permute-start(f32[80,512]{1,0:T(8,128)S(1)} %get-tuple-element.81), channel_id=1, source_target_pairs={{0,2},{1,3},{2,0},{3,1},{4,6},{5,7},{6,4},{7,5},{8,10},{9,11},{10,... | collective-permute-start | bytes 491528 | tf_op jit(solution)/shard_map/ppermute | solution.py:471
  60.9 11.0 %collective-permute-start.12 = (f32[80,512]{1,0:T(8,128)S(1)}, f32[80,512]{1,0:T(8,128)S(1)}, u32[]{:S(2)}, u32[]{:S(2)}) collective-permute-start(f32[80,512]{1,0:T(8,128)S(1)} %get-tuple-element.82), channel_id=1, source_target_pairs={{0,1},{1,2},{2,3},{3,0},{4,5},{5,6},{6,7},{7,4},{8,9},{9,10},{10,1... | collective-permute-start | bytes 491528 | tf_op jit(solution)/shard_map/ppermute | solution.py:471
  71.9 9.8 %collective-permute-start.16 = (f32[80,512]{1,0:T(8,128)S(1)}, f32[80,512]{1,0:T(8,128)S(1)}, u32[]{:S(2)}, u32[]{:S(2)}) collective-permute-start(f32[80,512]{1,0:T(8,128)S(1)} %col_mean.2.b0), channel_id=1, source_target_pairs={{0,2},{1,3},{2,0},{3,1},{4,6},{5,7},{6,4},{7,5},{8,10},{9,11},{10,... | collective-permute-start | bytes 491528 | tf_op jit(solution)/shard_map/ppermute | solution.py:471
  73.4 9.3 %collective-permute-start.15 = (f32[80,512]{1,0:T(8,128)S(1)}, f32[80,512]{1,0:T(8,128)S(1)}, u32[]{:S(2)}, u32[]{:S(2)}) collective-permute-start(f32[80,512]{1,0:T(8,128)S(1)} %col_mean.2.b0), channel_id=1, source_target_pairs={{0,1},{1,2},{2,3},{3,0},{4,5},{5,6},{6,7},{7,4},{8,9},{9,10},{10,1... | collective-permute-start | bytes 491528 | tf_op jit(solution)/shard_map/ppermute | solution.py:471
  75.6 8.8 %collective-permute-start.14 = (f32[80,512]{1,0:T(8,128)S(1)}, f32[80,512]{1,0:T(8,128)S(1)}, u32[]{:S(2)}, u32[]{:S(2)}) collective-permute-start(f32[80,512]{1,0:T(8,128)S(1)} %col_mean.2.b0), channel_id=1, source_target_pairs={{0,3},{1,0},{2,1},{3,2},{4,7},{5,4},{6,5},{7,6},{8,11},{9,8},{10,9... | collective-permute-start | bytes 491528 | tf_op jit(solution)/shard_map/ppermute | solution.py:471
  78.8 7.9 %collective-permute-start.21 = (f32[96,512]{1,0:T(8,128)S(1)}, f32[96,512]{1,0:T(8,128)S(1)}, u32[]{:S(2)}, u32[]{:S(2)}) collective-permute-start(f32[96,512]{1,0:T(8,128)S(1)} %get-tuple-element.96), channel_id=1, source_target_pairs={{0,2},{1,3},{2,0},{3,1},{4,6},{5,7},{6,4},{7,5},{8,10},{9,11},{10,... | collective-permute-start | bytes 589832 | tf_op jit(solution)/shard_map/ppermute | solution.py:471
  80.9 15.9 %collective-permute-start.8 = (f32[160,512]{1,0:T(8,128)S(1)}, f32[160,512]{1,0:T(8,128)S(1)}, u32[]{:S(2)}, u32[]{:S(2)}) collective-permute-start(f32[160,512]{1,0:T(8,128)S(1)} %get-tuple-element.65), channel_id=1, source_target_pairs={{0,32},{32,0},{64,96},{96,64},{128,160},{160,128},{192,224},{224,1... | collective-permute-start | bytes 983048 | tf_op jit(solution)/shard_map/ppermute | solution.py:463
  81.7 9.9 %collective-permute-start.22 = (f32[96,512]{1,0:T(8,128)S(1)}, f32[96,512]{1,0:T(8,128)S(1)}, u32[]{:S(2)}, u32[]{:S(2)}) collective-permute-start(f32[96,512]{1,0:T(8,128)S(1)} %get-tuple-element.97), channel_id=1, source_target_pairs={{0,1},{1,2},{2,3},{3,0},{4,5},{5,6},{6,7},{7,4},{8,9},{9,10},{10,1... | collective-permute-start | bytes 589832 | tf_op jit(solution)/shard_map/ppermute | solution.py:471
  82.7 8.9 %collective-permute-start.23 = (f32[96,512]{1,0:T(8,128)S(1)}, f32[96,512]{1,0:T(8,128)S(1)}, u32[]{:S(2)}, u32[]{:S(2)}) collective-permute-start(f32[96,512]{1,0:T(8,128)S(1)} %get-tuple-element.98), channel_id=1, source_target_pairs={{0,3},{1,0},{2,1},{3,2},{4,7},{5,4},{6,5},{7,6},{8,11},{9,8},{10,9... | collective-permute-start | bytes 589832 | tf_op jit(solution)/shard_map/ppermute | solution.py:471
  84.4 17.2 %collective-permute-start.20 = (f32[192,512]{1,0:T(8,128)S(1)}, f32[192,512]{1,0:T(8,128)S(1)}, u32[]{:S(2)}, u32[]{:S(2)}) collective-permute-start(f32[192,512]{1,0:T(8,128)S(1)} %get-tuple-element.93), channel_id=1, source_target_pairs={{0,32},{32,0},{64,96},{96,64},{128,160},{160,128},{192,224},{224,1... | collective-permute-start | bytes 1179656 | tf_op jit(solution)/shard_map/ppermute | solution.py:463
  86.7 11.4 %collective-permute-start.17 = (f32[160,512]{1,0:T(8,128)S(1)}, f32[160,512]{1,0:T(8,128)S(1)}, u32[]{:S(2)}, u32[]{:S(2)}) collective-permute-start(f32[160,512]{1,0:T(8,128)S(1)} %get-tuple-element.86), channel_id=1, source_target_pairs={{0,32},{32,0},{64,96},{96,64},{128,160},{160,128},{192,224},{224,1... | collective-permute-start | bytes 983048 | tf_op jit(solution)/shard_map/ppermute | solution.py:463
  93.8 7.8 %collective-permute-start.25 = (f32[96,512]{1,0:T(8,128)S(1)}, f32[96,512]{1,0:T(8,128)S(1)}, u32[]{:S(2)}, u32[]{:S(2)}) collective-permute-start(f32[96,512]{1,0:T(8,128)S(1)} %joined.1.b0), channel_id=1, source_target_pairs={{0,2},{1,3},{2,0},{3,1},{4,6},{5,7},{6,4},{7,5},{8,10},{9,11},{10,... | collective-permute-start | bytes 589832 | tf_op jit(solution)/shard_map/ppermute | solution.py:471
  95.3 11.1 %collective-permute-start.27 = (f32[96,512]{1,0:T(8,128)S(1)}, f32[96,512]{1,0:T(8,128)S(1)}, u32[]{:S(2)}, u32[]{:S(2)}) collective-permute-start(f32[96,512]{1,0:T(8,128)S(1)} %joined.1.b0), channel_id=1, source_target_pairs={{0,1},{1,2},{2,3},{3,0},{4,5},{5,6},{6,7},{7,4},{8,9},{9,10},{10,1... | collective-permute-start | bytes 589832 | tf_op jit(solution)/shard_map/ppermute | solution.py:471
  96.9 9.6 %collective-permute-start.26 = (f32[96,512]{1,0:T(8,128)S(1)}, f32[96,512]{1,0:T(8,128)S(1)}, u32[]{:S(2)}, u32[]{:S(2)}) collective-permute-start(f32[96,512]{1,0:T(8,128)S(1)} %joined.1.b0), channel_id=1, source_target_pairs={{0,3},{1,0},{2,1},{3,2},{4,7},{5,4},{6,5},{7,6},{8,11},{9,8},{10,9... | collective-permute-start | bytes 589832 | tf_op jit(solution)/shard_map/ppermute | solution.py:471
  (4 other events, 20.1 us)
